TPU v7x, 32 devices: a whole 2x2x4 slice. The times are simulated.
32 devices in a mesh: dp: 16 (over z, y, core), expert: 2 (over x).
Axes of the slice: x: 2, y: 2, z: 4, core: 2. Of those that a mesh axis runs over, the one named last changes fastest.
Arguments:
- tokens: bfloat16 [8192, 1536], P(('dp', 'expert')), may hold values from -6 to 6
- norm1_gain: bfloat16 [1536], P('dp'), may hold values from 0.5 to 1.5
- w_query: bfloat16 [1536, 1536], P('dp'), may hold values from -0.15625 to 0.15625
- w_key: bfloat16 [1536, 256], P('dp'), may hold values from -0.15625 to 0.15625
- w_value: bfloat16 [1536, 256], P('dp'), may hold values from -0.15625 to 0.15625
- w_out: bfloat16 [1536, 1536], P('dp'), may hold values from -0.625 to 0.625
- norm2_gain: bfloat16 [1536], P('dp'), may hold values from 0.5 to 1.5
- w_router: bfloat16 [1536, 8], P('dp'), may hold values from -0.06982422 to 0.06982422
- w_gate: bfloat16 [8, 1536, 768], P('expert'), may hold values from -0.15625 to 0.15625
- w_up: bfloat16 [8, 1536, 768], P('expert'), may hold values from -0.15625 to 0.15625
- w_down: bfloat16 [8, 768, 1536], P('expert'), may hold values from -0.44921875 to 0.44921875
- expert_ids: int32 [8192, 4], P(('dp', 'expert')), may hold values from 0 to 7, all different within a row; in each aligned block of 128 rows (0 to 127, 128 to 255, ...) at most 96 rows name the same one
- prefix_len: int32 [32], P(('dp', 'expert')), may hold values from 25 to 128
- out_grad: bfloat16 [8192, 1536], P(('dp', 'expert')), may hold values from -6 to 6
Outputs:
- block_out: bfloat16 [8192, 1536], P(('dp', 'expert'))
- tokens_grad: bfloat16 [8192, 1536], P(('dp', 'expert'))
- norm1_grad: float32 [1536], P('dp')
- query_grad: float32 [1536, 1536], P('dp')
- key_grad: float32 [1536, 256], P('dp')
- value_grad: float32 [1536, 256], P('dp')
- outproj_grad: float32 [1536, 1536], P('dp')
- norm2_grad: float32 [1536], P('dp')
- router_grad: float32 [1536, 8], P('dp')
- gate_grad: float32 [8, 1536, 768], P('expert', 'dp')
- up_grad: float32 [8, 1536, 768], P('expert', 'dp')
- down_grad: float32 [8, 768, 1536], P('expert', None, 'dp')
Inputs may be any that keep to these rules, and one draw needn't show every extreme that they name: `expert_ids`: each row names 4 different experts. Within the rows of one device's micro-batch (aligned blocks of 128 rows) no expert is named by more than 96 rows, and some block reaches 96.
All inputs are finite; a program needn't handle non-finite values.
Results may differ from a plain program's by a relative error of at most 0.024.
Values may be sent and summed in bfloat16 or wider, within the bound.
No kernel may reach another device: no remote copies, remote signals or barrier semaphores. Data moves between devices by JAX's collectives and lax.ppermute only.
A program may use at most 192 MiB of HBM per device.

v0:
```python
import functools
import math

import jax
import jax.numpy as jnp
from jax import lax
from jax.experimental import pallas as pl
from jax.experimental.pallas import tpu as pltpu
from jax.sharding import PartitionSpec as P

HQ = 12
HK = 2
HD = 128
MICRO = 2
PLANE = ("y", "c", "x")
GROUP = ("z", "y", "c")


def rms_scale(values, gain_vec):
    inverse = lax.rsqrt(jnp.mean(values * values, axis=-1, keepdims=True) + 1e-06)
    return values * inverse * gain_vec


def angles(length, head_size):
    positions = jnp.arange(length).astype(jnp.float32)
    freq_rates = jnp.exp(
        -(2.0 * jnp.arange(head_size // 2).astype(jnp.float32) / head_size) * math.log(1000000.0)
    )
    angle_tab = positions[:, None] * freq_rates[None, :]
    return (jnp.cos(angle_tab)[:, None, :], jnp.sin(angle_tab)[:, None, :])


def rotary(values, cosine_tab, sine_tab):
    half_dim = values.shape[-1] // 2
    first_half = values[..., :half_dim]
    second_half = values[..., half_dim:]
    return jnp.concatenate(
        [
            first_half * cosine_tab - second_half * sine_tab,
            second_half * cosine_tab + first_half * sine_tab,
        ],
        axis=-1,
    )


def expert_act(gate_pre, up_pre):
    return jax.nn.gelu(gate_pre, approximate=True) * up_pre


def left_product(left_mat, right_mat):
    return lax.dot_general(
        left_mat, right_mat, (((0,), (0,)), ((), ())), preferred_element_type=jnp.float32
    )


def gather(block, axes):
    return lax.all_gather(block, axes, axis=0, tiled=True)


def exchange(block, axes):
    return lax.all_to_all(block, axes, split_axis=0, concat_axis=0, tiled=True)


def scatter_sum(block, axes):
    return lax.psum_scatter(block, axes, scatter_dimension=0, tiled=True)


def by_owner(cols, parts):
    rows, total = cols.shape
    return jnp.moveaxis(cols.reshape(rows, parts, total // parts), 1, 0).reshape(
        parts * rows, total // parts
    )


def local_wide(
    tokens,
    norm1_gain,
    w_query,
    w_key,
    w_value,
    w_out,
    norm2_gain,
    w_router,
    w_gate,
    w_up,
    w_down,
    expert_ids,
    prefix_len,
    out_grad,
):
    bf16, f32 = jnp.bfloat16, jnp.float32
    length, model_width = tokens.shape
    shard_rows = w_query.shape[0]
    local_count, _, hidden_width = w_gate.shape
    owners = lax.axis_size("x")
    depth = lax.axis_size("z")
    plane = lax.axis_size(PLANE)
    experts_all = w_router.shape[1]
    top_count = expert_ids.shape[1]
    block_rows = length // MICRO
    capacity = 3 * block_rows * top_count // (2 * experts_all)
    plane_rows = plane * length
    blocks = plane_rows // block_rows
    group_size = HQ // HK
    score_scale = HD ** (-0.5)
    q_cols, kv_cols = w_query.shape[1], w_key.shape[1]
    own_local = lax.axis_index(("y", "c"))
    own_expert = lax.axis_index("x") * local_count + own_local
    own_place = lax.axis_index(PLANE)

    narrow = jnp.concatenate([w_router, norm1_gain[:, None], norm2_gain[:, None]], axis=1)
    narrow = jnp.pad(narrow, ((0, 0), (0, -narrow.shape[1] % 128)))
    packed = gather(jnp.concatenate([w_query, w_key, w_value, narrow], axis=1), GROUP)
    qkv_cols = q_cols + 2 * kv_cols
    qkv_w = packed[:, :qkv_cols]
    router_w = packed[:, qkv_cols : qkv_cols + experts_all]
    gains = packed[:, qkv_cols + experts_all : qkv_cols + experts_all + 2].T.astype(f32)
    gain_one, gain_two = gains[0], gains[1]
    output_w = gather(w_out, GROUP)

    ids_all = gather(expert_ids, PLANE)
    cot_all = gather(out_grad, PLANE)
    chosen_mask = jnp.any(
        ids_all[:, :, None] == jnp.arange(experts_all, dtype=jnp.int32)[None, None, :], axis=1
    )
    own_mask = jnp.any(ids_all == own_expert, axis=1).reshape(blocks, block_rows)
    place = jnp.cumsum(own_mask.astype(jnp.int32), axis=1) - 1
    dispatch = (
        own_mask[:, None, :]
        & (place[:, None, :] == jnp.arange(capacity, dtype=jnp.int32)[None, :, None])
    ).astype(bf16)

    cosine_tab, sine_tab = angles(length, HD)
    inputs_f = tokens.astype(f32)
    first_in = rms_scale(inputs_f, gain_one).astype(bf16)
    qkv = jnp.dot(first_in, qkv_w, preferred_element_type=f32)
    queries = (
        rotary(qkv[:, :q_cols].reshape(length, HQ, HD), cosine_tab, sine_tab)
        .astype(bf16)
        .reshape(length, HK, group_size, HD)
    )
    keys_rot = rotary(
        qkv[:, q_cols : q_cols + kv_cols].reshape(length, HK, HD), cosine_tab, sine_tab
    ).astype(bf16)
    values_b = qkv[:, q_cols + kv_cols :].astype(bf16).reshape(length, HK, HD)
    positions = jnp.arange(length)
    allowed = (positions[None, :] <= positions[:, None]) | (positions[None, :] < prefix_len[0])

    def masked_scores():
        scores = jnp.einsum("ihrd,jhd->hrij", queries, keys_rot, preferred_element_type=f32)
        return jnp.where(allowed, scores * score_scale, -1e30)

    masked = masked_scores()
    row_peak = jnp.max(masked, axis=-1, keepdims=True)
    log_total = row_peak + jnp.log(jnp.sum(jnp.exp(masked - row_peak), axis=-1, keepdims=True))
    prob_bf = jnp.exp(masked - log_total).astype(bf16)
    attended = jnp.einsum("hrij,jhd->ihrd", prob_bf, values_b, preferred_element_type=f32)
    attended = attended.reshape(length, HQ * HD).astype(bf16)
    resid = inputs_f + jnp.dot(attended, output_w, preferred_element_type=f32)
    second_in = rms_scale(resid, gain_two).astype(bf16)

    second_all = gather(second_in, PLANE)
    logits = jnp.dot(second_all, router_w, preferred_element_type=f32)
    gates_all = jax.nn.softmax(jnp.where(chosen_mask, logits, -jnp.inf), axis=-1)
    own_gates = lax.dynamic_index_in_dim(gates_all, own_expert, 1, keepdims=False)
    own_gates = own_gates.reshape(blocks, block_rows)
    gate_rows = jnp.einsum(
        "bct,bt->bc", dispatch.astype(f32), own_gates, precision=lax.Precision.HIGHEST
    )[:, :, None]
    gate_w = lax.dynamic_index_in_dim(w_gate, own_local, 0, keepdims=False)
    up_w = lax.dynamic_index_in_dim(w_up, own_local, 0, keepdims=False)
    down_w = lax.dynamic_index_in_dim(w_down, own_local, 0, keepdims=False)

    def to_rows(array):
        return jnp.einsum(
            "bct,btd->bcd",
            dispatch,
            array.reshape(blocks, block_rows, model_width),
            preferred_element_type=f32,
        ).astype(bf16)

    def to_tokens(rows):
        return (
            jnp.einsum("bct,bcd->btd", dispatch, rows.astype(bf16), preferred_element_type=f32)
            .astype(bf16)
            .reshape(plane_rows, model_width)
        )

    rows_in = to_rows(second_all)
    rows_cot = to_rows(cot_all)
    gate_pre = jnp.einsum("bcd,df->bcf", rows_in, gate_w, preferred_element_type=f32)
    up_pre = jnp.einsum("bcd,df->bcf", rows_in, up_w, preferred_element_type=f32)
    hidden, act_pull = jax.vjp(expert_act, gate_pre, up_pre)
    gated = (gate_rows * hidden).astype(bf16)
    down_part = jnp.einsum("bcd,bcf->df", rows_cot, gated, preferred_element_type=f32)
    down_sum = scatter_sum(down_part.astype(bf16), "z")
    cot_hidden = jnp.einsum("bcd,fd->bcf", rows_cot, down_w, preferred_element_type=f32)
    gate_signal_rows = jnp.sum(hidden * cot_hidden, axis=-1)
    gate_pgrad, up_pgrad = act_pull(gate_rows * cot_hidden)
    gate_pgrad = gate_pgrad.astype(bf16)
    up_pgrad = up_pgrad.astype(bf16)
    gate_part = jnp.einsum("bcd,bcf->df", rows_in, gate_pgrad, preferred_element_type=f32)
    gate_sum = scatter_sum(gate_part.astype(bf16), "z")
    up_part = jnp.einsum("bcd,bcf->df", rows_in, up_pgrad, preferred_element_type=f32)
    up_sum = scatter_sum(up_part.astype(bf16), "z")
    rows_grad = jnp.einsum("bcf,df->bcd", gate_pgrad, gate_w, preferred_element_type=f32)
    rows_grad = rows_grad + jnp.einsum("bcf,df->bcd", up_pgrad, up_w, preferred_element_type=f32)
    second_back = scatter_sum(to_tokens(rows_grad), PLANE).astype(f32)
    gate_signal = jnp.einsum(
        "bct,bc->bt", dispatch.astype(f32), gate_signal_rows, precision=lax.Precision.HIGHEST
    )
    gate_signal = exchange(gate_signal.reshape(plane, length), PLANE)
    gate_signal = jnp.transpose(
        gate_signal.reshape(local_count, owners, length), (2, 1, 0)
    ).reshape(length, experts_all)
    expert_rows = jnp.einsum("bcf,fd->bcd", gated, down_w, preferred_element_type=f32)
    mixture = scatter_sum(to_tokens(expert_rows), PLANE).astype(f32)
    block_out = (resid + mixture).astype(bf16)

    cotangent = out_grad.astype(f32)
    gate_probs = lax.dynamic_slice_in_dim(gates_all, own_place * length, length, 0)
    logit_grad = (
        gate_probs
        * (gate_signal - jnp.sum(gate_probs * gate_signal, axis=-1, keepdims=True))
    ).astype(bf16)
    router_acc = left_product(second_in, logit_grad)
    second_grad = second_back + jnp.dot(logit_grad, router_w.T, preferred_element_type=f32)
    _, norm_two_pull = jax.vjp(rms_scale, resid, gain_two)
    resid_norm_grad, gain_two_grad = norm_two_pull(second_grad)
    resid_grad = cotangent + resid_norm_grad
    branch_grad = resid_grad.astype(bf16)

    attended_all = gather(attended, PLANE)
    branch_cols = exchange(by_owner(branch_grad, plane), PLANE)
    output_part = left_product(attended_all, branch_cols)
    attended_grad = jnp.dot(branch_grad, output_w.T, preferred_element_type=f32).astype(bf16)
    attended_grad = attended_grad.reshape(length, HK, group_size, HD)
    masked = masked_scores()
    prob_full = jnp.exp(masked - log_total)
    prob_bf = prob_full.astype(bf16)
    prob_grad = jnp.einsum("ihrd,jhd->hrij", attended_grad, values_b, preferred_element_type=f32)
    row_inner = jnp.sum(prob_full * prob_grad, axis=-1, keepdims=True)
    score_grad = (prob_full * (prob_grad - row_inner)).astype(bf16)
    query_rot_grad = (
        jnp.einsum("hrij,jhd->ihrd", score_grad, keys_rot, preferred_element_type=f32)
        * score_scale
    )
    query_back = rotary(query_rot_grad.reshape(length, HQ, HD), cosine_tab, -sine_tab)
    query_back = query_back.astype(bf16).reshape(length, HQ * HD)
    key_rot_grad = (
        jnp.einsum("hrij,ihrd->jhd", score_grad, queries, preferred_element_type=f32)
        * score_scale
    )
    key_back = rotary(key_rot_grad, cosine_tab, -sine_tab).astype(bf16).reshape(length, HK * HD)
    value_back = jnp.einsum("hrij,ihrd->jhd", prob_bf, attended_grad, preferred_element_type=f32)
    value_back = value_back.astype(bf16).reshape(length, HK * HD)
    qkv_back = jnp.concatenate([query_back, key_back, value_back], axis=1)
    first_all = gather(first_in, PLANE)
    qkv_part = left_product(first_all, exchange(by_owner(qkv_back, plane), PLANE))
    first_grad = lax.dot_general(
        qkv_back, qkv_w, (((1,), (1,)), ((), ())), preferred_element_type=f32
    )
    _, norm_one_pull = jax.vjp(rms_scale, inputs_f, gain_one)
    input_norm_grad, gain_one_grad = norm_one_pull(first_grad)
    tokens_grad = (resid_grad + input_norm_grad).astype(bf16)

    narrow_part = jnp.concatenate(
        [router_acc, gain_one_grad[:, None], gain_two_grad[:, None]], axis=1
    ).astype(bf16)
    narrow_cols = narrow_part.shape[1]
    narrow_sum = lax.psum(scatter_sum(narrow_part, GROUP), "x").astype(f32)
    dense_part = jnp.concatenate([qkv_part, output_part], axis=1).astype(bf16)
    dense_sum = scatter_sum(dense_part, "z")
    dense_cols = dense_sum.shape[1]
    dense_sum = gather(dense_sum, PLANE).reshape(plane, local_count, shard_rows, dense_cols)
    dense_sum = lax.dynamic_index_in_dim(dense_sum, own_local, 1, keepdims=False).astype(f32)
    dense_sum = jnp.moveaxis(dense_sum, 0, 1)
    qkv_width = qkv_cols // plane
    qkv_sum = dense_sum[:, :, :qkv_width].reshape(shard_rows, qkv_cols)
    output_sum = dense_sum[:, :, qkv_width:].reshape(shard_rows, model_width)

    def placed(total):
        total = exchange(total, ("y", "c"))
        return total.reshape(local_count, shard_rows, hidden_width).astype(f32)

    return (
        block_out,
        tokens_grad,
        narrow_sum[:, experts_all],
        qkv_sum[:, :q_cols],
        qkv_sum[:, q_cols : q_cols + kv_cols],
        qkv_sum[:, q_cols + kv_cols :],
        output_sum,
        narrow_sum[:, experts_all + 1],
        narrow_sum[:, :experts_all],
        placed(gate_sum),
        placed(up_sum),
        jnp.swapaxes(placed(down_sum), 1, 2),
    )


def rounded(values):
    return lax.reduce_precision(values, 8, 7).astype(jnp.bfloat16)


def after(block, *others):
    return lax.optimization_barrier((block,) + others)[0]


def swap(block, axis):
    return lax.ppermute(block, axis, [(0, 1), (1, 0)])


def shifts(block):
    depth = lax.axis_size("z")
    return [
        lax.ppermute(block, "z", [(i, (i + k) % depth) for i in range(depth)])
        for k in range(1, depth)
    ]


def plane_sides(block):
    return swap(block, "x"), swap(block, "y")


def plane_corner(sides, before=()):
    over_x, over_y = sides
    half = over_x.shape[0] // 2
    over_y, over_x = lax.optimization_barrier((over_y[:half], over_x[half:]) + before)[:2]
    return jnp.concatenate([swap(over_y, "x"), swap(over_x, "y")], axis=0)


def plane_pieces(block, sides=None, corner=None):
    sides = plane_sides(block) if sides is None else sides
    corner = plane_corner(sides) if corner is None else corner
    pieces = [block, *sides, corner]
    return pieces + [swap(piece, "c") for piece in pieces]


def small_gather(block):
    for axis in ("x", "y", "c"):
        block = jnp.concatenate([block, swap(block, axis)], axis=0)
    return block


def small_group_gather(block):
    depth = lax.axis_size("z")
    order = jnp.stack(([block] + shifts(block))[::-1] * 2)
    start = (depth - 1 - lax.axis_index("z")) % depth
    total = lax.dynamic_slice_in_dim(order, start, depth, 0)[:, None, None]
    for dim, axis in ((1, "y"), (2, "c")):
        other = swap(total, axis)
        last = lax.axis_index(axis) == 1
        pair = [jnp.where(last, other, total), jnp.where(last, total, other)]
        total = jnp.concatenate(pair, axis=dim)
    return total.reshape(-1, block.shape[1])


def add(left, right):
    return rounded(left.astype(jnp.float32) + right.astype(jnp.float32))


def over_core(near, far):
    return add(near, swap(far, "c"))


def early_sums(over_x, over_y):
    half = over_x.shape[0] // 2
    return swap(over_x[:half], "x"), swap(over_y[half:], "y")


def corner_first(corner):
    half = corner.shape[0] // 2
    return swap(corner[:half], "x"), swap(corner[half:], "y")


def corner_last(over_x, over_y, first):
    half = over_x.shape[0] // 2
    return swap(add(over_y[:half], first[0]), "y"), swap(add(over_x[half:], first[1]), "x")


def cost(micros):
    return pl.CostEstimate(flops=micros * 10**9, bytes_accessed=micros * 10**6, transcendentals=0)


def dot(left, right, dims=((1,), (0,)), precision=None):
    return lax.dot_general(
        left, right, (dims, ((), ())), precision=precision, preferred_element_type=jnp.float32
    )


WHOLE = pl.BlockSpec(memory_space=pltpu.VMEM)
SCALARS = pl.BlockSpec(memory_space=pltpu.SMEM)


def run_kernel(kernel, micros, at, operands, outs, megabytes=40, scratch=()):
    return pl.pallas_call(
        kernel,
        out_shape=[jax.ShapeDtypeStruct(shape, dtype) for shape, dtype in outs],
        in_specs=[SCALARS] + [WHOLE] * len(operands),
        out_specs=[WHOLE] * len(outs),
        scratch_shapes=scratch,
        cost_estimate=cost(micros),
        compiler_params=pltpu.CompilerParams(vmem_limit_bytes=megabytes * 2**20),
    )(at, *operands)


def place_pieces(at, refs, weight):
    depth = weight.shape[1]
    for n, ref in enumerate(refs):
        dc, dy, dx = n // 4, n // 2 % 2, n % 2
        for k in range(depth):
            z = lax.rem(at[3] + depth - k, depth)
            weight[at[2] ^ dx, z, at[0] ^ dy, at[1] ^ dc] = ref[k]


def rms_kernel(values, gain):
    inverse = lax.rsqrt(jnp.mean(values * values, axis=-1, keepdims=True) + 1e-06)
    return (values * inverse * gain).astype(jnp.bfloat16)


def rms_back(values, gain, grad):
    inverse = lax.rsqrt(jnp.mean(values * values, axis=-1, keepdims=True) + 1e-06)
    normed = values * inverse
    gain_grad = jnp.sum(grad * normed, axis=0, keepdims=True)
    grad = grad * gain
    along = jnp.mean(grad * normed, axis=-1, keepdims=True)
    return inverse * (grad - normed * along), gain_grad


def turned(values, cosine_tab, sine_tab):
    return values * cosine_tab + pltpu.roll(values, HD // 2, 1) * sine_tab


def attend_kernel(at, tokens, gain, cosine, sine, *refs):
    first_ref, query_ref, key_ref, value_ref, prob_ref, out_ref, weight = refs[8:]
    place_pieces(at, refs[:8], weight)
    length = tokens.shape[0]
    first_in = rms_kernel(tokens[...].astype(jnp.float32), gain[...])
    first_ref[...] = first_in
    rows = lax.broadcasted_iota(jnp.int32, (length, length), 0)
    cols = lax.broadcasted_iota(jnp.int32, (length, length), 1)
    allowed = (cols <= rows) | (cols < at[4])
    cosine_tab, sine_tab = cosine[...], sine[...]
    group_size = HQ // HK
    for group in range(HK):
        matrix = weight[group].reshape(first_in.shape[1], -1)
        qkv = dot(first_in, matrix)
        at_key = group_size * HD
        key = turned(qkv[:, at_key : at_key + HD], cosine_tab, sine_tab).astype(jnp.bfloat16)
        value = qkv[:, at_key + HD :].astype(jnp.bfloat16)
        key_ref[:, group * HD : (group + 1) * HD] = key
        value_ref[:, group * HD : (group + 1) * HD] = value
        for member in range(group_size):
            head = group * group_size + member
            here = slice(head * HD, (head + 1) * HD)
            query = turned(qkv[:, member * HD : (member + 1) * HD], cosine_tab, sine_tab)
            query = query.astype(jnp.bfloat16)
            query_ref[:, here] = query
            scores = dot(query, key, ((1,), (1,)))
            scores = jnp.where(allowed, scores * HD ** (-0.5), -1e30)
            weights = jnp.exp(scores - jnp.max(scores, axis=-1, keepdims=True))
            prob = weights * (1.0 / jnp.sum(weights, axis=-1, keepdims=True))
            prob = prob.astype(jnp.bfloat16)
            prob_ref[head] = prob
            out_ref[:, here] = dot(prob, value).astype(jnp.bfloat16)


def project_kernel(at, tokens, gain, attended, *refs):
    resid_ref, second_ref, weight = refs[8:]
    place_pieces(at, refs[:8], weight)
    heads = attended[...]
    halves = [dot(heads, weight[half].reshape(heads.shape[1], -1)) for half in range(2)]
    resid = tokens[...].astype(jnp.float32) + jnp.concatenate(halves, axis=1)
    resid_ref[...] = resid
    second_ref[...] = rms_kernel(resid, gain[...])


def one_hot(slots, capacity, dtype):
    shape = (capacity, slots.shape[1])
    return (slots == lax.broadcasted_iota(jnp.int32, shape, 0)).astype(jnp.float32).astype(dtype)


def spread(slots, pieces, capacity, rows, outs):
    rows = rows.astype(jnp.bfloat16)
    block = slots.shape[1]
    for n, piece in enumerate(pieces):
        for part in range(2):
            pick = one_hot(slots[2 * piece + part : 2 * piece + part + 1], capacity, jnp.bfloat16)
            at_row = (2 * n + part) * capacity
            tokens = dot(pick, rows[at_row : at_row + capacity], ((0,), (0,)))
            outs[n][part * block : (part + 1) * block] = tokens.astype(jnp.bfloat16)


def expert_kernel(capacity, pieces, at, slots, bias, router, gate_w, up_w, down_w, *refs):
    count = len(pieces)
    second, cot = refs[:count], refs[count : 2 * count]
    rows_in, rows_cot, gated_ref, gate_back, up_back, signal_ref, gates_ref = refs[
        2 * count : 2 * count + 7
    ]
    backs = refs[2 * count + 7 : -1]
    gate_rows = refs[-1]
    f32, bf16 = jnp.float32, jnp.bfloat16
    length = second[0].shape[0]
    half = length // 2
    for n, piece in enumerate(pieces):
        tokens = second[n][...]
        logits = dot(tokens, router[...]) + bias[piece * length : (piece + 1) * length]
        weights = jnp.exp(logits - jnp.max(logits, axis=-1, keepdims=True))
        gates = weights * (1.0 / jnp.sum(weights, axis=-1, keepdims=True))
        if n == 0:
            gates_ref[...] = gates
        lanes = lax.broadcasted_iota(jnp.int32, (capacity, gates.shape[1]), 1)
        for part in range(2):
            block = 2 * piece + part
            here = slice(part * half, (part + 1) * half)
            place = slice((2 * n + part) * capacity, (2 * n + part + 1) * capacity)
            pick = one_hot(slots[block : block + 1], capacity, f32)
            rows_in[place] = dot(pick.astype(bf16), tokens[here]).astype(bf16)
            rows_cot[place] = dot(pick.astype(bf16), cot[n][here]).astype(bf16)
            picked = dot(pick, gates[here], precision=lax.Precision.HIGHEST)
            picked = jnp.where(lanes == at[5], picked, 0.0)
            gate_rows[place] = jnp.sum(picked, axis=1, keepdims=True)
    gate = gate_rows[...]
    gate_pre = dot(rows_in[...], gate_w[...])
    up_pre = dot(rows_in[...], up_w[...])
    cot_hidden = dot(rows_cot[...], down_w[...], ((1,), (1,)))
    scale = math.sqrt(2.0 / math.pi)
    square = gate_pre * gate_pre
    bent = jnp.tanh(scale * gate_pre * (1.0 + 0.044715 * square))
    open_part = 0.5 * (1.0 + bent)
    active = gate_pre * open_part
    slope = open_part + 0.5 * gate_pre * (1.0 - bent * bent) * scale * (
        1.0 + 3 * 0.044715 * square
    )
    hidden = active * up_pre
    gated_ref[...] = (gate * hidden).astype(bf16)
    signal = jnp.sum(hidden * cot_hidden, axis=1, keepdims=True)
    back = gate * cot_hidden
    gate_back[...] = (back * up_pre * slope).astype(bf16)
    up_back[...] = (back * active).astype(bf16)
    for n in range(2 * count):
        block = 2 * pieces[n // 2] + n % 2
        pick = one_hot(slots[block : block + 1], capacity, f32)
        own = signal[n * capacity : (n + 1) * capacity]
        signal_ref[n : n + 1] = jnp.sum(pick * own, axis=0, keepdims=True)
    by_rows = ((1,), (1,))
    rows = dot(gate_back[...], gate_w[...], by_rows) + dot(up_back[...], up_w[...], by_rows)
    spread(slots, pieces, capacity, rows, backs)


def run_expert(pieces, at, slots, bias, router, weights, second, cot, capacity):
    count = len(pieces)
    rows, lanes = 2 * count * capacity, slots.shape[1]
    (length, width), hidden = second[0].shape, weights[0].shape[1]
    bf16, f32 = jnp.bfloat16, jnp.float32
    outs = [(rows, width)] * 2 + [(rows, hidden)] * 3
    outs = [(shape, bf16) for shape in outs] + [((8, lanes), f32), ((length, lanes), f32)]
    outs = outs + [((length, width), bf16)] * count
    return run_kernel(
        functools.partial(expert_kernel, capacity, pieces),
        6 * count,
        at,
        (slots, bias, router, *weights, *second, *cot),
        outs,
        56,
        [pltpu.VMEM((rows, 1), f32)],
    )


def mixture_kernel(capacity, groups, at, slots, down_w, *refs):
    outs = refs[len(groups) :]
    for pieces, gated in zip(groups, refs):
        rows = dot(gated[...], down_w[...])
        spread(slots, pieces, capacity, rows, [outs[piece] for piece in pieces])


def row_sum_kernel(at, *refs):
    half = len(refs) // 2
    total = sum(
        dot(left[...], right[...], ((0,), (0,))) for left, right in zip(refs[:half], refs[half:-1])
    )
    refs[-1][...] = total.astype(jnp.bfloat16)


def row_sum(at, lefts, rights):
    shape = (lefts[0].shape[1], rights[0].shape[1])
    return run_kernel(row_sum_kernel, 6, at, (*lefts, *rights), [(shape, jnp.bfloat16)], 48)[0]


def branch_back_kernel(
    at, near, far, first_x, first_y, last_y, last_x, resid, gain, second, gates, signal, router, cot, weight, *outs
):
    resid_grad_ref, branch_ref, attended_ref, router_ref, gain_ref = outs
    f32, bf16 = jnp.float32, jnp.bfloat16
    chosen = gates[...]
    logit_grad = chosen * (
        signal[...] - jnp.sum(chosen * signal[...], axis=-1, keepdims=True)
    )
    logit_grad = logit_grad.astype(bf16)
    halves = [first_x[...].astype(f32) + last_y[...], first_y[...].astype(f32) + last_x[...]]
    second_grad = near[...].astype(f32) + far[...] + jnp.concatenate(halves, axis=0)
    second_grad = second_grad + dot(logit_grad, router[...], ((1,), (1,)))
    norm_grad, gain_grad = rms_back(resid[...], gain[...], second_grad)
    gain_ref[...] = gain_grad
    resid_grad = cot[...].astype(f32) + norm_grad
    resid_grad_ref[...] = resid_grad
    branch = resid_grad.astype(bf16)
    branch_ref[...] = branch
    wide = weight.shape[2]
    attended_ref[...] = (
        dot(branch[:, :wide], weight[0], ((1,), (1,)))
        + dot(branch[:, wide:], weight[1], ((1,), (1,)))
    ).astype(bf16)
    router_ref[...] = dot(second[...], logit_grad, ((0,), (0,)))


def attend_back_kernel(at, attended, probs, queries, keys, values, cosine, sine, back_ref):
    f32, bf16 = jnp.float32, jnp.bfloat16
    cosine_tab, sine_tab = cosine[...], -sine[...]
    group_size = HQ // HK
    width = back_ref.shape[2]
    scale = HD ** (-0.5)

    def put(position, block):
        back_ref[position // width, :, position % width : position % width + HD] = block

    for group in range(HK):
        own = slice(group * HD, (group + 1) * HD)
        key, value = keys[:, own], values[:, own]
        key_grad = value_grad = 0.0
        start = group * (group_size + 2) * HD
        for member in range(group_size):
            head = group * group_size + member
            here = slice(head * HD, (head + 1) * HD)
            out_grad, query, prob = attended[:, here], queries[:, here], probs[head]
            prob_grad = dot(out_grad, value, ((1,), (1,)))
            prob_f = prob.astype(f32)
            inner = jnp.sum(prob_f * prob_grad, axis=-1, keepdims=True)
            score_grad = (prob_f * (prob_grad - inner)).astype(bf16)
            query_grad = turned(dot(score_grad, key) * scale, cosine_tab, sine_tab)
            put(start + member * HD, query_grad.astype(bf16))
            key_grad = key_grad + dot(score_grad, query, ((0,), (0,)))
            value_grad = value_grad + dot(prob, out_grad, ((0,), (0,)))
        key_grad = turned(key_grad * scale, cosine_tab, sine_tab)
        put(start + group_size * HD, key_grad.astype(bf16))
        put(start + (group_size + 1) * HD, value_grad.astype(bf16))


def first_back_kernel(at, back, weight, tokens, gain, resid_grad, tokens_ref, gain_ref):
    f32 = jnp.float32
    parts, _, cols = back.shape
    first_grad = 0.0
    for part in range(parts):
        group, place = divmod(part * cols, weight.shape[2])
        first_grad = first_grad + dot(
            back[part], weight[group, :, place : place + cols], ((1,), (1,))
        )
    norm_grad, gain_grad = rms_back(tokens[...].astype(f32), gain[...], first_grad)
    gain_ref[...] = gain_grad
    tokens_ref[...] = (resid_grad[...] + norm_grad).astype(jnp.bfloat16)


def dense_grad_kernel(at, narrow, branch_cols, qkv_cols, *refs):
    pieces, out_ref, held, sems = refs[:8], refs[8], refs[9], refs[10]
    copies = [
        pltpu.make_async_copy(piece, held.at[n], sems.at[n]) for n, piece in enumerate(pieces)
    ]
    for copy in copies:
        copy.start()
    length = branch_cols.shape[1]
    sums = [0.0, 0.0]
    for n, copy in enumerate(copies):
        copy.wait()
        dc, dy, dx = n // 4, n // 2 % 2, n % 2
        place = 4 * (at[0] ^ dy) + 2 * (at[1] ^ dc) + (at[2] ^ dx)
        sums[0] = sums[0] + dot(held[n, length:], qkv_cols[place], ((0,), (0,)))
        sums[1] = sums[1] + dot(held[n, :length], branch_cols[place], ((0,), (0,)))
    depth, rows, _ = out_ref.shape
    wide = rows - narrow.shape[1]
    for z in range(depth):
        here = slice(z * wide, (z + 1) * wide)
        both = jnp.concatenate([part[here] for part in sums], axis=1)
        out_ref[z, :wide] = both.astype(jnp.bfloat16)
        out_ref[z, wide:] = narrow[z]


def local_pairs(
    tokens,
    norm1_gain,
    w_query,
    w_key,
    w_value,
    w_out,
    norm2_gain,
    w_router,
    w_gate,
    w_up,
    w_down,
    expert_ids,
    prefix_len,
    out_grad,
):
    bf16, f32 = jnp.bfloat16, jnp.float32
    length, model_width = tokens.shape
    shard_rows = w_query.shape[0]
    local_count, _, hidden_width = w_gate.shape
    owners = lax.axis_size("x")
    depth = lax.axis_size("z")
    plane = lax.axis_size(PLANE)
    experts_all = w_router.shape[1]
    block_rows = length // MICRO
    capacity = 3 * block_rows * expert_ids.shape[1] // (2 * experts_all)
    plane_rows = plane * length
    blocks = plane_rows // block_rows
    q_cols, kv_cols = w_query.shape[1], w_key.shape[1]
    qkv_cols = q_cols + 2 * kv_cols
    q_group, out_half = q_cols // HK, model_width // 2
    y, c, x, z = (lax.axis_index(axis) for axis in ("y", "c", "x", "z"))
    own_local = 2 * y + c
    own_expert = x * local_count + own_local
    at = jnp.stack([y, c, x, z, prefix_len[0], own_expert, own_local])

    own_half = jnp.concatenate(
        [
            lax.dynamic_slice_in_dim(part, x * (part.shape[1] // 2), part.shape[1] // 2, 1)
            for part in (w_query, w_key, w_value, w_out)
        ],
        axis=1,
    )
    narrow = jnp.concatenate([w_router, norm1_gain[:, None], norm2_gain[:, None]], axis=1)
    narrow = small_group_gather(narrow)
    column = [own_half] + shifts(own_half)
    cot_sides = plane_sides(after(out_grad, narrow))
    qkv_half = qkv_cols // 2
    qkv_column = jnp.stack([part[:, :qkv_half] for part in column])
    out_column = jnp.stack([part[:, qkv_half:] for part in column])
    qkv_column = after(qkv_column, *cot_sides)
    qkv_sides = plane_sides(qkv_column)
    qkv_corner = plane_corner(qkv_sides)
    out_sides = plane_sides(after(out_column, qkv_corner))
    qkv_pieces = plane_pieces(qkv_column, qkv_sides, qkv_corner)
    router_w = jnp.pad(narrow[:, :experts_all], ((0, 0), (0, 128 - experts_all)))
    gains = narrow[:, experts_all : experts_all + 2].T.astype(f32)
    gain_one, gain_two = gains[:1], gains[1:]

    cosine_tab, sine_tab = angles(length, HD)
    cosine_all = jnp.concatenate([cosine_tab, cosine_tab], axis=2)[:, 0]
    sine_all = jnp.concatenate([-sine_tab, sine_tab], axis=2)[:, 0]
    weight_lead = (2, depth, 2, 2, shard_rows)
    first_in, queries, keys_rot, values_b, probs, attended, qkv_w = run_kernel(
        attend_kernel,
        11,
        at,
        (tokens, gain_one, cosine_all, sine_all, *qkv_pieces),
        [
            ((length, model_width), bf16),
            ((length, q_cols), bf16),
            ((length, kv_cols), bf16),
            ((length, kv_cols), bf16),
            ((HQ, length, length), bf16),
            ((length, q_cols), bf16),
            (weight_lead + (qkv_half,), bf16),
        ],
    )
    out_sides = lax.optimization_barrier((*out_sides, attended))[:2]
    out_corner = plane_corner(out_sides)
    out_pieces = plane_pieces(out_column, out_sides, out_corner)
    resid, second_in, output_w = run_kernel(
        project_kernel,
        4,
        at,
        (tokens, gain_two, attended, *out_pieces),
        [
            ((length, model_width), f32),
            ((length, model_width), bf16),
            (weight_lead + (out_half,), bf16),
        ],
    )
    qkv_w = qkv_w.reshape(HK, model_width, qkv_half)
    output_w = output_w.reshape(2, q_cols, out_half)

    ids_all = small_gather(after(expert_ids, out_corner))
    cot_corner = plane_corner(cot_sides, (out_corner,))
    cot_pieces = plane_pieces(out_grad, cot_sides, cot_corner)
    expert_range = jnp.arange(128, dtype=jnp.int32)
    chosen_mask = jnp.any(ids_all[:, :, None] == expert_range[None, None, :], axis=1)
    bias = jnp.where(chosen_mask, 0.0, -1e30).astype(f32)
    own_mask = jnp.any(ids_all == own_expert, axis=1).reshape(blocks, block_rows)
    place = jnp.cumsum(own_mask.astype(jnp.int32), axis=1) - 1
    slots = jnp.where(own_mask, place, -1)

    gate_w, up_w, down_w = (
        lax.dynamic_index_in_dim(weight, own_local, 0, keepdims=False)
        for weight in (w_gate, w_up, w_down)
    )

    expert = functools.partial(
        run_expert,
        at=at,
        slots=slots,
        bias=bias,
        router=router_w,
        weights=(gate_w, up_w, down_w),
        capacity=capacity,
    )
    second_sides = plane_sides(second_in)
    groups = ((0, 4), (1, 5, 2, 6), (3, 7))
    second_pieces = {0: second_in, 4: swap(second_in, "c")}

    def run_group(pieces):
        return expert(
            pieces,
            second=[second_pieces[piece] for piece in pieces],
            cot=[cot_pieces[piece] for piece in pieces],
        )

    stage_own = run_group(groups[0])
    second_sides = lax.optimization_barrier((*second_sides, stage_own[0]))[:2]
    second_corner = plane_corner(second_sides)
    for piece, block in zip((1, 2), second_sides):
        second_pieces[piece], second_pieces[piece + 4] = block, swap(block, "c")
    stage_sides = run_group(groups[1])
    second_corner = after(second_corner, stage_sides[0])
    second_pieces[3], second_pieces[7] = second_corner, swap(second_corner, "c")
    own_near, own_far = stage_own[7:]
    own_far = swap(own_far, "c")
    x_near, x_far, y_near, y_far = stage_sides[7:]
    back_x, back_y = over_core(x_near, x_far), over_core(y_near, y_far)
    first_x, first_y = early_sums(back_x, back_y)
    stage_corner = run_group(groups[2])
    corner = over_core(*stage_corner[7:])
    passed = corner_first(corner)
    stages = (stage_own, stage_sides, stage_corner)

    def expert_grad(left, right, *before):
        lefts = [stage[left] for stage in stages]
        rights = [stage[right] for stage in stages]
        lefts[0] = after(lefts[0], *before)
        return row_sum(at, lefts, rights)

    down_part = expert_grad(1, 2, corner)
    down_sum = scatter_sum(down_part, "z")
    gate_part = expert_grad(0, 3, down_part)
    gate_sum = scatter_sum(gate_part, "z")
    last_y, last_x = corner_last(back_x, back_y, passed)
    up_part = expert_grad(0, 4, gate_part)
    gates = stage_own[6]
    signal = [None] * 8
    for pieces, stage in zip(groups, stages):
        for n, piece in enumerate(pieces):
            signal[piece] = stage[5][2 * n : 2 * n + 2]
    signal = jnp.stack(signal).reshape(2, 2, 2, length)
    for dim, axis in enumerate(("c", "y", "x")):
        signal = jnp.where(lax.axis_index(axis) == 1, jnp.flip(signal, dim), signal)
    signal = exchange(jnp.swapaxes(signal, 0, 1).reshape(plane, length), PLANE)
    signal = jnp.transpose(signal.reshape(2, 2, owners, length), (3, 2, 0, 1))
    signal = signal.reshape(length, experts_all)
    signal = jnp.pad(signal, ((0, 0), (0, 128 - experts_all)))

    resid_grad, branch_grad, attended_grad, router_acc, gain_two_grad = run_kernel(
        branch_back_kernel,
        6,
        at,
        (
            own_near,
            own_far,
            first_x,
            first_y,
            last_y,
            last_x,
            resid,
            gain_two,
            second_in,
            gates,
            signal,
            router_w,
            out_grad,
            output_w,
        ),
        [
            ((length, model_width), f32),
            ((length, model_width), bf16),
            ((length, q_cols), bf16),
            ((model_width, 128), f32),
            ((1, model_width), f32),
        ],
    )
    (qkv_back,) = run_kernel(
        attend_back_kernel,
        12,
        at,
        (attended_grad, probs, queries, keys_rot, values_b, cosine_all, sine_all),
        [((plane, length, qkv_cols // plane), bf16)],
    )
    branch_back = jnp.moveaxis(branch_grad.reshape(length, plane, model_width // plane), 1, 0)
    branch_cols = exchange(branch_back, PLANE)
    qkv_cols_back = exchange(qkv_back, PLANE)
    tokens_grad, gain_one_grad = run_kernel(
        first_back_kernel,
        6,
        at,
        (qkv_back, qkv_w, tokens, gain_one, resid_grad),
        [((length, model_width), bf16), ((1, model_width), f32)],
    )

    both = jnp.concatenate(lax.optimization_barrier((attended, first_in, qkv_back))[:2], axis=0)
    both_pieces = plane_pieces(both)
    narrow_part = jnp.concatenate(
        [router_acc[:, :experts_all], gain_one_grad.T, gain_two_grad.T], axis=1
    )
    narrow_cols = -(-narrow_part.shape[1] // owners) * owners
    narrow_part = jnp.pad(narrow_part, ((0, 0), (0, narrow_cols - narrow_part.shape[1])))
    narrow_part = jnp.transpose(
        narrow_part.reshape(depth, 2, 2, shard_rows, owners, narrow_cols // owners),
        (1, 2, 4, 0, 3, 5),
    ).reshape(plane, depth, shard_rows * narrow_cols // owners)
    narrow_part = jnp.sum(exchange(narrow_part, PLANE), axis=0)
    qkv_width = qkv_cols // plane
    dense_cols = qkv_width + model_width // plane
    narrow_len = narrow_part.shape[1]
    narrow_rows = -(-narrow_len // dense_cols)
    kept_rows = -(-narrow_rows // 16) * 16
    narrow_part = jnp.pad(narrow_part, ((0, 0), (0, kept_rows * dense_cols - narrow_len)))
    wide_rows = local_count * shard_rows
    dense_shape = (depth, wide_rows + kept_rows, dense_cols)
    anywhere = pl.BlockSpec(memory_space=pl.ANY)
    dense_part = pl.pallas_call(
        dense_grad_kernel,
        out_shape=jax.ShapeDtypeStruct(dense_shape, bf16),
        in_specs=[SCALARS] + [WHOLE] * 3 + [anywhere] * 8,
        out_specs=WHOLE,
        scratch_shapes=[
            pltpu.VMEM((plane, 2 * length, model_width), bf16),
            pltpu.SemaphoreType.DMA((plane,)),
        ],
        cost_estimate=cost(7),
        compiler_params=pltpu.CompilerParams(vmem_limit_bytes=48 * 2**20),
    )(
        at,
        narrow_part.reshape(depth, kept_rows, dense_cols).astype(bf16),
        branch_cols,
        qkv_cols_back,
        *both_pieces,
    )
    dense_sum = scatter_sum(dense_part.reshape(-1, dense_cols), "z")
    wide_sum = dense_sum[: local_count * shard_rows].reshape(2, 2, 1, shard_rows, dense_cols)
    wide_sum = jnp.broadcast_to(wide_sum, (2, 2, owners, shard_rows, dense_cols)).reshape(
        plane, shard_rows, dense_cols
    )
    narrow_sum = dense_sum[local_count * shard_rows :][:narrow_rows]
    narrow_sum = jnp.broadcast_to(narrow_sum[None], (plane, narrow_rows, dense_cols))
    pad_rows = -(shard_rows + narrow_rows) % 16
    padding = jnp.zeros((plane, pad_rows, dense_cols), bf16)
    dense_sum = exchange(jnp.concatenate([wide_sum, narrow_sum, padding], axis=1), PLANE)
    wide_sum = jnp.moveaxis(dense_sum[:, :shard_rows].astype(f32), 0, 1)
    qkv_sum = wide_sum[:, :, :qkv_width].reshape(shard_rows, HK, qkv_half)
    output_sum = wide_sum[:, :, qkv_width:].reshape(shard_rows, model_width)
    narrow_sum = dense_sum[:, shard_rows : shard_rows + narrow_rows].reshape(
        2, 2, owners, narrow_rows * dense_cols
    )
    narrow_sum = narrow_sum[y, c, :, :narrow_len].reshape(owners, shard_rows, -1)
    narrow_sum = jnp.moveaxis(narrow_sum, 0, 1).reshape(shard_rows, narrow_cols).astype(f32)

    up_sum = scatter_sum(after(up_part, dense_sum), "z")

    shares = run_kernel(
        functools.partial(mixture_kernel, capacity, groups),
        10,
        at,
        (slots, down_w, after(stage_own[2], both_pieces[3]), stage_sides[2], stage_corner[2]),
        [((length, model_width), bf16)] * plane,
        48,
    )
    mixed = [over_core(near, far) for near, far in zip(shares[:4], shares[4:])]
    early = early_sums(mixed[1], mixed[2])
    last = corner_last(mixed[1], mixed[2], corner_first(mixed[3]))
    mixture = jnp.concatenate(
        [left.astype(f32) + right.astype(f32) for left, right in zip(early, last)], axis=0
    )
    block_out = (resid + (mixture + mixed[0].astype(f32))).astype(bf16)

    def placed(total):
        total = exchange(total, ("y", "c"))
        return total.reshape(local_count, shard_rows, hidden_width).astype(f32)

    return (
        block_out,
        tokens_grad,
        narrow_sum[:, experts_all],
        qkv_sum[:, :, :q_group].reshape(shard_rows, q_cols),
        qkv_sum[:, :, q_group : q_group + HD].reshape(shard_rows, kv_cols),
        qkv_sum[:, :, q_group + HD :].reshape(shard_rows, kv_cols),
        output_sum,
        narrow_sum[:, experts_all + 1],
        narrow_sum[:, :experts_all],
        placed(gate_sum),
        placed(up_sum),
        jnp.swapaxes(placed(down_sum), 1, 2),
    )


def solution(mesh):
    groups, owners = mesh.shape["dp"], mesh.shape["expert"]
    grid = jax.sharding.Mesh(
        mesh.devices.reshape(groups // 4, 2, 2, owners), ("z", "y", "c", "x")
    )
    rows = P(("z", "y", "c", "x"), None)
    shard, shard_rows = P(GROUP), P(GROUP, None)
    expert = P("x", None, None)
    return jax.shard_map(
        local_pairs if owners == 2 else local_wide,
        mesh=grid,
        in_specs=(
            rows,
            shard,
            shard_rows,
            shard_rows,
            shard_rows,
            shard_rows,
            shard,
            shard_rows,
            expert,
            expert,
            expert,
            rows,
            P(("z", "y", "c", "x")),
            rows,
        ),
        out_specs=(
            rows,
            rows,
            shard,
            shard_rows,
            shard_rows,
            shard_rows,
            shard_rows,
            shard,
            shard_rows,
            P("x", GROUP, None),
            P("x", GROUP, None),
            P("x", None, GROUP),
        ),
        check_vma=False,
    )
```

profile of v0, /device:TPU:0, one launch (start us, length us, event | category | flops | bytes accessed | tf_op | source)
XLA Modules:
  0.0 578.8 jit_solution(4682210747556901414)
XLA Ops:
  8.0 5.1 collective-permute-start
  15.9 2.9 collective-permute-start.7
  29.1 19.8 %collective-permute-done.6 = bf16[96,1792]{1,0:T(8,128)(2,1)S(1)} collective-permute-done((bf16[96,1792]{1,0:T(8,128)(2,1)S(1)}, bf16[96,1792]{1,0:T(8,128)(2,1)S(1)}, u32[]{:S(2)}, u32[]{:S(2)}) %collective-permute-start.6) | collective-permute-done | bytes 344096 | tf_op jit(solution)/shard_map/ppermute | solution.py:317
  52.2 4.8 dynamic-slice_bitcast_fusion
  57.0 11.0 %collective-permute-done.11.refs_2_ = bf16[4,96,1024]{2,1,0:T(8,128)(2,1)S(1)} collective-permute-done((bf16[4,96,1024]{2,1,0:T(8,128)(2,1)S(1)}, bf16[4,96,1024]{2,1,0:T(8,128)(2,1)S(1)}, u32[]{:S(2)}, u32[]{:S(2)}) %collective-permute-start.11) | collective-permute-done | bytes 786464 | tf_op jit(solution)/shard_map/ppermute | solution.py:311
  70.7 5.2 collective-permute-done.12
  79.8 8.4 %shard_map.229 = (bf16[256,1536]{1,0:T(8,128)(2,1)S(1)}, bf16[256,1536]{1,0:T(8,128)(2,1)S(1)}, bf16[256,256]{1,0:T(8,128)(2,1)S(1)}, bf16[256,256]{1,0:T(8,128)...) custom-call(s32[7]{0:T(128)S(1)} %stack.103.at, ...), custom_call_target="tpu_custom_call" | custom-call | flops 11000000512 | bytes 11000000 | tf_op jit(solution)/shard_map/pallas_call | solution.py:397
  88.3 4.1 collective-permute-done.18.refs_1_
  96.5 3.3 dynamic-slice_bitcast_fusion.2.down_w
  111.8 3.1 collective-permute-done.27
  118.5 3.3 shard_map.230
  128.8 12.8 %shard_map.231 = (bf16[384,1536]{1,0:T(8,128)(2,1)}, bf16[384,1536]{1,0:T(8,128)(2,1)}, bf16[384,768]{1,0:T(8,128)(2,1)}, bf16[384,768]{1,0:T(8,128)(2,1)}, bf16...) custom-call(s32[7]{0:T(128)} %copy-done.23, ...), custom_call_target="tpu_custom_call" | custom-call | flops 12000000000 | bytes 12000000 | tf_op jit(solution)/shard_map/pallas_call | solution.py:397
  141.6 6.5 %collective-permute-done.32.refs_0_ = bf16[256,1536]{1,0:T(8,128)(2,1)} collective-permute-done((bf16[256,1536]{1,0:T(8,128)(2,1)}, bf16[256,1536]{1,0:T(8,128)(2,1)}, u32[]{:S(2)}, u32[]{:S(2)}) %collective-permute-start.32) | collective-permute-done | bytes 786464 | tf_op jit(solution)/shard_map/ppermute | solution.py:311
  150.3 9.7 %collective-permute-done.46 = bf16[128,1536]{1,0:T(8,128)(2,1)} collective-permute-done((bf16[128,1536]{1,0:T(8,128)(2,1)S(1)}, bf16[128,1536]{1,0:T(8,128)(2,1)}, u32[]{:S(2)}, u32[]{:S(2)}) %collective-permute-start.46) | collective-permute-done | bytes 393248 | tf_op jit(solution)/shard_map/ppermute | solution.py:311
  165.8 21.1 %shard_map.232 = (bf16[768,1536]{1,0:T(8,128)(2,1)}, bf16[768,1536]{1,0:T(8,128)(2,1)}, bf16[768,768]{1,0:T(8,128)(2,1)}, bf16[768,768]{1,0:T(8,128)(2,1)}, bf16...) custom-call(s32[7]{0:T(128)} %copy-done.23, ...), custom_call_target="tpu_custom_call" | custom-call | flops 24000000000 | bytes 24000000 | tf_op jit(solution)/shard_map/pallas_call | solution.py:397
  193.9 13.2 %shard_map.233 = (bf16[384,1536]{1,0:T(8,128)(2,1)}, bf16[384,1536]{1,0:T(8,128)(2,1)}, bf16[384,768]{1,0:T(8,128)(2,1)}, bf16[384,768]{1,0:T(8,128)(2,1)}, bf16...) custom-call(s32[7]{0:T(128)} %copy-done.23, ...), custom_call_target="tpu_custom_call" | custom-call | flops 12000000000 | bytes 12000000 | tf_op jit(solution)/shard_map/pallas_call | solution.py:397
  216.4 7.7 %collective-permute-done.49 = bf16[128,1536]{1,0:T(8,128)(2,1)} collective-permute-done((bf16[128,1536]{1,0:T(8,128)(2,1)}, bf16[128,1536]{1,0:T(8,128)(2,1)}, u32[]{:S(2)}, u32[]{:S(2)}) %collective-permute-start.49) | collective-permute-done | bytes 393248 | tf_op jit(solution)/shard_map/ppermute | solution.py:311
  233.9 8.1 %all_to_all.57 = f32[8,1,256]{2,1,0:T(1,128)S(1)} all-to-all(f32[8,1,256]{2,1,0:T(1,128)} %all_to_all.48), channel_id=1, replica_groups=mesh['z'=4,'y'=2,'c'=2,'x'=2] {'y','c','x'}, dimensions={0} | all-to-all | bytes 16384 | tf_op jit(solution)/shard_map/all_to_all | solution.py:61
  249.7 6.4 %shard_map.234 = (f32[256,1536]{1,0:T(8,128)S(1)}, bf16[256,1536]{1,0:T(8,128)(2,1)S(1)}, bf16[256,1536]{1,0:T(8,128)(2,1)S(1)}, f32[1536,128]{1,0:T(8,128)S(1)}, f32[1,1536]{1,0:T(1,128)S(1)}) custom-call(s32[7]{0:T(128)S(1)} %copy-done.24, bf16[256,1536]{1,0:T(8,128)(2,1)S(1)} %copy-done.44, bf16[256,1536]{1,0:T(8,128)(2,1)} %collective-permute-done.31.far, ...), custom_call_target="tpu_custom_call" | custom-call | flops 6000000000 | bytes 6000000 | tf_op jit(solution)/shard_map/pallas_call | solution.py:397
  257.4 6.0 %shard_map.235.back = bf16[8,256,256]{2,1,0:T(8,128)(2,1)} custom-call(s32[7]{0:T(128)S(1)} %copy-done.24, bf16[256,1536]{1,0:T(8,128)(2,1)S(1)} %get-tuple-element.127.attended, bf16[12,256,256]{2,1,0:T(8,128)(2,1)S(1)} %copy-done.54, bf16[256,1536]{1,0:T(8,128)(2,1)S(1)} %copy-done.57, bf16[256,256]{1,0:T(8,128)(2,1)S(1)} %copy-done.59, ...), custom_call_target="tpu_custom_call" | custom-call | flops 12000000000 | bytes 12000000 | tf_op jit(solution)/shard_map/pallas_call | solution.py:397
  266.7 35.4 %collective-permute-done.53.refs_2_ = bf16[512,1536]{1,0:T(8,128)(2,1)} collective-permute-done((bf16[512,1536]{1,0:T(8,128)(2,1)}, bf16[512,1536]{1,0:T(8,128)(2,1)}, u32[]{:S(2)}, u32[]{:S(2)}) %collective-permute-start.53) | collective-permute-done | bytes 1572896 | tf_op jit(solution)/shard_map/ppermute | solution.py:311
  306.9 2.8 copy-done.31
  309.7 4.5 shard_map.237
  316.1 2.8 reshape.259
  318.9 4.1 all-to-all-start.1
  327.9 3.5 all-to-all-start.2
  333.9 9.6 %all-to-all-done.2 = bf16[8,256,192]{1,2,0:T(8,128)(2,1)S(1)} async-done(((bf16[8,256,192]{1,2,0:T(8,128)(2,1)}), bf16[8,256,192]{1,2,0:T(8,128)(2,1)S(1)}, u32[]{:S(2)}, u32[]{:S(2)}) %all-to-all-start.2) | async-done | bytes 786464 | tf_op jit(solution)/shard_map/all_to_all | solution.py:61
  343.5 4.2 all-to-all-start.3
  348.6 14.0 %all-to-all-done.3.qkv_cols = bf16[8,256,256]{2,1,0:T(8,128)(2,1)} async-done(((bf16[8,256,256]{2,1,0:T(8,128)(2,1)}), bf16[8,256,256]{2,1,0:T(8,128)(2,1)}, u32[]{:S(2)}, u32[]{:S(2)}) %all-to-all-start.3) | async-done | bytes 1048608 | tf_op jit(solution)/shard_map/all_to_all | solution.py:61
  362.7 9.3 %shard_map.238 = bf16[4,400,448]{2,1,0:T(8,128)(2,1)} custom-call(s32[7]{0:T(128)S(1)} %copy-done.25, bf16[4,16,448]{2,1,0:T(8,128)(2,1)S(1)} %convert_element_type.225.narrow, bf16[8,256,192]{2,1,0:T(8,128)(2,1)S(1)} %copy.125.branch_cols, bf16[8,256,256]{2,1,0:T(8,128)(2,1)} %all-to-all-done.3.qkv_cols, ...), custom_call_target="tpu_custom_call" | custom-call | flops 7000000000 | bytes 7000000 | tf_op jit(solution)/shard_map/pallas_call | solution.py:928
  377.9 7.7 %shard_map.239 = bf16[1536,768]{1,0:T(8,128)(2,1)} custom-call(s32[7]{0:T(128)S(1)} %copy-done.25, bf16[384,1536]{1,0:T(8,128)(2,1)S(1)} %copy-done.38, bf16[768,1536]{1,0:T(8,128)(2,1)} %get-tuple-element.156.refs_1_, bf16[384,1536]{1,0:T(8,128)(2,1)S(1)} %copy-done.43, bf16[384,768]{1,0:T(8,128)(2,1)S(1)} %copy-done.46, bf16[768,768]{1,0:T(8,128)(2,1)S(1)} %copy-done.39, ...), custom_call_target="tpu_custom_call" | custom-call | flops 6000000000 | bytes 6000000 | tf_op jit(solution)/shard_map/pallas_call | solution.py:397
  390.3 7.7 %shard_map.240 = bf16[1536,768]{1,0:T(8,128)(2,1)} custom-call(s32[7]{0:T(128)S(1)} %copy-done.25, bf16[384,1536]{1,0:T(8,128)(2,1)S(1)} %copy-done.35, bf16[768,1536]{1,0:T(8,128)(2,1)} %get-tuple-element.116.refs_1_, bf16[384,1536]{1,0:T(8,128)(2,1)S(1)} %copy-done.40, bf16[384,768]{1,0:T(8,128)(2,1)S(1)} %copy-done.48, bf16[768,768]{1,0:T(8,128)(2,1)S(1)} %copy-done.42, ...), custom_call_target="tpu_custom_call" | custom-call | flops 6000000000 | bytes 6000000 | tf_op jit(solution)/shard_map/pallas_call | solution.py:397
  400.9 8.4 %shard_map.236 = (bf16[256,1536]{1,0:T(8,128)(2,1)S(1)}, bf16[256,1536]{1,0:T(8,128)(2,1)S(1)}, bf16[256,1536]{1,0:T(8,128)(2,1)S(1)}, bf16[256,1536]{1,0:T(8,12...) custom-call(s32[7]{0:T(128)S(1)} %copy-done.25, ...), custom_call_target="tpu_custom_call" | custom-call | flops 10000000000 | bytes 10000000 | tf_op jit(solution)/shard_map/pallas_call | solution.py:397
  416.0 4.2 all-to-all-start.4
  426.2 7.7 %shard_map.241 = bf16[1536,768]{1,0:T(8,128)(2,1)} custom-call(s32[7]{0:T(128)S(1)} %copy-done.25, bf16[384,1536]{1,0:T(8,128)(2,1)S(1)} %copy-done.36, bf16[768,1536]{1,0:T(8,128)(2,1)} %get-tuple-element.116.refs_1_, bf16[384,1536]{1,0:T(8,128)(2,1)S(1)} %copy-done.41, bf16[384,768]{1,0:T(8,128)(2,1)S(1)} %copy-done.45, bf16[768,768]{1,0:T(8,128)(2,1)S(1)} %copy-done.37, ...), custom_call_target="tpu_custom_call" | custom-call | flops 6000000000 | bytes 6000000 | tf_op jit(solution)/shard_map/pallas_call | solution.py:397
  434.9 2.5 reduce-precision_convert_fusion.1
  445.5 5.0 collective-permute-done.64
  457.9 4.2 all-to-all-start.5
  462.1 7.5 %collective-permute-done.65 = bf16[128,1536]{1,0:T(8,128)(2,1)S(1)} collective-permute-done((bf16[128,1536]{1,0:T(8,128)(2,1)S(1)}, bf16[128,1536]{1,0:T(8,128)(2,1)S(1)}, u32[]{:S(2)}, u32[]{:S(2)}) %collective-permute-start.65) | collective-permute-done | bytes 393248 | tf_op jit(solution)/shard_map/ppermute | solution.py:311
  472.9 35.0 %reduce-scatter.11.cloned.1.call-done = bf16[384,768]{1,0:T(8,128)(2,1)} async-done(((bf16[1536,768]{1,0:T(8,128)(2,1)}), bf16[384,768]{1,0:T(8,128)(2,1)}) %reduce-scatter.11.cloned.1.call-update) | async-done | bytes 589840 | tf_op jit(solution)/shard_map/reduce_scatter | solution.py:65
  507.9 4.4 all-to-all-start.7
  512.3 2.7 fusion.2
  515.0 2.3 convert_element_type.230
  517.3 4.6 all-to-all-done.7
  521.9 2.2 convert_bitcast_fusion.1
  528.9 28.8 %reduce-scatter.9.cloned.1.call-done = bf16[384,768]{1,0:T(8,128)(2,1)} async-done(((bf16[1536,768]{1,0:T(8,128)(2,1)}), bf16[384,768]{1,0:T(8,128)(2,1)}) %reduce-scatter.9.cloned.1.call-update) | async-done | bytes 589840 | tf_op jit(solution)/shard_map/reduce_scatter | solution.py:65
  557.7 3.5 all-to-all-start.6
  565.2 5.5 all-to-all-done.6
  (446 shorter events, 166.4 us)
Async XLA Ops:
  15.9 13.2 %collective-permute-start.7 = (bf16[96,1792]{1,0:T(8,128)(2,1)S(1)}, bf16[96,1792]{1,0:T(8,128)(2,1)S(1)}, u32[]{:S(2)}, u32[]{:S(2)}) collective-permute-start(bf16[96,1792]{1,0:T(8,128)(2,1)S(1)} %pad_maximum_fusion.3), channel_id=1, source_target_pairs={{0,24},{8,0},{16,8},{24,16},{1,25},{9,1},{17,9},{25,17},{2,26},{10... | collective-permute-start | bytes 1032200 | tf_op jit(solution)/shard_map/ppermute | solution.py:317
  18.7 30.2 %collective-permute-start.6 = (bf16[96,1792]{1,0:T(8,128)(2,1)S(1)}, bf16[96,1792]{1,0:T(8,128)(2,1)S(1)}, u32[]{:S(2)}, u32[]{:S(2)}) collective-permute-start(bf16[96,1792]{1,0:T(8,128)(2,1)S(1)} %pad_maximum_fusion.3), channel_id=1, source_target_pairs={{0,16},{8,24},{16,0},{24,8},{1,17},{9,25},{17,1},{25,9},{2,18},{10... | collective-permute-start | bytes 1032200 | tf_op jit(solution)/shard_map/ppermute | solution.py:317
  20.4 28.5 %collective-permute-start.5 = (bf16[96,1792]{1,0:T(8,128)(2,1)S(1)}, bf16[96,1792]{1,0:T(8,128)(2,1)S(1)}, u32[]{:S(2)}, u32[]{:S(2)}) collective-permute-start(bf16[96,1792]{1,0:T(8,128)(2,1)S(1)} %pad_maximum_fusion.3), channel_id=1, source_target_pairs={{0,8},{8,16},{16,24},{24,0},{1,9},{9,17},{17,25},{25,1},{2,10},{10... | collective-permute-start | bytes 1032200 | tf_op jit(solution)/shard_map/ppermute | solution.py:317
  26.0 23.1 %collective-permute-start.8 = (bf16[256,1536]{1,0:T(8,128)(2,1)}, bf16[256,1536]{1,0:T(8,128)(2,1)}, u32[]{:S(2)}, u32[]{:S(2)}) collective-permute-start(bf16[256,1536]{1,0:T(8,128)(2,1)} %cot.1), channel_id=1, source_target_pairs={{0,1},{1,0},{2,3},{3,2},{4,5},{5,4},{6,7},{7,6},{8,9},{9,8},{10,11... | collective-permute-start | bytes 2359304 | tf_op jit(solution)/shard_map/ppermute | solution.py:311
  27.5 21.5 %collective-permute-start.9 = (bf16[256,1536]{1,0:T(8,128)(2,1)}, bf16[256,1536]{1,0:T(8,128)(2,1)}, u32[]{:S(2)}, u32[]{:S(2)}) collective-permute-start(bf16[256,1536]{1,0:T(8,128)(2,1)} %cot.1), channel_id=1, source_target_pairs={{0,4},{4,0},{1,5},{5,1},{2,6},{6,2},{3,7},{7,3},{8,12},{12,8},{9,1... | collective-permute-start | bytes 2359304 | tf_op jit(solution)/shard_map/ppermute | solution.py:311
  49.1 18.9 %collective-permute-start.10 = (bf16[4,96,1024]{2,1,0:T(8,128)(2,1)S(1)}, bf16[4,96,1024]{2,1,0:T(8,128)(2,1)S(1)}, u32[]{:S(2)}, u32[]{:S(2)}) collective-permute-start(bf16[4,96,1024]{2,1,0:T(8,128)(2,1)S(1)} %pad_maximum_fusion.refs_0_), channel_id=1, source_target_pairs={{0,1},{1,0},{2,3},{3,2},{4,5},{5,4},{6,7},{7,6},{8,9},{9,8},{10,11... | collective-permute-start | bytes 2359304 | tf_op jit(solution)/shard_map/ppermute | solution.py:311
  50.6 17.3 %collective-permute-start.11 = (bf16[4,96,1024]{2,1,0:T(8,128)(2,1)S(1)}, bf16[4,96,1024]{2,1,0:T(8,128)(2,1)S(1)}, u32[]{:S(2)}, u32[]{:S(2)}) collective-permute-start(bf16[4,96,1024]{2,1,0:T(8,128)(2,1)S(1)} %pad_maximum_fusion.refs_0_), channel_id=1, source_target_pairs={{0,4},{4,0},{1,5},{5,1},{2,6},{6,2},{3,7},{7,3},{8,12},{12,8},{9,1... | collective-permute-start | bytes 2359304 | tf_op jit(solution)/shard_map/ppermute | solution.py:311
  76.6 15.8 %collective-permute-start.18 = (bf16[4,96,768]{2,1,0:T(8,128)(2,1)S(1)}, bf16[4,96,768]{2,1,0:T(8,128)(2,1)S(1)}, u32[]{:S(2)}, u32[]{:S(2)}) collective-permute-start(bf16[4,96,768]{2,1,0:T(8,128)(2,1)S(1)} %pad_maximum_fusion.2.refs_0_), channel_id=1, source_target_pairs={{0,1},{1,0},{2,3},{3,2},{4,5},{5,4},{6,7},{7,6},{8,9},{9,8},{10,11... | collective-permute-start | bytes 1769480 | tf_op jit(solution)/shard_map/ppermute | solution.py:311
  78.2 15.4 %collective-permute-start.19 = (bf16[4,96,768]{2,1,0:T(8,128)(2,1)S(1)}, bf16[4,96,768]{2,1,0:T(8,128)(2,1)S(1)}, u32[]{:S(2)}, u32[]{:S(2)}) collective-permute-start(bf16[4,96,768]{2,1,0:T(8,128)(2,1)S(1)} %pad_maximum_fusion.2.refs_0_), channel_id=1, source_target_pairs={{0,4},{4,0},{1,5},{5,1},{2,6},{6,2},{3,7},{7,3},{8,12},{12,8},{9,1... | collective-permute-start | bytes 1769480 | tf_op jit(solution)/shard_map/ppermute | solution.py:311
  101.0 15.4 %collective-permute-start.22 = (bf16[4,96,768]{2,1,0:T(8,128)(2,1)S(1)}, bf16[4,96,768]{2,1,0:T(8,128)(2,1)S(1)}, u32[]{:S(2)}, u32[]{:S(2)}) collective-permute-start(bf16[4,96,768]{2,1,0:T(8,128)(2,1)S(1)} %copy-done.8), channel_id=1, source_target_pairs={{0,2},{2,0},{1,3},{3,1},{4,6},{6,4},{5,7},{7,5},{8,10},{10,8},{9,1... | collective-permute-start | bytes 1769480 | tf_op jit(solution)/shard_map/ppermute | solution.py:311
  116.3 47.0 %collective-permute-start.36 = (bf16[256,1536]{1,0:T(8,128)(2,1)}, bf16[256,1536]{1,0:T(8,128)(2,1)}, u32[]{:S(2)}, u32[]{:S(2)}) collective-permute-start(bf16[256,1536]{1,0:T(8,128)(2,1)} %collective-permute-done.8.refs_4_), channel_id=1, source_target_pairs={{0,2},{2,0},{1,3},{3,1},{4,6},{6,4},{5,7},{7,5},{8,10},{10,8},{9,1... | collective-permute-start | bytes 2359304 | tf_op jit(solution)/shard_map/ppermute | solution.py:311
  116.8 47.0 %collective-permute-start.37 = (bf16[256,1536]{1,0:T(8,128)(2,1)}, bf16[256,1536]{1,0:T(8,128)(2,1)}, u32[]{:S(2)}, u32[]{:S(2)}) collective-permute-start(bf16[256,1536]{1,0:T(8,128)(2,1)} %collective-permute-done.9.refs_6_), channel_id=1, source_target_pairs={{0,2},{2,0},{1,3},{3,1},{4,6},{6,4},{5,7},{7,5},{8,10},{10,8},{9,1... | collective-permute-start | bytes 2359304 | tf_op jit(solution)/shard_map/ppermute | solution.py:311
  116.9 31.9 %collective-permute-start.45 = (bf16[128,1536]{1,0:T(8,128)(2,1)}, bf16[128,1536]{1,0:T(8,128)(2,1)}, u32[]{:S(2)}, u32[]{:S(2)}) collective-permute-start(bf16[128,1536]{1,0:T(8,128)(2,1)} %slice.231), channel_id=1, source_target_pairs={{0,1},{1,0},{2,3},{3,2},{4,5},{5,4},{6,7},{7,6},{8,9},{9,8},{10,11... | collective-permute-start | bytes 1179656 | tf_op jit(solution)/shard_map/ppermute | solution.py:311
  127.9 20.2 %collective-permute-start.32 = (bf16[256,1536]{1,0:T(8,128)(2,1)}, bf16[256,1536]{1,0:T(8,128)(2,1)}, u32[]{:S(2)}, u32[]{:S(2)}) collective-permute-start(bf16[256,1536]{1,0:T(8,128)(2,1)} %get-tuple-element.102.refs_0_.second), channel_id=1, source_target_pairs={{0,1},{1,0},{2,3},{3,2},{4,5},{5,4},{6,7},{7,6},{8,9},{9,8},{10,11... | collective-permute-start | bytes 2359304 | tf_op jit(solution)/shard_map/ppermute | solution.py:311
  128.3 19.9 %collective-permute-start.33 = (bf16[256,1536]{1,0:T(8,128)(2,1)}, bf16[256,1536]{1,0:T(8,128)(2,1)}, u32[]{:S(2)}, u32[]{:S(2)}) collective-permute-start(bf16[256,1536]{1,0:T(8,128)(2,1)} %get-tuple-element.102.refs_0_.second), channel_id=1, source_target_pairs={{0,4},{4,0},{1,5},{5,1},{2,6},{6,2},{3,7},{7,3},{8,12},{12,8},{9,1... | collective-permute-start | bytes 2359304 | tf_op jit(solution)/shard_map/ppermute | solution.py:311
  148.3 16.0 %collective-permute-start.34 = (bf16[256,1536]{1,0:T(8,128)(2,1)}, bf16[256,1536]{1,0:T(8,128)(2,1)}, u32[]{:S(2)}, u32[]{:S(2)}) collective-permute-start(bf16[256,1536]{1,0:T(8,128)(2,1)} %collective-permute-done.32.refs_0_), channel_id=1, source_target_pairs={{0,2},{2,0},{1,3},{3,1},{4,6},{6,4},{5,7},{7,5},{8,10},{10,8},{9,1... | collective-permute-start | bytes 2359304 | tf_op jit(solution)/shard_map/ppermute | solution.py:311
  148.3 17.5 %collective-permute-start.35 = (bf16[256,1536]{1,0:T(8,128)(2,1)}, bf16[256,1536]{1,0:T(8,128)(2,1)}, u32[]{:S(2)}, u32[]{:S(2)}) collective-permute-start(bf16[256,1536]{1,0:T(8,128)(2,1)} %collective-permute-done.33.refs_2_), channel_id=1, source_target_pairs={{0,2},{2,0},{1,3},{3,1},{4,6},{6,4},{5,7},{7,5},{8,10},{10,8},{9,1... | collective-permute-start | bytes 2359304 | tf_op jit(solution)/shard_map/ppermute | solution.py:311
  161.0 32.9 %collective-permute-start.47 = (bf16[256,1536]{1,0:T(8,128)(2,1)S(1)}, bf16[256,1536]{1,0:T(8,128)(2,1)}, u32[]{:S(2)}, u32[]{:S(2)}) collective-permute-start(bf16[256,1536]{1,0:T(8,128)(2,1)S(1)} %constant_dynamic-update-slice_fusion.16.refs_2_), channel_id=1, source_target_pairs={{0,2},{2,0},{1,3},{3,1},{4,6},{6,4},{5,7},{7,5},{8,10},{10,8},{9,1... | collective-permute-start | bytes 2359304 | tf_op jit(solution)/shard_map/ppermute | solution.py:311
  163.4 82.9 %collective-permute-start.31 = (bf16[256,1536]{1,0:T(8,128)(2,1)}, bf16[256,1536]{1,0:T(8,128)(2,1)}, u32[]{:S(2)}, u32[]{:S(2)}) collective-permute-start(bf16[256,1536]{1,0:T(8,128)(2,1)} %get-tuple-element.106), channel_id=1, source_target_pairs={{0,2},{2,0},{1,3},{3,1},{4,6},{6,4},{5,7},{7,5},{8,10},{10,8},{9,1... | collective-permute-start | bytes 2359304 | tf_op jit(solution)/shard_map/ppermute | solution.py:311
  163.7 23.9 %collective-permute-start.43 = (bf16[128,1536]{1,0:T(8,128)(2,1)S(1)}, bf16[128,1536]{1,0:T(8,128)(2,1)S(1)}, u32[]{:S(2)}, u32[]{:S(2)}) collective-permute-start(bf16[128,1536]{1,0:T(8,128)(2,1)S(1)} %slice.181), channel_id=1, source_target_pairs={{0,4},{4,0},{1,5},{5,1},{2,6},{6,2},{3,7},{7,3},{8,12},{12,8},{9,1... | collective-permute-start | bytes 1179656 | tf_op jit(solution)/shard_map/ppermute | solution.py:311
  164.2 23.4 %collective-permute-start.42 = (bf16[128,1536]{1,0:T(8,128)(2,1)S(1)}, bf16[128,1536]{1,0:T(8,128)(2,1)S(1)}, u32[]{:S(2)}, u32[]{:S(2)}) collective-permute-start(bf16[128,1536]{1,0:T(8,128)(2,1)S(1)} %slice.180), channel_id=1, source_target_pairs={{0,1},{1,0},{2,3},{3,2},{4,5},{5,4},{6,7},{7,6},{8,9},{9,8},{10,11... | collective-permute-start | bytes 1179656 | tf_op jit(solution)/shard_map/ppermute | solution.py:311
  190.7 55.6 %collective-permute-start.39 = (bf16[128,1536]{1,0:T(8,128)(2,1)}, bf16[128,1536]{1,0:T(8,128)(2,1)}, u32[]{:S(2)}, u32[]{:S(2)}) collective-permute-start(bf16[128,1536]{1,0:T(8,128)(2,1)} %slice.228), channel_id=1, source_target_pairs={{0,1},{1,0},{2,3},{3,2},{4,5},{5,4},{6,7},{7,6},{8,9},{9,8},{10,11... | collective-permute-start | bytes 1179656 | tf_op jit(solution)/shard_map/ppermute | solution.py:311
  192.4 53.9 %collective-permute-start.41 = (bf16[128,1536]{1,0:T(8,128)(2,1)}, bf16[128,1536]{1,0:T(8,128)(2,1)}, u32[]{:S(2)}, u32[]{:S(2)}) collective-permute-start(bf16[128,1536]{1,0:T(8,128)(2,1)} %slice.229), channel_id=1, source_target_pairs={{0,4},{4,0},{1,5},{5,1},{2,6},{6,2},{3,7},{7,3},{8,12},{12,8},{9,1... | collective-permute-start | bytes 1179656 | tf_op jit(solution)/shard_map/ppermute | solution.py:311
  226.1 20.2 %collective-permute-start.50 = (bf16[128,1536]{1,0:T(8,128)(2,1)}, bf16[128,1536]{1,0:T(8,128)(2,1)}, u32[]{:S(2)}, u32[]{:S(2)}) collective-permute-start(bf16[128,1536]{1,0:T(8,128)(2,1)} %reduce-precision_convert_fusion.10), channel_id=1, source_target_pairs={{0,4},{4,0},{1,5},{5,1},{2,6},{6,2},{3,7},{7,3},{8,12},{12,8},{9,1... | collective-permute-start | bytes 1179656 | tf_op jit(solution)/shard_map/ppermute | solution.py:311
  229.2 17.1 %collective-permute-start.52 = (bf16[128,1536]{1,0:T(8,128)(2,1)}, bf16[128,1536]{1,0:T(8,128)(2,1)}, u32[]{:S(2)}, u32[]{:S(2)}) collective-permute-start(bf16[128,1536]{1,0:T(8,128)(2,1)} %reduce-precision_convert_fusion.9), channel_id=1, source_target_pairs={{0,1},{1,0},{2,3},{3,2},{4,5},{5,4},{6,7},{7,6},{8,9},{9,8},{10,11... | collective-permute-start | bytes 1179656 | tf_op jit(solution)/shard_map/ppermute | solution.py:311
  265.4 36.7 %collective-permute-start.53 = (bf16[512,1536]{1,0:T(8,128)(2,1)}, bf16[512,1536]{1,0:T(8,128)(2,1)}, u32[]{:S(2)}, u32[]{:S(2)}) collective-permute-start(bf16[512,1536]{1,0:T(8,128)(2,1)} %constant_dynamic-update-slice_fusion.26.refs_0_), channel_id=1, source_target_pairs={{0,4},{4,0},{1,5},{5,1},{2,6},{6,2},{3,7},{7,3},{8,12},{12,8},{9,1... | collective-permute-start | bytes 4718600 | tf_op jit(solution)/shard_map/ppermute | solution.py:311
  265.9 38.2 %collective-permute-start.54 = (bf16[512,1536]{1,0:T(8,128)(2,1)}, bf16[512,1536]{1,0:T(8,128)(2,1)}, u32[]{:S(2)}, u32[]{:S(2)}) collective-permute-start(bf16[512,1536]{1,0:T(8,128)(2,1)} %constant_dynamic-update-slice_fusion.26.refs_0_), channel_id=1, source_target_pairs={{0,1},{1,0},{2,3},{3,2},{4,5},{5,4},{6,7},{7,6},{8,9},{9,8},{10,11... | collective-permute-start | bytes 4718600 | tf_op jit(solution)/shard_map/ppermute | solution.py:311
  266.5 96.2 %collective-permute-start.67 = (bf16[512,1536]{1,0:T(8,128)(2,1)}, bf16[512,1536]{1,0:T(8,128)(2,1)}, u32[]{:S(2)}, u32[]{:S(2)}) collective-permute-start(bf16[512,1536]{1,0:T(8,128)(2,1)} %constant_dynamic-update-slice_fusion.26.refs_0_), channel_id=1, source_target_pairs={{0,2},{2,0},{1,3},{3,1},{4,6},{6,4},{5,7},{7,5},{8,10},{10,8},{9,1... | collective-permute-start | bytes 4718600 | tf_op jit(solution)/shard_map/ppermute | solution.py:311
  306.2 19.0 %collective-permute-start.55 = (bf16[256,1536]{1,0:T(8,128)(2,1)}, bf16[256,1536]{1,0:T(8,128)(2,1)}, u32[]{:S(2)}, u32[]{:S(2)}) collective-permute-start(bf16[256,1536]{1,0:T(8,128)(2,1)} %slice.236), channel_id=1, source_target_pairs={{0,1},{1,0},{2,3},{3,2},{4,5},{5,4},{6,7},{7,6},{8,9},{9,8},{10,11... | collective-permute-start | bytes 2359304 | tf_op jit(solution)/shard_map/ppermute | solution.py:311
  306.6 24.8 %collective-permute-start.56 = (bf16[256,1536]{1,0:T(8,128)(2,1)}, bf16[256,1536]{1,0:T(8,128)(2,1)}, u32[]{:S(2)}, u32[]{:S(2)}) collective-permute-start(bf16[256,1536]{1,0:T(8,128)(2,1)} %slice.237), channel_id=1, source_target_pairs={{0,4},{4,0},{1,5},{5,1},{2,6},{6,2},{3,7},{7,3},{8,12},{12,8},{9,1... | collective-permute-start | bytes 2359304 | tf_op jit(solution)/shard_map/ppermute | solution.py:311
  324.2 38.5 %collective-permute-start.68 = (bf16[512,1536]{1,0:T(8,128)(2,1)}, bf16[512,1536]{1,0:T(8,128)(2,1)}, u32[]{:S(2)}, u32[]{:S(2)}) collective-permute-start(bf16[512,1536]{1,0:T(8,128)(2,1)} %collective-permute-done.54.refs_1_), channel_id=1, source_target_pairs={{0,2},{2,0},{1,3},{3,1},{4,6},{6,4},{5,7},{7,5},{8,10},{10,8},{9,1... | collective-permute-start | bytes 4718600 | tf_op jit(solution)/shard_map/ppermute | solution.py:311
  324.7 38.0 %collective-permute-start.69 = (bf16[512,1536]{1,0:T(8,128)(2,1)}, bf16[512,1536]{1,0:T(8,128)(2,1)}, u32[]{:S(2)}, u32[]{:S(2)}) collective-permute-start(bf16[512,1536]{1,0:T(8,128)(2,1)} %collective-permute-done.53.refs_2_), channel_id=1, source_target_pairs={{0,2},{2,0},{1,3},{3,1},{4,6},{6,4},{5,7},{7,5},{8,10},{10,8},{9,1... | collective-permute-start | bytes 4718600 | tf_op jit(solution)/shard_map/ppermute | solution.py:311
  327.9 15.6 %all-to-all-start.2 = ((bf16[8,256,192]{1,2,0:T(8,128)(2,1)}), bf16[8,256,192]{1,2,0:T(8,128)(2,1)S(1)}, u32[]{:S(2)}, u32[]{:S(2)}) async-start(bf16[8,256,192]{1,2,0:T(8,128)(2,1)} %bitcast.44), calls=%async_computation.2 | async-start | bytes 1572864 | tf_op jit(solution)/shard_map/all_to_all | solution.py:61
  333.5 29.2 %collective-permute-start.70 = (bf16[512,1536]{1,0:T(8,128)(2,1)}, bf16[512,1536]{1,0:T(8,128)(2,1)}, u32[]{:S(2)}, u32[]{:S(2)}) collective-permute-start(bf16[512,1536]{1,0:T(8,128)(2,1)} %constant_dynamic-update-slice_fusion.28.refs_3_), channel_id=1, source_target_pairs={{0,2},{2,0},{1,3},{3,1},{4,6},{6,4},{5,7},{7,5},{8,10},{10,8},{9,1... | collective-permute-start | bytes 4718600 | tf_op jit(solution)/shard_map/ppermute | solution.py:311
  343.5 19.2 %all-to-all-start.3 = ((bf16[8,256,256]{2,1,0:T(8,128)(2,1)}), bf16[8,256,256]{2,1,0:T(8,128)(2,1)}, u32[]{:S(2)}, u32[]{:S(2)}) async-start(bf16[8,256,256]{2,1,0:T(8,128)(2,1)} %shard_map.235.back), calls=%async_computation.3 | async-start | bytes 2097152 | tf_op jit(solution)/shard_map/all_to_all | solution.py:61
  347.7 65.2 %reduce-scatter.5.cloned.1.call-start = ((), (), s32[]{:S(2)}) async-start(), calls=%async_computation.12 | async-start | bytes 2048000 | tf_op jit(solution)/shard_map/reduce_scatter | solution.py:65
  372.0 86.0 %reduce-scatter.7.cloned.1.call-start = ((), (), s32[]{:S(2)}) async-start(), calls=%async_computation.13 | async-start | bytes 2949120 | tf_op jit(solution)/shard_map/reduce_scatter | solution.py:65
  398.0 109.9 %reduce-scatter.11.cloned.1.call-start = ((), (), s32[]{:S(2)}) async-start(), calls=%async_computation.15 | async-start | bytes 2949120 | tf_op jit(solution)/shard_map/reduce_scatter | solution.py:65
  412.9 22.0 %collective-permute-start.60 = (bf16[256,1536]{1,0:T(8,128)(2,1)}, bf16[256,1536]{1,0:T(8,128)(2,1)}, u32[]{:S(2)}, u32[]{:S(2)}) collective-permute-start(bf16[256,1536]{1,0:T(8,128)(2,1)} %get-tuple-element.144), channel_id=1, source_target_pairs={{0,2},{2,0},{1,3},{3,1},{4,6},{6,4},{5,7},{7,5},{8,10},{10,8},{9,1... | collective-permute-start | bytes 2359304 | tf_op jit(solution)/shard_map/ppermute | solution.py:311
  416.0 21.4 %all-to-all-start.4 = ((bf16[8,112,448]{2,1,0:T(8,128)(2,1)}), bf16[8,112,448]{2,1,0:T(8,128)(2,1)}, u32[]{:S(2)}, u32[]{:S(2)}) async-start(bf16[8,112,448]{2,1,0:T(8,128)(2,1)} %maximum_maximum_fusion), calls=%async_computation.5 | async-start | bytes 1835008 | tf_op jit(solution)/shard_map/all_to_all | solution.py:61
  420.2 137.5 %reduce-scatter.9.cloned.1.call-start = ((), (), s32[]{:S(2)}) async-start(), calls=%async_computation.14 | async-start | bytes 2949120 | tf_op jit(solution)/shard_map/reduce_scatter | solution.py:65
  434.4 78.0 %collective-permute-start.66 = (bf16[256,1536]{1,0:T(8,128)(2,1)}, bf16[256,1536]{1,0:T(8,128)(2,1)}, u32[]{:S(2)}, u32[]{:S(2)}) collective-permute-start(bf16[256,1536]{1,0:T(8,128)(2,1)} %copy-done.29), channel_id=1, source_target_pairs={{0,2},{2,0},{1,3},{3,1},{4,6},{6,4},{5,7},{7,5},{8,10},{10,8},{9,1... | collective-permute-start | bytes 2359304 | tf_op jit(solution)/shard_map/ppermute | solution.py:311
  441.5 20.6 %collective-permute-start.63 = (bf16[128,1536]{1,0:T(8,128)(2,1)S(1)}, bf16[128,1536]{1,0:T(8,128)(2,1)}, u32[]{:S(2)}, u32[]{:S(2)}) collective-permute-start(bf16[128,1536]{1,0:T(8,128)(2,1)S(1)} %slice.241), channel_id=1, source_target_pairs={{0,4},{4,0},{1,5},{5,1},{2,6},{6,2},{3,7},{7,3},{8,12},{12,8},{9,1... | collective-permute-start | bytes 1179656 | tf_op jit(solution)/shard_map/ppermute | solution.py:311
  445.0 25.8 %collective-permute-start.58 = (bf16[128,1536]{1,0:T(8,128)(2,1)S(1)}, bf16[128,1536]{1,0:T(8,128)(2,1)}, u32[]{:S(2)}, u32[]{:S(2)}) collective-permute-start(bf16[128,1536]{1,0:T(8,128)(2,1)S(1)} %slice.238), channel_id=1, source_target_pairs={{0,1},{1,0},{2,3},{3,2},{4,5},{5,4},{6,7},{7,6},{8,9},{9,8},{10,11... | collective-permute-start | bytes 1179656 | tf_op jit(solution)/shard_map/ppermute | solution.py:311
  450.7 19.0 %collective-permute-start.65 = (bf16[128,1536]{1,0:T(8,128)(2,1)S(1)}, bf16[128,1536]{1,0:T(8,128)(2,1)S(1)}, u32[]{:S(2)}, u32[]{:S(2)}) collective-permute-start(bf16[128,1536]{1,0:T(8,128)(2,1)S(1)} %reduce-precision_convert_fusion.7), channel_id=1, source_target_pairs={{0,1},{1,0},{2,3},{3,2},{4,5},{5,4},{6,7},{7,6},{8,9},{9,8},{10,11... | collective-permute-start | bytes 1179656 | tf_op jit(solution)/shard_map/ppermute | solution.py:311
  454.9 15.8 %collective-permute-start.62 = (bf16[128,1536]{1,0:T(8,128)(2,1)}, bf16[128,1536]{1,0:T(8,128)(2,1)}, u32[]{:S(2)}, u32[]{:S(2)}) collective-permute-start(bf16[128,1536]{1,0:T(8,128)(2,1)} %reduce-precision_convert_fusion.8), channel_id=1, source_target_pairs={{0,4},{4,0},{1,5},{5,1},{2,6},{6,2},{3,7},{7,3},{8,12},{12,8},{9,1... | collective-permute-start | bytes 1179656 | tf_op jit(solution)/shard_map/ppermute | solution.py:311
  457.9 50.0 %all-to-all-start.5 = ((bf16[4,96,768]{2,1,0:T(8,128)(2,1)}), bf16[4,96,768]{2,1,0:T(8,128)(2,1)}, u32[]{:S(2)}, u32[]{:S(2)}) async-start(bf16[4,96,768]{2,1,0:T(8,128)(2,1)} %bitcast.129), calls=%async_computation.7 | async-start | bytes 1179648 | tf_op jit(solution)/shard_map/all_to_all | solution.py:61
  507.9 14.0 %all-to-all-start.7 = ((bf16[4,96,768]{2,1,0:T(8,128)(2,1)}), bf16[4,96,768]{2,1,0:T(8,128)(2,1)}, u32[]{:S(2)}, u32[]{:S(2)}) async-start(bf16[4,96,768]{2,1,0:T(8,128)(2,1)} %bitcast.128), calls=%async_computation.11 | async-start | bytes 1179648 | tf_op jit(solution)/shard_map/all_to_all | solution.py:61
  (114 other events, 1177.8 us)
Sparse Core Ops, SparseCore 0:
  372.1 36.3 reduce-scatter.4
  410.8 47.0 reduce-scatter.6
  460.3 47.5 reduce-scatter.10
  510.2 47.5 reduce-scatter.8
where the time goes:
time: 591 us; the launch traced here: 579 us
  waiting for transfers between devices  226 us (38%)
  Pallas kernels  116 us (20%)
  local copies, waits for them, and re-layouts  97.7 us (17%)
  starting transfers between devices  81.4 us (14%)
  other arithmetic  33.3 us (6%)
  between operations  16.2 us (3%)
  blocking collectives  8.08 us (1%)
    pallas_call x12, Pallas kernels, run_kernel(): pl.pallas_call(kernel, out_shape=[jax.ShapeDtypeStruct(shape, dtype) for...  107 us
    ppermute x65, waiting for transfers between devices, swap(): return lax.ppermute(block, axis, [(0, 1), (1, 0)])  106 us
    reduce_scatter x4, waiting for transfers between devices, scatter_sum(): return lax.psum_scatter(block, axes, scatter_dimension=0, tiled=True)  65.3 us
    unnamed x181, local copies, waits for them, and re-layouts  44.7 us
    ppermute x65, starting transfers between devices, swap(): return lax.ppermute(block, axis, [(0, 1), (1, 0)])  42.8 us
    all_to_all x7, waiting for transfers between devices, exchange(): return lax.all_to_all(block, axes, split_axis=0, concat_axis=0, tiled=True)  34.2 us
    all_to_all x7, starting transfers between devices, exchange(): return lax.all_to_all(block, axes, split_axis=0, concat_axis=0, tiled=True)  28.1 us
    ppermute x6, waiting for transfers between devices, shifts(): lax.ppermute(block, 'z', [(i, (i + k) % depth) for i in range(depth)])  19.8 us
  transfers between devices with their start and end apart: 82, of which 29 were waited for; matrix products, arithmetic and copies ran while one was open for 16% of the time, Pallas kernels for 16%

commit v1 on v0

--- a/solution.py
+++ b/solution.py
@@ -376,7 +376,8 @@
 
 def corner_last(over_x, over_y, first):
     half = over_x.shape[0] // 2
-    return swap(add(over_y[:half], first[0]), "y"), swap(add(over_x[half:], first[1]), "x")
+    over_y, over_x = add(over_y[:half], first[0]), add(over_x[half:], first[1])
+    return swap(over_y, "y"), swap(over_x, "x"), over_x
 
 
 def cost(micros):
@@ -495,10 +496,8 @@
 def expert_kernel(capacity, pieces, at, slots, bias, router, gate_w, up_w, down_w, *refs):
     count = len(pieces)
     second, cot = refs[:count], refs[count : 2 * count]
-    rows_in, rows_cot, gated_ref, gate_back, up_back, signal_ref, gates_ref = refs[
-        2 * count : 2 * count + 7
-    ]
-    backs = refs[2 * count + 7 : -1]
+    rows_in, rows_cot, gated_ref, gate_back, up_back, gates_ref = refs[2 * count : 2 * count + 6]
+    backs = refs[2 * count + 6 : -1]
     gate_rows = refs[-1]
     f32, bf16 = jnp.float32, jnp.bfloat16
     length = second[0].shape[0]
@@ -539,24 +538,24 @@
     back = gate * cot_hidden
     gate_back[...] = (back * up_pre * slope).astype(bf16)
     up_back[...] = (back * active).astype(bf16)
-    for n in range(2 * count):
-        block = 2 * pieces[n // 2] + n % 2
-        pick = one_hot(slots[block : block + 1], capacity, f32)
-        own = signal[n * capacity : (n + 1) * capacity]
-        signal_ref[n : n + 1] = jnp.sum(pick * own, axis=0, keepdims=True)
+    high = signal.astype(bf16)
+    low = (signal - high.astype(f32)).astype(bf16)
+    lanes = lax.broadcasted_iota(jnp.int32, (signal.shape[0], bias.shape[1]), 1)
+    signal = jnp.where(lanes == at[5], high.astype(f32), 0.0)
+    signal = jnp.where(lanes == at[5] + bias.shape[1] // 2, low.astype(f32), signal)
     by_rows = ((1,), (1,))
     rows = dot(gate_back[...], gate_w[...], by_rows) + dot(up_back[...], up_w[...], by_rows)
-    spread(slots, pieces, capacity, rows, backs)
+    spread(slots, pieces, capacity, jnp.concatenate([rows, signal], axis=1), backs)
 
 
 def run_expert(pieces, at, slots, bias, router, weights, second, cot, capacity):
     count = len(pieces)
-    rows, lanes = 2 * count * capacity, slots.shape[1]
+    rows = 2 * count * capacity
     (length, width), hidden = second[0].shape, weights[0].shape[1]
     bf16, f32 = jnp.bfloat16, jnp.float32
     outs = [(rows, width)] * 2 + [(rows, hidden)] * 3
-    outs = [(shape, bf16) for shape in outs] + [((8, lanes), f32), ((length, lanes), f32)]
-    outs = outs + [((length, width), bf16)] * count
+    outs = [(shape, bf16) for shape in outs] + [((length, bias.shape[1]), f32)]
+    outs = outs + [((length, width + bias.shape[1]), bf16)] * count
     return run_kernel(
         functools.partial(expert_kernel, capacity, pieces),
         6 * count,
@@ -575,32 +574,54 @@
         spread(slots, pieces, capacity, rows, [outs[piece] for piece in pieces])
 
 
-def row_sum_kernel(at, *refs):
-    half = len(refs) // 2
-    total = sum(
-        dot(left[...], right[...], ((0,), (0,))) for left, right in zip(refs[:half], refs[half:-1])
-    )
-    refs[-1][...] = total.astype(jnp.bfloat16)
-
-
-def row_sum(at, lefts, rights):
-    shape = (lefts[0].shape[1], rights[0].shape[1])
-    return run_kernel(row_sum_kernel, 6, at, (*lefts, *rights), [(shape, jnp.bfloat16)], 48)[0]
+def row_sum_kernel(counts, at, *refs):
+    parts = len(counts)
+    rights = len(refs) // (parts + 2) - 1
+    sources, outs = refs[: parts * (rights + 1)], refs[parts * (rights + 1) : -rights - 2]
+    held, sems = refs[-rights - 2 : -1], refs[-1]
+    copies = []
+    for n, source in enumerate(sources):
+        array, part = divmod(n, parts)
+        target = held[array].at[pl.ds(sum(counts[:part]), counts[part])]
+        copies.append(pltpu.make_async_copy(source, target, sems.at[n]))
+        copies[-1].start()
+    for copy in copies:
+        copy.wait()
+    for out, right in zip(outs, held[1:]):
+        out[...] = dot(held[0][...], right[...], ((0,), (0,))).astype(jnp.bfloat16)
+
+
+def row_sums(at, left, *rights):
+    counts = [part.shape[0] for part in left]
+    widths = [parts[0].shape[1] for parts in (left, *rights)]
+    sources = [part for parts in (left, *rights) for part in parts]
+    anywhere = pl.BlockSpec(memory_space=pl.ANY)
+    return pl.pallas_call(
+        functools.partial(row_sum_kernel, counts),
+        out_shape=[jax.ShapeDtypeStruct((widths[0], width), jnp.bfloat16) for width in widths[1:]],
+        in_specs=[SCALARS] + [anywhere] * len(sources),
+        out_specs=[WHOLE] * len(rights),
+        scratch_shapes=[pltpu.VMEM((sum(counts), width), jnp.bfloat16) for width in widths]
+        + [pltpu.SemaphoreType.DMA((len(sources),))],
+        cost_estimate=cost(6 * len(rights)),
+        compiler_params=pltpu.CompilerParams(vmem_limit_bytes=40 * 2**20),
+    )(at, *sources)
 
 
 def branch_back_kernel(
-    at, near, far, first_x, first_y, last_y, last_x, resid, gain, second, gates, signal, router, cot, weight, *outs
+    at, near, far, first_x, first_y, last_y, last_x, resid, gain, second, gates, router, cot, weight, *outs
 ):
     resid_grad_ref, branch_ref, attended_ref, router_ref, gain_ref = outs
     f32, bf16 = jnp.float32, jnp.bfloat16
+    halves = [first_x[...].astype(f32) + last_y[...], first_y[...].astype(f32) + last_x[...]]
+    total = near[...].astype(f32) + far[...] + jnp.concatenate(halves, axis=0)
+    width = resid.shape[1]
+    signal = total[:, width:]
+    signal = signal + pltpu.roll(signal, signal.shape[1] // 2, 1)
     chosen = gates[...]
-    logit_grad = chosen * (
-        signal[...] - jnp.sum(chosen * signal[...], axis=-1, keepdims=True)
-    )
+    logit_grad = chosen * (signal - jnp.sum(chosen * signal, axis=-1, keepdims=True))
     logit_grad = logit_grad.astype(bf16)
-    halves = [first_x[...].astype(f32) + last_y[...], first_y[...].astype(f32) + last_x[...]]
-    second_grad = near[...].astype(f32) + far[...] + jnp.concatenate(halves, axis=0)
-    second_grad = second_grad + dot(logit_grad, router[...], ((1,), (1,)))
+    second_grad = total[:, :width] + dot(logit_grad, router[...], ((1,), (1,)))
     norm_grad, gain_grad = rms_back(resid[...], gain[...], second_grad)
     gain_ref[...] = gain_grad
     resid_grad = cot[...].astype(f32) + norm_grad
@@ -730,8 +751,9 @@
     )
     narrow = jnp.concatenate([w_router, norm1_gain[:, None], norm2_gain[:, None]], axis=1)
     narrow = small_group_gather(narrow)
+    ids_all = small_gather(expert_ids)
     column = [own_half] + shifts(own_half)
-    cot_sides = plane_sides(after(out_grad, narrow))
+    cot_sides = plane_sides(after(out_grad, narrow, ids_all))
     qkv_half = qkv_cols // 2
     qkv_column = jnp.stack([part[:, :qkv_half] for part in column])
     out_column = jnp.stack([part[:, qkv_half:] for part in column])
@@ -780,7 +802,6 @@
     qkv_w = qkv_w.reshape(HK, model_width, qkv_half)
     output_w = output_w.reshape(2, q_cols, out_half)
 
-    ids_all = small_gather(after(expert_ids, out_corner))
     cot_corner = plane_corner(cot_sides, (out_corner,))
     cot_pieces = plane_pieces(out_grad, cot_sides, cot_corner)
     expert_range = jnp.arange(128, dtype=jnp.int32)
@@ -823,40 +844,30 @@
     stage_sides = run_group(groups[1])
     second_corner = after(second_corner, stage_sides[0])
     second_pieces[3], second_pieces[7] = second_corner, swap(second_corner, "c")
-    own_near, own_far = stage_own[7:]
+    own_near, own_far = stage_own[6:]
     own_far = swap(own_far, "c")
-    x_near, x_far, y_near, y_far = stage_sides[7:]
+    both = jnp.concatenate(
+        lax.optimization_barrier((attended, first_in, second_corner))[:2], axis=0
+    )
+    both_sides = plane_sides(both)
+    x_near, x_far, y_near, y_far = stage_sides[6:]
     back_x, back_y = over_core(x_near, x_far), over_core(y_near, y_far)
     first_x, first_y = early_sums(back_x, back_y)
     stage_corner = run_group(groups[2])
-    corner = over_core(*stage_corner[7:])
+    corner = over_core(*stage_corner[6:])
     passed = corner_first(corner)
     stages = (stage_own, stage_sides, stage_corner)
-
-    def expert_grad(left, right, *before):
-        lefts = [stage[left] for stage in stages]
-        rights = [stage[right] for stage in stages]
-        lefts[0] = after(lefts[0], *before)
-        return row_sum(at, lefts, rights)
-
-    down_part = expert_grad(1, 2, corner)
+    rows_in, rows_cot, gated, gate_back, up_back = ([stage[n] for stage in stages] for n in range(5))
+    gates = stage_own[5]
+    (down_part,) = row_sums(at, [after(rows_cot[0], corner)] + rows_cot[1:], gated)
     down_sum = scatter_sum(down_part, "z")
-    gate_part = expert_grad(0, 3, down_part)
+    passed = lax.optimization_barrier((*passed, down_part))[:2]
+    last_y, last_x, sent = corner_last(back_x, back_y, passed)
+    gate_part, up_part = row_sums(
+        at, [after(rows_in[0], sent)] + rows_in[1:], gate_back, up_back
+    )
     gate_sum = scatter_sum(gate_part, "z")
-    last_y, last_x = corner_last(back_x, back_y, passed)
-    up_part = expert_grad(0, 4, gate_part)
-    gates = stage_own[6]
-    signal = [None] * 8
-    for pieces, stage in zip(groups, stages):
-        for n, piece in enumerate(pieces):
-            signal[piece] = stage[5][2 * n : 2 * n + 2]
-    signal = jnp.stack(signal).reshape(2, 2, 2, length)
-    for dim, axis in enumerate(("c", "y", "x")):
-        signal = jnp.where(lax.axis_index(axis) == 1, jnp.flip(signal, dim), signal)
-    signal = exchange(jnp.swapaxes(signal, 0, 1).reshape(plane, length), PLANE)
-    signal = jnp.transpose(signal.reshape(2, 2, owners, length), (3, 2, 0, 1))
-    signal = signal.reshape(length, experts_all)
-    signal = jnp.pad(signal, ((0, 0), (0, 128 - experts_all)))
+    own_near = after(own_near, gate_part)
 
     resid_grad, branch_grad, attended_grad, router_acc, gain_two_grad = run_kernel(
         branch_back_kernel,
@@ -873,7 +884,6 @@
             gain_two,
             second_in,
             gates,
-            signal,
             router_w,
             out_grad,
             output_w,
@@ -900,12 +910,12 @@
         first_back_kernel,
         6,
         at,
-        (qkv_back, qkv_w, tokens, gain_one, resid_grad),
+        (qkv_back, qkv_w, tokens, gain_one, after(resid_grad, branch_cols)),
         [((length, model_width), bf16), ((1, model_width), f32)],
     )
 
-    both = jnp.concatenate(lax.optimization_barrier((attended, first_in, qkv_back))[:2], axis=0)
-    both_pieces = plane_pieces(both)
+    both_corner = plane_corner(both_sides, (qkv_cols_back,))
+    both_pieces = plane_pieces(both, both_sides, both_corner)
     narrow_part = jnp.concatenate(
         [router_acc[:, :experts_all], gain_one_grad.T, gain_two_grad.T], axis=1
     )
@@ -968,13 +978,13 @@
         functools.partial(mixture_kernel, capacity, groups),
         10,
         at,
-        (slots, down_w, after(stage_own[2], both_pieces[3]), stage_sides[2], stage_corner[2]),
+        (slots, down_w, after(gated[0], both_corner), *gated[1:]),
         [((length, model_width), bf16)] * plane,
         48,
     )
     mixed = [over_core(near, far) for near, far in zip(shares[:4], shares[4:])]
     early = early_sums(mixed[1], mixed[2])
-    last = corner_last(mixed[1], mixed[2], corner_first(mixed[3]))
+    last = corner_last(mixed[1], mixed[2], corner_first(mixed[3]))[:2]
     mixture = jnp.concatenate(
         [left.astype(f32) + right.astype(f32) for left, right in zip(early, last)], axis=0
     )

time: 591 us -> 614 us (1.039)
  waiting for transfers between devices: 226 us -> 277 us
  local copies, waits for them, and re-layouts: 97.7 us -> 85.8 us
  blocking collectives: 8.08 us -> 0 us
    reduce_scatter x4, waiting for transfers between devices: 65.3 us -> 91 us  [scatter_sum(): return lax.psum_scatter(block, axes, scatter_dimension=0, tiled=True)]
    ppermute x65, waiting for transfers between devices: 106 us -> 131 us  [swap(): return lax.ppermute(block, axis, [(0, 1), (1, 0)])]
    pallas_call x12 -> x9, Pallas kernels: 107 us -> 84.1 us  [run_kernel(): pl.pallas_call(kernel, out_shape=[jax.ShapeDtypeStruct(shape, dtype) for...]
    pallas_call x0 -> x2, Pallas kernels: none -> 18.6 us  [row_sums(): pl.pallas_call(functools.partial(row_sum_kernel, counts), out_shape=[jax....]
    all_to_all x1 -> x0, blocking collectives: 8.08 us -> none  [exchange(): return lax.all_to_all(block, axes, split_axis=0, concat_axis=0, tiled=True)]
    unnamed x181 -> x172, local copies, waits for them, and re-layouts: 44.7 us -> 45 us
  transfers between devices with their start and end apart: 82 -> 82, of which waited for: 29 -> 34; matrix products, arithmetic and copies ran while one was open for 16% -> 13% of each run, Pallas kernels for 16% -> 17%
where the time goes in v1:
time: 614 us; the launch traced here: 603 us
  waiting for transfers between devices  277 us (45%)
  Pallas kernels  111 us (18%)
  local copies, waits for them, and re-layouts  85.8 us (14%)
  starting transfers between devices  82.8 us (13%)
  other arithmetic  31 us (5%)
  between operations  15.9 us (3%)
    ppermute x65, waiting for transfers between devices, swap(): return lax.ppermute(block, axis, [(0, 1), (1, 0)])  131 us
    reduce_scatter x4, waiting for transfers between devices, scatter_sum(): return lax.psum_scatter(block, axes, scatter_dimension=0, tiled=True)  91 us
    pallas_call x9, Pallas kernels, run_kernel(): pl.pallas_call(kernel, out_shape=[jax.ShapeDtypeStruct(shape, dtype) for...  84.1 us
    unnamed x172, local copies, waits for them, and re-layouts  45 us
    ppermute x65, starting transfers between devices, swap(): return lax.ppermute(block, axis, [(0, 1), (1, 0)])  45 us
    all_to_all x7, waiting for transfers between devices, exchange(): return lax.all_to_all(block, axes, split_axis=0, concat_axis=0, tiled=True)  38.7 us
    all_to_all x7, starting transfers between devices, exchange(): return lax.all_to_all(block, axes, split_axis=0, concat_axis=0, tiled=True)  27.3 us
    pallas_call x2, Pallas kernels, row_sums(): pl.pallas_call(functools.partial(row_sum_kernel, counts), out_shape=[jax....  18.6 us
  transfers between devices with their start and end apart: 82, of which 34 were waited for; matrix products, arithmetic and copies ran while one was open for 13% of the time, Pallas kernels for 17%

profile of v1, /device:TPU:0, one launch (start us, length us, event | category | flops | bytes accessed | tf_op | source)
XLA Modules:
  0.0 603.5 jit_solution(5625893289370585513)
XLA Ops:
  8.0 5.1 collective-permute-start
  17.3 2.9 collective-permute-start.7
  35.0 15.1 %collective-permute-done.6 = bf16[96,1792]{1,0:T(8,128)(2,1)S(1)} collective-permute-done((bf16[96,1792]{1,0:T(8,128)(2,1)S(1)}, bf16[96,1792]{1,0:T(8,128)(2,1)S(1)}, u32[]{:S(2)}, u32[]{:S(2)}) %collective-permute-start.6) | collective-permute-done | bytes 344096 | tf_op jit(solution)/shard_map/ppermute | solution.py:317
  56.7 14.9 %collective-permute-done.14.refs_2_ = bf16[4,96,1024]{2,1,0:T(8,128)(2,1)S(1)} collective-permute-done((bf16[4,96,1024]{2,1,0:T(8,128)(2,1)S(1)}, bf16[4,96,1024]{2,1,0:T(8,128)(2,1)S(1)}, u32[]{:S(2)}, u32[]{:S(2)}) %collective-permute-start.14) | collective-permute-done | bytes 786464 | tf_op jit(solution)/shard_map/ppermute | solution.py:311
  75.4 6.5 %collective-permute-done.15 = bf16[2,96,1024]{2,1,0:T(8,128)(2,1)S(1)} collective-permute-done((bf16[2,96,1024]{2,1,0:T(8,128)(2,1)S(1)}, bf16[2,96,1024]{2,1,0:T(8,128)(2,1)S(1)}, u32[]{:S(2)}, u32[]{:S(2)}) %collective-permute-start.15) | collective-permute-done | bytes 393248 | tf_op jit(solution)/shard_map/ppermute | solution.py:311
  88.2 8.4 %shard_map.229 = (bf16[256,1536]{1,0:T(8,128)(2,1)S(1)}, bf16[256,1536]{1,0:T(8,128)(2,1)S(1)}, bf16[256,256]{1,0:T(8,128)(2,1)S(1)}, bf16[256,256]{1,0:T(8,128)...) custom-call(s32[7]{0:T(128)S(1)} %stack.76.at, ...), custom_call_target="tpu_custom_call" | custom-call | flops 11000000512 | bytes 11000000 | tf_op jit(solution)/shard_map/pallas_call | solution.py:398
  96.6 6.1 %collective-permute-done.21.refs_1_ = bf16[4,96,768]{2,1,0:T(8,128)(2,1)} collective-permute-done((bf16[4,96,768]{2,1,0:T(8,128)(2,1)}, bf16[4,96,768]{2,1,0:T(8,128)(2,1)}, u32[]{:S(2)}, u32[]{:S(2)}) %collective-permute-start.21) | collective-permute-done | bytes 589856 | tf_op jit(solution)/shard_map/ppermute | solution.py:311
  107.1 4.8 dynamic-slice_bitcast_fusion
  114.6 3.4 dynamic-slice_bitcast_fusion.2.down_w
  123.2 4.7 shard_map.230
  130.6 2.6 fusion
  141.3 12.8 %shard_map.231 = (bf16[384,1536]{1,0:T(8,128)(2,1)}, bf16[384,1536]{1,0:T(8,128)(2,1)}, bf16[384,768]{1,0:T(8,128)(2,1)}, bf16[384,768]{1,0:T(8,128)(2,1)}, bf16...) custom-call(s32[7]{0:T(128)} %copy-done.12, ...), custom_call_target="tpu_custom_call" | custom-call | flops 12000000000 | bytes 12000000 | tf_op jit(solution)/shard_map/pallas_call | solution.py:398
  154.1 11.3 %collective-permute-done.31.refs_0_ = bf16[256,1536]{1,0:T(8,128)(2,1)} collective-permute-done((bf16[256,1536]{1,0:T(8,128)(2,1)}, bf16[256,1536]{1,0:T(8,128)(2,1)}, u32[]{:S(2)}, u32[]{:S(2)}) %collective-permute-start.31) | collective-permute-done | bytes 786464 | tf_op jit(solution)/shard_map/ppermute | solution.py:311
  170.2 7.7 %collective-permute-done.33 = bf16[128,1536]{1,0:T(8,128)(2,1)S(1)} collective-permute-done((bf16[128,1536]{1,0:T(8,128)(2,1)S(1)}, bf16[128,1536]{1,0:T(8,128)(2,1)S(1)}, u32[]{:S(2)}, u32[]{:S(2)}) %collective-permute-start.33) | collective-permute-done | bytes 393248 | tf_op jit(solution)/shard_map/ppermute | solution.py:311
  180.1 6.9 %collective-permute-done.34 = bf16[128,1536]{1,0:T(8,128)(2,1)S(1)} collective-permute-done((bf16[128,1536]{1,0:T(8,128)(2,1)S(1)}, bf16[128,1536]{1,0:T(8,128)(2,1)S(1)}, u32[]{:S(2)}, u32[]{:S(2)}) %collective-permute-start.34) | collective-permute-done | bytes 393248 | tf_op jit(solution)/shard_map/ppermute | solution.py:311
  190.7 21.3 %shard_map.232 = (bf16[768,1536]{1,0:T(8,128)(2,1)}, bf16[768,1536]{1,0:T(8,128)(2,1)}, bf16[768,768]{1,0:T(8,128)(2,1)}, bf16[768,768]{1,0:T(8,128)(2,1)}, bf16...) custom-call(s32[7]{0:T(128)} %copy-done.12, ...), custom_call_target="tpu_custom_call" | custom-call | flops 24000000000 | bytes 24000000 | tf_op jit(solution)/shard_map/pallas_call | solution.py:398
  216.0 13.1 %shard_map.233 = (bf16[384,1536]{1,0:T(8,128)(2,1)}, bf16[384,1536]{1,0:T(8,128)(2,1)}, bf16[384,768]{1,0:T(8,128)(2,1)}, bf16[384,768]{1,0:T(8,128)(2,1)}, bf16...) custom-call(s32[7]{0:T(128)} %copy-done.12, ...), custom_call_target="tpu_custom_call" | custom-call | flops 12000000000 | bytes 12000000 | tf_op jit(solution)/shard_map/pallas_call | solution.py:398
  236.9 7.0 %shard_map.234 = bf16[1536,768]{1,0:T(8,128)(2,1)} custom-call(s32[7]{0:T(128)S(1)} %copy-done.13, bf16[384,1536]{1,0:T(8,128)(2,1)S(1)} %copy-done.30, bf16[768,1536]{1,0:T(8,128)(2,1)S(1)} %copy-done.27, bf16[384,1536]{1,0:T(8,128)(2,1)S(1)} %copy-done.31, bf16[384,768]{1,0:T(8,128)(2,1)S(1)} %copy-done.32, bf16[768,768]{1,0:T(8,128)(2,1)S(1)} %copy-done.29, ...), custom_call_target="tpu_custom_call" | custom-call | flops 6000000000 | bytes 6000000 | tf_op jit(solution)/shard_map/pallas_call | solution.py:599
  244.0 9.1 %collective-permute-done.47 = bf16[128,1664]{1,0:T(8,128)(2,1)S(1)} collective-permute-done((bf16[128,1664]{1,0:T(8,128)(2,1)}, bf16[128,1664]{1,0:T(8,128)(2,1)S(1)}, u32[]{:S(2)}, u32[]{:S(2)}) %collective-permute-start.47) | collective-permute-done | bytes 426016 | tf_op jit(solution)/shard_map/ppermute | solution.py:311
  269.0 11.6 %shard_map.235 = (bf16[1536,768]{1,0:T(8,128)(2,1)}, bf16[1536,768]{1,0:T(8,128)(2,1)}) custom-call(s32[7]{0:T(128)S(1)} %copy-done.13, bf16[384,1536]{1,0:T(8,128)(2,1)S(1)} %copy-done.40, bf16[768,1536]{1,0:T(8,128)(2,1)S(1)} %copy-done.36, bf16[384,1536]{1,0:T(8,128)(2,1)S(1)} %copy-done.41, bf16[384,768]{1,0:T(8,128)(2,1)S(1)} %copy-done.46, ...), custom_call_target="tpu_custom_call" | custom-call | flops 12000000000 | bytes 12000000 | tf_op jit(solution)/shard_map/pallas_call | solution.py:599
  285.0 6.4 %shard_map.236 = (f32[256,1536]{1,0:T(8,128)S(1)}, bf16[256,1536]{1,0:T(8,128)(2,1)S(1)}, bf16[256,1536]{1,0:T(8,128)(2,1)S(1)}, f32[1536,128]{1,0:T(8,128)S(1)}, f32[1,1536]{1,0:T(1,128)S(1)}) custom-call(s32[7]{0:T(128)S(1)} %copy-done.13, bf16[256,1664]{1,0:T(8,128)(2,1)S(1)} %copy-done.28, bf16[256,1664]{1,0:T(8,128)(2,1)} %collective-permute-done.49.far, ...), custom_call_target="tpu_custom_call" | custom-call | flops 6000000000 | bytes 6000000 | tf_op jit(solution)/shard_map/pallas_call | solution.py:398
  293.5 5.2 shard_map.237.back
  299.7 3.6 all-to-all-start
  303.2 15.9 %collective-permute-done.39.refs_2_ = bf16[512,1536]{1,0:T(8,128)(2,1)} collective-permute-done((bf16[512,1536]{1,0:T(8,128)(2,1)}, bf16[512,1536]{1,0:T(8,128)(2,1)}, u32[]{:S(2)}, u32[]{:S(2)}) %collective-permute-start.39) | collective-permute-done | bytes 1572896 | tf_op jit(solution)/shard_map/ppermute | solution.py:311
  323.3 3.0 all-to-all-done.qkv_cols
  330.5 16.6 %collective-permute-done.55 = bf16[256,1536]{1,0:T(8,128)(2,1)S(1)} collective-permute-done((bf16[256,1536]{1,0:T(8,128)(2,1)}, bf16[256,1536]{1,0:T(8,128)(2,1)S(1)}, u32[]{:S(2)}, u32[]{:S(2)}) %collective-permute-start.55) | collective-permute-done | bytes 786464 | tf_op jit(solution)/shard_map/ppermute | solution.py:311
  351.5 4.3 all-to-all-start.1
  356.1 11.9 %all-to-all-done.1 = bf16[8,256,192]{1,2,0:T(8,128)(2,1)} async-done(((bf16[8,256,192]{1,2,0:T(8,128)(2,1)}), bf16[8,256,192]{1,2,0:T(8,128)(2,1)}, u32[]{:S(2)}, u32[]{:S(2)}) %all-to-all-start.1) | async-done | bytes 786464 | tf_op jit(solution)/shard_map/all_to_all | solution.py:61
  369.1 2.8 copy-done.23
  373.3 3.7 shard_map.239
  379.2 3.4 all-to-all-start.2
  384.0 3.3 all-to-all-done.2
  388.7 8.4 %shard_map.240 = bf16[4,400,448]{2,1,0:T(8,128)(2,1)} custom-call(s32[7]{0:T(128)S(1)} %copy-done.13, bf16[4,16,448]{2,1,0:T(8,128)(2,1)S(1)} %convert_element_type.223.narrow, bf16[8,256,192]{2,1,0:T(8,128)(2,1)S(1)} %copy.102.branch_cols, bf16[8,256,256]{2,1,0:T(8,128)(2,1)S(1)} %copy-done.1, ...), custom_call_target="tpu_custom_call" | custom-call | flops 7000000000 | bytes 7000000 | tf_op jit(solution)/shard_map/pallas_call | solution.py:938
  400.9 8.4 %shard_map.238 = (bf16[256,1536]{1,0:T(8,128)(2,1)S(1)}, bf16[256,1536]{1,0:T(8,128)(2,1)S(1)}, bf16[256,1536]{1,0:T(8,128)(2,1)S(1)}, bf16[256,1536]{1,0:T(8,12...) custom-call(s32[7]{0:T(128)S(1)} %copy-done.13, ...), custom_call_target="tpu_custom_call" | custom-call | flops 10000000000 | bytes 10000000 | tf_op jit(solution)/shard_map/pallas_call | solution.py:398
  413.0 20.3 %reduce-scatter.5.cloned.1.call-done = bf16[400,448]{1,0:T(8,128)(2,1)} async-done(((bf16[1600,448]{1,0:T(8,128)(2,1)}), bf16[400,448]{1,0:T(8,128)(2,1)}) %reduce-scatter.5.cloned.1.call-update) | async-done | bytes 358416 | tf_op jit(solution)/shard_map/reduce_scatter | solution.py:65
  435.7 4.2 all-to-all-start.3
  440.9 12.6 %all-to-all-done.3 = bf16[8,112,448]{2,1,0:T(8,128)(2,1)} async-done(((bf16[8,112,448]{2,1,0:T(8,128)(2,1)}), bf16[8,112,448]{2,1,0:T(8,128)(2,1)}, u32[]{:S(2)}, u32[]{:S(2)}) %all-to-all-start.3) | async-done | bytes 802848 | tf_op jit(solution)/shard_map/all_to_all | solution.py:61
  462.1 5.1 collective-permute-done.61
  467.9 12.7 %collective-permute-done.64 = bf16[128,1536]{1,0:T(8,128)(2,1)S(1)} collective-permute-done((bf16[128,1536]{1,0:T(8,128)(2,1)S(1)}, bf16[128,1536]{1,0:T(8,128)(2,1)S(1)}, u32[]{:S(2)}, u32[]{:S(2)}) %collective-permute-start.64) | collective-permute-done | bytes 393248 | tf_op jit(solution)/shard_map/ppermute | solution.py:311
  482.4 4.7 collective-permute-done.62
  487.2 4.2 all-to-all-start.6
  493.6 39.2 %reduce-scatter.7.cloned.1.call-done = bf16[384,768]{1,0:T(8,128)(2,1)} async-done(((bf16[1536,768]{1,0:T(8,128)(2,1)}), bf16[384,768]{1,0:T(8,128)(2,1)}) %reduce-scatter.7.cloned.1.call-update) | async-done | bytes 589840 | tf_op jit(solution)/shard_map/reduce_scatter | solution.py:65
  532.8 4.2 all-to-all-start.4
  537.0 2.7 fusion.2
  542.0 4.6 all-to-all-done.4
  551.2 31.5 %reduce-scatter.9.cloned.1.call-done = bf16[384,768]{1,0:T(8,128)(2,1)} async-done(((bf16[1536,768]{1,0:T(8,128)(2,1)}), bf16[384,768]{1,0:T(8,128)(2,1)}) %reduce-scatter.9.cloned.1.call-update) | async-done | bytes 589840 | tf_op jit(solution)/shard_map/reduce_scatter | solution.py:65
  582.6 3.5 all-to-all-start.5
  592.3 3.3 all-to-all-done.5
  (421 shorter events, 162.9 us)
Async XLA Ops:
  21.7 28.4 %collective-permute-start.6 = (bf16[96,1792]{1,0:T(8,128)(2,1)S(1)}, bf16[96,1792]{1,0:T(8,128)(2,1)S(1)}, u32[]{:S(2)}, u32[]{:S(2)}) collective-permute-start(bf16[96,1792]{1,0:T(8,128)(2,1)S(1)} %pad_maximum_fusion.3), channel_id=1, source_target_pairs={{0,16},{8,24},{16,0},{24,8},{1,17},{9,25},{17,1},{25,9},{2,18},{10... | collective-permute-start | bytes 1032200 | tf_op jit(solution)/shard_map/ppermute | solution.py:317
  22.9 27.2 %collective-permute-start.5 = (bf16[96,1792]{1,0:T(8,128)(2,1)S(1)}, bf16[96,1792]{1,0:T(8,128)(2,1)S(1)}, u32[]{:S(2)}, u32[]{:S(2)}) collective-permute-start(bf16[96,1792]{1,0:T(8,128)(2,1)S(1)} %pad_maximum_fusion.3), channel_id=1, source_target_pairs={{0,8},{8,16},{16,24},{24,0},{1,9},{9,17},{17,25},{25,1},{2,10},{10... | collective-permute-start | bytes 1032200 | tf_op jit(solution)/shard_map/ppermute | solution.py:317
  22.9 116.9 %collective-permute-start.30 = (bf16[256,1536]{1,0:T(8,128)(2,1)}, bf16[256,1536]{1,0:T(8,128)(2,1)}, u32[]{:S(2)}, u32[]{:S(2)}) collective-permute-start(bf16[256,1536]{1,0:T(8,128)(2,1)} %cot.1), channel_id=1, source_target_pairs={{0,2},{2,0},{1,3},{3,1},{4,6},{6,4},{5,7},{7,5},{8,10},{10,8},{9,1... | collective-permute-start | bytes 2359304 | tf_op jit(solution)/shard_map/ppermute | solution.py:311
  33.0 19.8 %collective-permute-start.11 = (bf16[256,1536]{1,0:T(8,128)(2,1)}, bf16[256,1536]{1,0:T(8,128)(2,1)S(1)}, u32[]{:S(2)}, u32[]{:S(2)}) collective-permute-start(bf16[256,1536]{1,0:T(8,128)(2,1)} %cot.1), channel_id=1, source_target_pairs={{0,1},{1,0},{2,3},{3,2},{4,5},{5,4},{6,7},{7,6},{8,9},{9,8},{10,11... | collective-permute-start | bytes 2359304 | tf_op jit(solution)/shard_map/ppermute | solution.py:311
  33.5 19.5 %collective-permute-start.12 = (bf16[256,1536]{1,0:T(8,128)(2,1)}, bf16[256,1536]{1,0:T(8,128)(2,1)S(1)}, u32[]{:S(2)}, u32[]{:S(2)}) collective-permute-start(bf16[256,1536]{1,0:T(8,128)(2,1)} %cot.1), channel_id=1, source_target_pairs={{0,4},{4,0},{1,5},{5,1},{2,6},{6,2},{3,7},{7,3},{8,12},{12,8},{9,1... | collective-permute-start | bytes 2359304 | tf_op jit(solution)/shard_map/ppermute | solution.py:311
  53.0 18.6 %collective-permute-start.14 = (bf16[4,96,1024]{2,1,0:T(8,128)(2,1)S(1)}, bf16[4,96,1024]{2,1,0:T(8,128)(2,1)S(1)}, u32[]{:S(2)}, u32[]{:S(2)}) collective-permute-start(bf16[4,96,1024]{2,1,0:T(8,128)(2,1)S(1)} %pad_maximum_fusion.refs_0_), channel_id=1, source_target_pairs={{0,4},{4,0},{1,5},{5,1},{2,6},{6,2},{3,7},{7,3},{8,12},{12,8},{9,1... | collective-permute-start | bytes 2359304 | tf_op jit(solution)/shard_map/ppermute | solution.py:311
  54.6 18.3 %collective-permute-start.13 = (bf16[4,96,1024]{2,1,0:T(8,128)(2,1)S(1)}, bf16[4,96,1024]{2,1,0:T(8,128)(2,1)S(1)}, u32[]{:S(2)}, u32[]{:S(2)}) collective-permute-start(bf16[4,96,1024]{2,1,0:T(8,128)(2,1)S(1)} %pad_maximum_fusion.refs_0_), channel_id=1, source_target_pairs={{0,1},{1,0},{2,3},{3,2},{4,5},{5,4},{6,7},{7,6},{8,9},{9,8},{10,11... | collective-permute-start | bytes 2359304 | tf_op jit(solution)/shard_map/ppermute | solution.py:311
  137.1 32.6 %collective-permute-start.43 = (bf16[128,1536]{1,0:T(8,128)(2,1)S(1)}, bf16[128,1536]{1,0:T(8,128)(2,1)S(1)}, u32[]{:S(2)}, u32[]{:S(2)}) collective-permute-start(bf16[128,1536]{1,0:T(8,128)(2,1)S(1)} %slice.199), channel_id=1, source_target_pairs={{0,1},{1,0},{2,3},{3,2},{4,5},{5,4},{6,7},{7,6},{8,9},{9,8},{10,11... | collective-permute-start | bytes 1179656 | tf_op jit(solution)/shard_map/ppermute | solution.py:311
  137.9 31.8 %collective-permute-start.44 = (bf16[128,1536]{1,0:T(8,128)(2,1)S(1)}, bf16[128,1536]{1,0:T(8,128)(2,1)S(1)}, u32[]{:S(2)}, u32[]{:S(2)}) collective-permute-start(bf16[128,1536]{1,0:T(8,128)(2,1)S(1)} %slice.200), channel_id=1, source_target_pairs={{0,4},{4,0},{1,5},{5,1},{2,6},{6,2},{3,7},{7,3},{8,12},{12,8},{9,1... | collective-permute-start | bytes 1179656 | tf_op jit(solution)/shard_map/ppermute | solution.py:311
  138.6 26.8 %collective-permute-start.31 = (bf16[256,1536]{1,0:T(8,128)(2,1)}, bf16[256,1536]{1,0:T(8,128)(2,1)}, u32[]{:S(2)}, u32[]{:S(2)}) collective-permute-start(bf16[256,1536]{1,0:T(8,128)(2,1)} %get-tuple-element.102.refs_0_.second), channel_id=1, source_target_pairs={{0,1},{1,0},{2,3},{3,2},{4,5},{5,4},{6,7},{7,6},{8,9},{9,8},{10,11... | collective-permute-start | bytes 2359304 | tf_op jit(solution)/shard_map/ppermute | solution.py:311
  139.9 25.9 %collective-permute-start.32 = (bf16[256,1536]{1,0:T(8,128)(2,1)}, bf16[256,1536]{1,0:T(8,128)(2,1)}, u32[]{:S(2)}, u32[]{:S(2)}) collective-permute-start(bf16[256,1536]{1,0:T(8,128)(2,1)} %get-tuple-element.102.refs_0_.second), channel_id=1, source_target_pairs={{0,4},{4,0},{1,5},{5,1},{2,6},{6,2},{3,7},{7,3},{8,12},{12,8},{9,1... | collective-permute-start | bytes 2359304 | tf_op jit(solution)/shard_map/ppermute | solution.py:311
  169.2 17.9 %collective-permute-start.37 = (bf16[256,1536]{1,0:T(8,128)(2,1)S(1)}, bf16[256,1536]{1,0:T(8,128)(2,1)S(1)}, u32[]{:S(2)}, u32[]{:S(2)}) collective-permute-start(bf16[256,1536]{1,0:T(8,128)(2,1)S(1)} %copy-done.65), channel_id=1, source_target_pairs={{0,2},{2,0},{1,3},{3,1},{4,6},{6,4},{5,7},{7,5},{8,10},{10,8},{9,1... | collective-permute-start | bytes 2359304 | tf_op jit(solution)/shard_map/ppermute | solution.py:311
  169.2 17.9 %collective-permute-start.38 = (bf16[256,1536]{1,0:T(8,128)(2,1)S(1)}, bf16[256,1536]{1,0:T(8,128)(2,1)S(1)}, u32[]{:S(2)}, u32[]{:S(2)}) collective-permute-start(bf16[256,1536]{1,0:T(8,128)(2,1)S(1)} %copy-done.67), channel_id=1, source_target_pairs={{0,2},{2,0},{1,3},{3,1},{4,6},{6,4},{5,7},{7,5},{8,10},{10,8},{9,1... | collective-permute-start | bytes 2359304 | tf_op jit(solution)/shard_map/ppermute | solution.py:311
  169.7 18.3 %collective-permute-start.35 = (bf16[256,1536]{1,0:T(8,128)(2,1)}, bf16[256,1536]{1,0:T(8,128)(2,1)S(1)}, u32[]{:S(2)}, u32[]{:S(2)}) collective-permute-start(bf16[256,1536]{1,0:T(8,128)(2,1)} %collective-permute-done.31.refs_0_), channel_id=1, source_target_pairs={{0,2},{2,0},{1,3},{3,1},{4,6},{6,4},{5,7},{7,5},{8,10},{10,8},{9,1... | collective-permute-start | bytes 2359304 | tf_op jit(solution)/shard_map/ppermute | solution.py:311
  169.8 20.0 %collective-permute-start.36 = (bf16[256,1536]{1,0:T(8,128)(2,1)}, bf16[256,1536]{1,0:T(8,128)(2,1)S(1)}, u32[]{:S(2)}, u32[]{:S(2)}) collective-permute-start(bf16[256,1536]{1,0:T(8,128)(2,1)} %collective-permute-done.32.refs_2_), channel_id=1, source_target_pairs={{0,2},{2,0},{1,3},{3,1},{4,6},{6,4},{5,7},{7,5},{8,10},{10,8},{9,1... | collective-permute-start | bytes 2359304 | tf_op jit(solution)/shard_map/ppermute | solution.py:311
  187.0 28.1 %collective-permute-start.45 = (bf16[256,1536]{1,0:T(8,128)(2,1)}, bf16[256,1536]{1,0:T(8,128)(2,1)}, u32[]{:S(2)}, u32[]{:S(2)}) collective-permute-start(bf16[256,1536]{1,0:T(8,128)(2,1)} %constant_dynamic-update-slice_fusion.18.refs_2_), channel_id=1, source_target_pairs={{0,2},{2,0},{1,3},{3,1},{4,6},{6,4},{5,7},{7,5},{8,10},{10,8},{9,1... | collective-permute-start | bytes 2359304 | tf_op jit(solution)/shard_map/ppermute | solution.py:311
  212.6 68.0 %collective-permute-start.49 = (bf16[256,1664]{1,0:T(8,128)(2,1)}, bf16[256,1664]{1,0:T(8,128)(2,1)}, u32[]{:S(2)}, u32[]{:S(2)}) collective-permute-start(bf16[256,1664]{1,0:T(8,128)(2,1)} %get-tuple-element.138), channel_id=1, source_target_pairs={{0,2},{2,0},{1,3},{3,1},{4,6},{6,4},{5,7},{7,5},{8,10},{10,8},{9,1... | collective-permute-start | bytes 2555912 | tf_op jit(solution)/shard_map/ppermute | solution.py:311
  212.7 16.8 %collective-permute-start.51 = (bf16[256,1664]{1,0:T(8,128)(2,1)}, bf16[256,1664]{1,0:T(8,128)(2,1)S(1)}, u32[]{:S(2)}, u32[]{:S(2)}) collective-permute-start(bf16[256,1664]{1,0:T(8,128)(2,1)} %get-tuple-element.140), channel_id=1, source_target_pairs={{0,2},{2,0},{1,3},{3,1},{4,6},{6,4},{5,7},{7,5},{8,10},{10,8},{9,1... | collective-permute-start | bytes 2555912 | tf_op jit(solution)/shard_map/ppermute | solution.py:311
  213.1 18.0 %collective-permute-start.41 = (bf16[256,1664]{1,0:T(8,128)(2,1)}, bf16[256,1664]{1,0:T(8,128)(2,1)S(1)}, u32[]{:S(2)}, u32[]{:S(2)}) collective-permute-start(bf16[256,1664]{1,0:T(8,128)(2,1)} %get-tuple-element.116), channel_id=1, source_target_pairs={{0,2},{2,0},{1,3},{3,1},{4,6},{6,4},{5,7},{7,5},{8,10},{10,8},{9,1... | collective-permute-start | bytes 2555912 | tf_op jit(solution)/shard_map/ppermute | solution.py:311
  230.5 50.7 %collective-permute-start.52 = (bf16[128,1664]{1,0:T(8,128)(2,1)}, bf16[128,1664]{1,0:T(8,128)(2,1)S(1)}, u32[]{:S(2)}, u32[]{:S(2)}) collective-permute-start(bf16[128,1664]{1,0:T(8,128)(2,1)} %slice.204), channel_id=1, source_target_pairs={{0,4},{4,0},{1,5},{5,1},{2,6},{6,2},{3,7},{7,3},{8,12},{12,8},{9,1... | collective-permute-start | bytes 1277960 | tf_op jit(solution)/shard_map/ppermute | solution.py:311
  232.2 50.5 %collective-permute-start.50 = (bf16[128,1664]{1,0:T(8,128)(2,1)}, bf16[128,1664]{1,0:T(8,128)(2,1)}, u32[]{:S(2)}, u32[]{:S(2)}) collective-permute-start(bf16[128,1664]{1,0:T(8,128)(2,1)} %slice.203), channel_id=1, source_target_pairs={{0,1},{1,0},{2,3},{3,2},{4,5},{5,4},{6,7},{7,6},{8,9},{9,8},{10,11... | collective-permute-start | bytes 1277960 | tf_op jit(solution)/shard_map/ppermute | solution.py:311
  234.7 18.3 %collective-permute-start.47 = (bf16[128,1664]{1,0:T(8,128)(2,1)}, bf16[128,1664]{1,0:T(8,128)(2,1)S(1)}, u32[]{:S(2)}, u32[]{:S(2)}) collective-permute-start(bf16[128,1664]{1,0:T(8,128)(2,1)} %get-tuple-element.171), channel_id=1, source_target_pairs={{0,1},{1,0},{2,3},{3,2},{4,5},{5,4},{6,7},{7,6},{8,9},{9,8},{10,11... | collective-permute-start | bytes 1277960 | tf_op jit(solution)/shard_map/ppermute | solution.py:311
  235.4 17.6 %collective-permute-start.48 = (bf16[128,1664]{1,0:T(8,128)(2,1)}, bf16[128,1664]{1,0:T(8,128)(2,1)}, u32[]{:S(2)}, u32[]{:S(2)}) collective-permute-start(bf16[128,1664]{1,0:T(8,128)(2,1)} %get-tuple-element.170), channel_id=1, source_target_pairs={{0,4},{4,0},{1,5},{5,1},{2,6},{6,2},{3,7},{7,3},{8,12},{12,8},{9,1... | collective-permute-start | bytes 1277960 | tf_op jit(solution)/shard_map/ppermute | solution.py:311
  255.1 27.7 %collective-permute-start.54 = (bf16[128,1664]{1,0:T(8,128)(2,1)}, bf16[128,1664]{1,0:T(8,128)(2,1)}, u32[]{:S(2)}, u32[]{:S(2)}) collective-permute-start(bf16[128,1664]{1,0:T(8,128)(2,1)} %reduce-precision_convert_fusion.8), channel_id=1, source_target_pairs={{0,1},{1,0},{2,3},{3,2},{4,5},{5,4},{6,7},{7,6},{8,9},{9,8},{10,11... | collective-permute-start | bytes 1277960 | tf_op jit(solution)/shard_map/ppermute | solution.py:311
  258.2 24.5 %collective-permute-start.53 = (bf16[128,1664]{1,0:T(8,128)(2,1)}, bf16[128,1664]{1,0:T(8,128)(2,1)}, u32[]{:S(2)}, u32[]{:S(2)}) collective-permute-start(bf16[128,1664]{1,0:T(8,128)(2,1)} %reduce-precision_convert_fusion.7), channel_id=1, source_target_pairs={{0,4},{4,0},{1,5},{5,1},{2,6},{6,2},{3,7},{7,3},{8,12},{12,8},{9,1... | collective-permute-start | bytes 1277960 | tf_op jit(solution)/shard_map/ppermute | solution.py:311
  280.6 38.6 %collective-permute-start.39 = (bf16[512,1536]{1,0:T(8,128)(2,1)}, bf16[512,1536]{1,0:T(8,128)(2,1)}, u32[]{:S(2)}, u32[]{:S(2)}) collective-permute-start(bf16[512,1536]{1,0:T(8,128)(2,1)} %constant_dynamic-update-slice_fusion.16.refs_0_), channel_id=1, source_target_pairs={{0,4},{4,0},{1,5},{5,1},{2,6},{6,2},{3,7},{7,3},{8,12},{12,8},{9,1... | collective-permute-start | bytes 4718600 | tf_op jit(solution)/shard_map/ppermute | solution.py:311
  282.0 39.2 %collective-permute-start.40 = (bf16[512,1536]{1,0:T(8,128)(2,1)}, bf16[512,1536]{1,0:T(8,128)(2,1)}, u32[]{:S(2)}, u32[]{:S(2)}) collective-permute-start(bf16[512,1536]{1,0:T(8,128)(2,1)} %constant_dynamic-update-slice_fusion.16.refs_0_), channel_id=1, source_target_pairs={{0,1},{1,0},{2,3},{3,2},{4,5},{5,4},{6,7},{7,6},{8,9},{9,8},{10,11... | collective-permute-start | bytes 4718600 | tf_op jit(solution)/shard_map/ppermute | solution.py:311
  299.7 26.6 %all-to-all-start = ((bf16[8,256,256]{2,1,0:T(8,128)(2,1)}), bf16[8,256,256]{2,1,0:T(8,128)(2,1)S(1)}, u32[]{:S(2)}, u32[]{:S(2)}) async-start(bf16[8,256,256]{2,1,0:T(8,128)(2,1)} %copy-done.2), calls=%async_computation | async-start | bytes 2097152 | tf_op jit(solution)/shard_map/all_to_all | solution.py:61
  326.2 20.9 %collective-permute-start.55 = (bf16[256,1536]{1,0:T(8,128)(2,1)}, bf16[256,1536]{1,0:T(8,128)(2,1)S(1)}, u32[]{:S(2)}, u32[]{:S(2)}) collective-permute-start(bf16[256,1536]{1,0:T(8,128)(2,1)} %slice.196), channel_id=1, source_target_pairs={{0,1},{1,0},{2,3},{3,2},{4,5},{5,4},{6,7},{7,6},{8,9},{9,8},{10,11... | collective-permute-start | bytes 2359304 | tf_op jit(solution)/shard_map/ppermute | solution.py:311
  328.6 19.4 %collective-permute-start.56 = (bf16[256,1536]{1,0:T(8,128)(2,1)}, bf16[256,1536]{1,0:T(8,128)(2,1)S(1)}, u32[]{:S(2)}, u32[]{:S(2)}) collective-permute-start(bf16[256,1536]{1,0:T(8,128)(2,1)} %slice.197), channel_id=1, source_target_pairs={{0,4},{4,0},{1,5},{5,1},{2,6},{6,2},{3,7},{7,3},{8,12},{12,8},{9,1... | collective-permute-start | bytes 2359304 | tf_op jit(solution)/shard_map/ppermute | solution.py:311
  330.0 57.5 %collective-permute-start.67 = (bf16[512,1536]{1,0:T(8,128)(2,1)}, bf16[512,1536]{1,0:T(8,128)(2,1)}, u32[]{:S(2)}, u32[]{:S(2)}) collective-permute-start(bf16[512,1536]{1,0:T(8,128)(2,1)} %constant_dynamic-update-slice_fusion.16.refs_0_), channel_id=1, source_target_pairs={{0,2},{2,0},{1,3},{3,1},{4,6},{6,4},{5,7},{7,5},{8,10},{10,8},{9,1... | collective-permute-start | bytes 4718600 | tf_op jit(solution)/shard_map/ppermute | solution.py:311
  330.0 57.5 %collective-permute-start.68 = (bf16[512,1536]{1,0:T(8,128)(2,1)}, bf16[512,1536]{1,0:T(8,128)(2,1)}, u32[]{:S(2)}, u32[]{:S(2)}) collective-permute-start(bf16[512,1536]{1,0:T(8,128)(2,1)} %collective-permute-done.40.refs_1_), channel_id=1, source_target_pairs={{0,2},{2,0},{1,3},{3,1},{4,6},{6,4},{5,7},{7,5},{8,10},{10,8},{9,1... | collective-permute-start | bytes 4718600 | tf_op jit(solution)/shard_map/ppermute | solution.py:311
  330.5 57.0 %collective-permute-start.69 = (bf16[512,1536]{1,0:T(8,128)(2,1)}, bf16[512,1536]{1,0:T(8,128)(2,1)}, u32[]{:S(2)}, u32[]{:S(2)}) collective-permute-start(bf16[512,1536]{1,0:T(8,128)(2,1)} %collective-permute-done.39.refs_2_), channel_id=1, source_target_pairs={{0,2},{2,0},{1,3},{3,1},{4,6},{6,4},{5,7},{7,5},{8,10},{10,8},{9,1... | collective-permute-start | bytes 4718600 | tf_op jit(solution)/shard_map/ppermute | solution.py:311
  349.0 38.5 %collective-permute-start.70 = (bf16[512,1536]{1,0:T(8,128)(2,1)}, bf16[512,1536]{1,0:T(8,128)(2,1)}, u32[]{:S(2)}, u32[]{:S(2)}) collective-permute-start(bf16[512,1536]{1,0:T(8,128)(2,1)} %constant_dynamic-update-slice_fusion.20.refs_3_), channel_id=1, source_target_pairs={{0,2},{2,0},{1,3},{3,1},{4,6},{6,4},{5,7},{7,5},{8,10},{10,8},{9,1... | collective-permute-start | bytes 4718600 | tf_op jit(solution)/shard_map/ppermute | solution.py:311
  351.5 16.5 %all-to-all-start.1 = ((bf16[8,256,192]{1,2,0:T(8,128)(2,1)}), bf16[8,256,192]{1,2,0:T(8,128)(2,1)}, u32[]{:S(2)}, u32[]{:S(2)}) async-start(bf16[8,256,192]{1,2,0:T(8,128)(2,1)} %bitcast.102), calls=%async_computation.1 | async-start | bytes 1572864 | tf_op jit(solution)/shard_map/all_to_all | solution.py:61
  382.5 50.8 %reduce-scatter.5.cloned.1.call-start = ((), (), s32[]{:S(2)}) async-start(), calls=%async_computation.11 | async-start | bytes 2048000 | tf_op jit(solution)/shard_map/reduce_scatter | solution.py:65
  397.2 90.0 %reduce-scatter.11.cloned.1.call-start = ((), (), s32[]{:S(2)}) async-start(), calls=%async_computation.14 | async-start | bytes 2949120 | tf_op jit(solution)/shard_map/reduce_scatter | solution.py:65
  398.0 134.8 %reduce-scatter.7.cloned.1.call-start = ((), (), s32[]{:S(2)}) async-start(), calls=%async_computation.12 | async-start | bytes 2949120 | tf_op jit(solution)/shard_map/reduce_scatter | solution.py:65
  412.9 40.6 %collective-permute-start.60 = (bf16[256,1536]{1,0:T(8,128)(2,1)}, bf16[256,1536]{1,0:T(8,128)(2,1)}, u32[]{:S(2)}, u32[]{:S(2)}) collective-permute-start(bf16[256,1536]{1,0:T(8,128)(2,1)} %get-tuple-element.157), channel_id=1, source_target_pairs={{0,2},{2,0},{1,3},{3,1},{4,6},{6,4},{5,7},{7,5},{8,10},{10,8},{9,1... | collective-permute-start | bytes 2359304 | tf_op jit(solution)/shard_map/ppermute | solution.py:311
  435.7 17.8 %all-to-all-start.3 = ((bf16[8,112,448]{2,1,0:T(8,128)(2,1)}), bf16[8,112,448]{2,1,0:T(8,128)(2,1)}, u32[]{:S(2)}, u32[]{:S(2)}) async-start(bf16[8,112,448]{2,1,0:T(8,128)(2,1)} %maximum_maximum_fusion), calls=%async_computation.4 | async-start | bytes 1835008 | tf_op jit(solution)/shard_map/all_to_all | solution.py:61
  440.0 142.7 %reduce-scatter.9.cloned.1.call-start = ((), (), s32[]{:S(2)}) async-start(), calls=%async_computation.13 | async-start | bytes 2949120 | tf_op jit(solution)/shard_map/reduce_scatter | solution.py:65
  440.0 18.7 %collective-permute-start.59 = (bf16[256,1536]{1,0:T(8,128)(2,1)}, bf16[256,1536]{1,0:T(8,128)(2,1)}, u32[]{:S(2)}, u32[]{:S(2)}) collective-permute-start(bf16[256,1536]{1,0:T(8,128)(2,1)} %get-tuple-element.155), channel_id=1, source_target_pairs={{0,2},{2,0},{1,3},{3,1},{4,6},{6,4},{5,7},{7,5},{8,10},{10,8},{9,1... | collective-permute-start | bytes 2359304 | tf_op jit(solution)/shard_map/ppermute | solution.py:311
  440.6 96.4 %collective-permute-start.66 = (bf16[256,1536]{1,0:T(8,128)(2,1)}, bf16[256,1536]{1,0:T(8,128)(2,1)}, u32[]{:S(2)}, u32[]{:S(2)}) collective-permute-start(bf16[256,1536]{1,0:T(8,128)(2,1)} %copy-done.17), channel_id=1, source_target_pairs={{0,2},{2,0},{1,3},{3,1},{4,6},{6,4},{5,7},{7,5},{8,10},{10,8},{9,1... | collective-permute-start | bytes 2359304 | tf_op jit(solution)/shard_map/ppermute | solution.py:311
  457.6 24.8 %collective-permute-start.58 = (bf16[128,1536]{1,0:T(8,128)(2,1)S(1)}, bf16[128,1536]{1,0:T(8,128)(2,1)S(1)}, u32[]{:S(2)}, u32[]{:S(2)}) collective-permute-start(bf16[128,1536]{1,0:T(8,128)(2,1)S(1)} %slice.206), channel_id=1, source_target_pairs={{0,1},{1,0},{2,3},{3,2},{4,5},{5,4},{6,7},{7,6},{8,9},{9,8},{10,11... | collective-permute-start | bytes 1179656 | tf_op jit(solution)/shard_map/ppermute | solution.py:311
  460.1 31.4 %collective-permute-start.63 = (bf16[128,1536]{1,0:T(8,128)(2,1)S(1)}, bf16[128,1536]{1,0:T(8,128)(2,1)}, u32[]{:S(2)}, u32[]{:S(2)}) collective-permute-start(bf16[128,1536]{1,0:T(8,128)(2,1)S(1)} %slice.209), channel_id=1, source_target_pairs={{0,4},{4,0},{1,5},{5,1},{2,6},{6,2},{3,7},{7,3},{8,12},{12,8},{9,1... | collective-permute-start | bytes 1179656 | tf_op jit(solution)/shard_map/ppermute | solution.py:311
  460.7 19.9 %collective-permute-start.64 = (bf16[128,1536]{1,0:T(8,128)(2,1)S(1)}, bf16[128,1536]{1,0:T(8,128)(2,1)S(1)}, u32[]{:S(2)}, u32[]{:S(2)}) collective-permute-start(bf16[128,1536]{1,0:T(8,128)(2,1)S(1)} %get-tuple-element.175), channel_id=1, source_target_pairs={{0,4},{4,0},{1,5},{5,1},{2,6},{6,2},{3,7},{7,3},{8,12},{12,8},{9,1... | collective-permute-start | bytes 1179656 | tf_op jit(solution)/shard_map/ppermute | solution.py:311
  467.4 19.7 %collective-permute-start.62 = (bf16[128,1536]{1,0:T(8,128)(2,1)S(1)}, bf16[128,1536]{1,0:T(8,128)(2,1)S(1)}, u32[]{:S(2)}, u32[]{:S(2)}) collective-permute-start(bf16[128,1536]{1,0:T(8,128)(2,1)S(1)} %reduce-precision_convert_fusion.10), channel_id=1, source_target_pairs={{0,4},{4,0},{1,5},{5,1},{2,6},{6,2},{3,7},{7,3},{8,12},{12,8},{9,1... | collective-permute-start | bytes 1179656 | tf_op jit(solution)/shard_map/ppermute | solution.py:311
  487.2 45.6 %all-to-all-start.6 = ((bf16[4,96,768]{2,1,0:T(8,128)(2,1)}), bf16[4,96,768]{2,1,0:T(8,128)(2,1)}, u32[]{:S(2)}, u32[]{:S(2)}) async-start(bf16[4,96,768]{2,1,0:T(8,128)(2,1)} %bitcast.109), calls=%async_computation.10 | async-start | bytes 1179648 | tf_op jit(solution)/shard_map/all_to_all | solution.py:61
  (113 other events, 953.6 us)
Sparse Core Ops, SparseCore 0:
  397.3 35.9 reduce-scatter.4
  435.8 47.0 reduce-scatter.10
  485.3 47.5 reduce-scatter.6
  535.1 47.5 reduce-scatter.8

commit v2 on v1

--- a/solution.py
+++ b/solution.py
@@ -394,7 +394,7 @@
 SCALARS = pl.BlockSpec(memory_space=pltpu.SMEM)
 
 
-def run_kernel(kernel, micros, at, operands, outs, megabytes=40, scratch=()):
+def run_kernel(kernel, micros, at, operands, outs, megabytes=16, scratch=()):
     return pl.pallas_call(
         kernel,
         out_shape=[jax.ShapeDtypeStruct(shape, dtype) for shape, dtype in outs],
@@ -558,11 +558,11 @@
     outs = outs + [((length, width + bias.shape[1]), bf16)] * count
     return run_kernel(
         functools.partial(expert_kernel, capacity, pieces),
-        6 * count,
+        4 * count,
         at,
         (slots, bias, router, *weights, *second, *cot),
         outs,
-        56,
+        8 + 6 * count,
         [pltpu.VMEM((rows, 1), f32)],
     )
 
@@ -574,38 +574,21 @@
         spread(slots, pieces, capacity, rows, [outs[piece] for piece in pieces])
 
 
-def row_sum_kernel(counts, at, *refs):
-    parts = len(counts)
-    rights = len(refs) // (parts + 2) - 1
-    sources, outs = refs[: parts * (rights + 1)], refs[parts * (rights + 1) : -rights - 2]
-    held, sems = refs[-rights - 2 : -1], refs[-1]
-    copies = []
-    for n, source in enumerate(sources):
-        array, part = divmod(n, parts)
-        target = held[array].at[pl.ds(sum(counts[:part]), counts[part])]
-        copies.append(pltpu.make_async_copy(source, target, sems.at[n]))
-        copies[-1].start()
-    for copy in copies:
-        copy.wait()
-    for out, right in zip(outs, held[1:]):
-        out[...] = dot(held[0][...], right[...], ((0,), (0,))).astype(jnp.bfloat16)
+def row_sum_kernel(parts, at, *refs):
+    arrays = [
+        jnp.concatenate([ref[...] for ref in refs[n : n + parts]], axis=0)
+        for n in range(0, len(refs) - len(refs) // (parts + 1), parts)
+    ]
+    outs = refs[len(arrays) * parts :]
+    for out, right in zip(outs, arrays[1:]):
+        out[...] = dot(arrays[0], right, ((0,), (0,))).astype(jnp.bfloat16)
 
 
 def row_sums(at, left, *rights):
-    counts = [part.shape[0] for part in left]
-    widths = [parts[0].shape[1] for parts in (left, *rights)]
-    sources = [part for parts in (left, *rights) for part in parts]
-    anywhere = pl.BlockSpec(memory_space=pl.ANY)
-    return pl.pallas_call(
-        functools.partial(row_sum_kernel, counts),
-        out_shape=[jax.ShapeDtypeStruct((widths[0], width), jnp.bfloat16) for width in widths[1:]],
-        in_specs=[SCALARS] + [anywhere] * len(sources),
-        out_specs=[WHOLE] * len(rights),
-        scratch_shapes=[pltpu.VMEM((sum(counts), width), jnp.bfloat16) for width in widths]
-        + [pltpu.SemaphoreType.DMA((len(sources),))],
-        cost_estimate=cost(6 * len(rights)),
-        compiler_params=pltpu.CompilerParams(vmem_limit_bytes=40 * 2**20),
-    )(at, *sources)
+    operands = [part for parts in (left, *rights) for part in parts]
+    outs = [((left[0].shape[1], right[0].shape[1]), jnp.bfloat16) for right in rights]
+    kernel = functools.partial(row_sum_kernel, len(left))
+    return run_kernel(kernel, 6 * len(rights), at, operands, outs, 24)
 
 
 def branch_back_kernel(
@@ -636,11 +619,18 @@
     router_ref[...] = dot(second[...], logit_grad, ((0,), (0,)))
 
 
-def attend_back_kernel(at, attended, probs, queries, keys, values, cosine, sine, back_ref):
+def attend_back_kernel(
+    at, attended, probs, queries, keys, values, cosine, sine, branch, back_ref
+):
     f32, bf16 = jnp.float32, jnp.bfloat16
     cosine_tab, sine_tab = cosine[...], -sine[...]
     group_size = HQ // HK
-    width = back_ref.shape[2]
+    places = back_ref.shape[0]
+    branch_width = branch.shape[1] // places
+    width = back_ref.shape[2] - branch_width
+    for place in range(places):
+        here = slice(place * branch_width, (place + 1) * branch_width)
+        back_ref[place, :, width:] = branch[:, here]
     scale = HD ** (-0.5)
 
     def put(position, block):
@@ -670,40 +660,46 @@
 
 def first_back_kernel(at, back, weight, tokens, gain, resid_grad, tokens_ref, gain_ref):
     f32 = jnp.float32
-    parts, _, cols = back.shape
+    parts = back.shape[0]
+    cols = weight.shape[0] * weight.shape[2] // parts
     first_grad = 0.0
     for part in range(parts):
         group, place = divmod(part * cols, weight.shape[2])
         first_grad = first_grad + dot(
-            back[part], weight[group, :, place : place + cols], ((1,), (1,))
+            back[part, :, :cols], weight[group, :, place : place + cols], ((1,), (1,))
         )
     norm_grad, gain_grad = rms_back(tokens[...].astype(f32), gain[...], first_grad)
     gain_ref[...] = gain_grad
     tokens_ref[...] = (resid_grad[...] + norm_grad).astype(jnp.bfloat16)
 
 
-def dense_grad_kernel(at, narrow, branch_cols, qkv_cols, *refs):
+def dense_grad_kernel(at, back, *refs):
     pieces, out_ref, held, sems = refs[:8], refs[8], refs[9], refs[10]
     copies = [
         pltpu.make_async_copy(piece, held.at[n], sems.at[n]) for n, piece in enumerate(pieces)
     ]
     for copy in copies:
         copy.start()
-    length = branch_cols.shape[1]
+    depth, rows, cols = out_ref.shape
+    length = held.shape[1] // 2
+    qkv_width = cols - held.shape[2] // back.shape[0]
+    narrow = sum(back[place, length:].astype(jnp.float32) for place in range(back.shape[0]))
     sums = [0.0, 0.0]
     for n, copy in enumerate(copies):
         copy.wait()
         dc, dy, dx = n // 4, n // 2 % 2, n % 2
         place = 4 * (at[0] ^ dy) + 2 * (at[1] ^ dc) + (at[2] ^ dx)
-        sums[0] = sums[0] + dot(held[n, length:], qkv_cols[place], ((0,), (0,)))
-        sums[1] = sums[1] + dot(held[n, :length], branch_cols[place], ((0,), (0,)))
-    depth, rows, _ = out_ref.shape
-    wide = rows - narrow.shape[1]
+        own = back[place, :length]
+        sums[0] = sums[0] + dot(held[n, length:], own[:, :qkv_width], ((0,), (0,)))
+        sums[1] = sums[1] + dot(held[n, :length], own[:, qkv_width:], ((0,), (0,)))
+    wide = held.shape[2] // depth
+    each = narrow.shape[0] // depth
     for z in range(depth):
         here = slice(z * wide, (z + 1) * wide)
         both = jnp.concatenate([part[here] for part in sums], axis=1)
         out_ref[z, :wide] = both.astype(jnp.bfloat16)
-        out_ref[z, wide:] = narrow[z]
+        kept = [narrow[z * each : (z + 1) * each], jnp.zeros((rows - wide - each, cols), jnp.float32)]
+        out_ref[z, wide:] = jnp.concatenate(kept, axis=0).astype(jnp.bfloat16)
 
 
 def local_pairs(
@@ -753,18 +749,36 @@
     narrow = small_group_gather(narrow)
     ids_all = small_gather(expert_ids)
     column = [own_half] + shifts(own_half)
-    cot_sides = plane_sides(after(out_grad, narrow, ids_all))
+    cot_sides = plane_sides(out_grad)
+    cot_corner = plane_corner(cot_sides)
+    gate_w, up_w, down_w = (
+        lax.dynamic_index_in_dim(weight, own_local, 0, keepdims=False)
+        for weight in (w_gate, w_up, w_down)
+    )
     qkv_half = qkv_cols // 2
     qkv_column = jnp.stack([part[:, :qkv_half] for part in column])
     out_column = jnp.stack([part[:, qkv_half:] for part in column])
-    qkv_column = after(qkv_column, *cot_sides)
+    qkv_column, out_column, narrow, ids_all, cot_corner, gate_w, up_w, down_w = (
+        lax.optimization_barrier(
+            (qkv_column, out_column, narrow, ids_all, cot_corner, gate_w, up_w, down_w)
+        )
+    )
     qkv_sides = plane_sides(qkv_column)
     qkv_corner = plane_corner(qkv_sides)
     out_sides = plane_sides(after(out_column, qkv_corner))
     qkv_pieces = plane_pieces(qkv_column, qkv_sides, qkv_corner)
+    cot_pieces = plane_pieces(out_grad, cot_sides, cot_corner)
     router_w = jnp.pad(narrow[:, :experts_all], ((0, 0), (0, 128 - experts_all)))
     gains = narrow[:, experts_all : experts_all + 2].T.astype(f32)
     gain_one, gain_two = gains[:1], gains[1:]
+
+    expert_range = jnp.arange(128, dtype=jnp.int32)
+    chosen_mask = jnp.any(ids_all[:, :, None] == expert_range[None, None, :], axis=1)
+    bias = jnp.where(chosen_mask, 0.0, -1e30).astype(f32)
+    own_mask = jnp.any(ids_all == own_expert, axis=1).reshape(blocks, block_rows)
+    place = jnp.cumsum(own_mask.astype(jnp.int32), axis=1) - 1
+    slots = jnp.where(own_mask, place, -1)
+    gain_one, bias, slots, router_w = lax.optimization_barrier((gain_one, bias, slots, router_w))
 
     cosine_tab, sine_tab = angles(length, HD)
     cosine_all = jnp.concatenate([cosine_tab, cosine_tab], axis=2)[:, 0]
@@ -802,20 +816,6 @@
     qkv_w = qkv_w.reshape(HK, model_width, qkv_half)
     output_w = output_w.reshape(2, q_cols, out_half)
 
-    cot_corner = plane_corner(cot_sides, (out_corner,))
-    cot_pieces = plane_pieces(out_grad, cot_sides, cot_corner)
-    expert_range = jnp.arange(128, dtype=jnp.int32)
-    chosen_mask = jnp.any(ids_all[:, :, None] == expert_range[None, None, :], axis=1)
-    bias = jnp.where(chosen_mask, 0.0, -1e30).astype(f32)
-    own_mask = jnp.any(ids_all == own_expert, axis=1).reshape(blocks, block_rows)
-    place = jnp.cumsum(own_mask.astype(jnp.int32), axis=1) - 1
-    slots = jnp.where(own_mask, place, -1)
-
-    gate_w, up_w, down_w = (
-        lax.dynamic_index_in_dim(weight, own_local, 0, keepdims=False)
-        for weight in (w_gate, w_up, w_down)
-    )
-
     expert = functools.partial(
         run_expert,
         at=at,
@@ -846,10 +846,6 @@
     second_pieces[3], second_pieces[7] = second_corner, swap(second_corner, "c")
     own_near, own_far = stage_own[6:]
     own_far = swap(own_far, "c")
-    both = jnp.concatenate(
-        lax.optimization_barrier((attended, first_in, second_corner))[:2], axis=0
-    )
-    both_sides = plane_sides(both)
     x_near, x_far, y_near, y_far = stage_sides[6:]
     back_x, back_y = over_core(x_near, x_far), over_core(y_near, y_far)
     first_x, first_y = early_sums(back_x, back_y)
@@ -866,7 +862,8 @@
     gate_part, up_part = row_sums(
         at, [after(rows_in[0], sent)] + rows_in[1:], gate_back, up_back
     )
-    gate_sum = scatter_sum(gate_part, "z")
+    gate_sum = scatter_sum(after(gate_part, down_sum), "z")
+    up_sum = scatter_sum(after(up_part, gate_sum), "z")
     own_near = after(own_near, gate_part)
 
     resid_grad, branch_grad, attended_grad, router_acc, gain_two_grad = run_kernel(
@@ -896,26 +893,37 @@
             ((1, model_width), f32),
         ],
     )
-    (qkv_back,) = run_kernel(
+    qkv_width, branch_width = qkv_cols // plane, model_width // plane
+    dense_cols = qkv_width + branch_width
+    (back_cols,) = run_kernel(
         attend_back_kernel,
-        12,
+        6,
         at,
-        (attended_grad, probs, queries, keys_rot, values_b, cosine_all, sine_all),
-        [((plane, length, qkv_cols // plane), bf16)],
-    )
-    branch_back = jnp.moveaxis(branch_grad.reshape(length, plane, model_width // plane), 1, 0)
-    branch_cols = exchange(branch_back, PLANE)
-    qkv_cols_back = exchange(qkv_back, PLANE)
+        (
+            attended_grad,
+            probs,
+            queries,
+            keys_rot,
+            values_b,
+            cosine_all,
+            sine_all,
+            branch_grad,
+        ),
+        [((plane, length, dense_cols), bf16)],
+    )
     tokens_grad, gain_one_grad = run_kernel(
         first_back_kernel,
-        6,
+        5,
         at,
-        (qkv_back, qkv_w, tokens, gain_one, after(resid_grad, branch_cols)),
+        (back_cols, qkv_w, tokens, gain_one, resid_grad),
         [((length, model_width), bf16), ((1, model_width), f32)],
-    )
-
-    both_corner = plane_corner(both_sides, (qkv_cols_back,))
-    both_pieces = plane_pieces(both, both_sides, both_corner)
+        24,
+    )
+
+    both = jnp.concatenate(
+        lax.optimization_barrier((attended, first_in, resid_grad))[:2], axis=0
+    )
+    both_pieces = plane_pieces(both)
     narrow_part = jnp.concatenate(
         [router_acc[:, :experts_all], gain_one_grad.T, gain_two_grad.T], axis=1
     )
@@ -925,34 +933,30 @@
         narrow_part.reshape(depth, 2, 2, shard_rows, owners, narrow_cols // owners),
         (1, 2, 4, 0, 3, 5),
     ).reshape(plane, depth, shard_rows * narrow_cols // owners)
-    narrow_part = jnp.sum(exchange(narrow_part, PLANE), axis=0)
-    qkv_width = qkv_cols // plane
-    dense_cols = qkv_width + model_width // plane
-    narrow_len = narrow_part.shape[1]
+    narrow_len = narrow_part.shape[2]
     narrow_rows = -(-narrow_len // dense_cols)
+    each_rows = -(-narrow_rows // 4) * 4
+    narrow_part = jnp.pad(
+        narrow_part, ((0, 0), (0, 0), (0, each_rows * dense_cols - narrow_len))
+    ).reshape(plane, depth * each_rows, dense_cols)
+    back_cols = exchange(jnp.concatenate([back_cols, narrow_part.astype(bf16)], axis=1), PLANE)
     kept_rows = -(-narrow_rows // 16) * 16
-    narrow_part = jnp.pad(narrow_part, ((0, 0), (0, kept_rows * dense_cols - narrow_len)))
     wide_rows = local_count * shard_rows
     dense_shape = (depth, wide_rows + kept_rows, dense_cols)
     anywhere = pl.BlockSpec(memory_space=pl.ANY)
     dense_part = pl.pallas_call(
         dense_grad_kernel,
         out_shape=jax.ShapeDtypeStruct(dense_shape, bf16),
-        in_specs=[SCALARS] + [WHOLE] * 3 + [anywhere] * 8,
+        in_specs=[SCALARS, WHOLE] + [anywhere] * 8,
         out_specs=WHOLE,
         scratch_shapes=[
             pltpu.VMEM((plane, 2 * length, model_width), bf16),
             pltpu.SemaphoreType.DMA((plane,)),
         ],
-        cost_estimate=cost(7),
-        compiler_params=pltpu.CompilerParams(vmem_limit_bytes=48 * 2**20),
-    )(
-        at,
-        narrow_part.reshape(depth, kept_rows, dense_cols).astype(bf16),
-        branch_cols,
-        qkv_cols_back,
-        *both_pieces,
-    )
+        cost_estimate=cost(8),
+        compiler_params=pltpu.CompilerParams(vmem_limit_bytes=32 * 2**20),
+    )(at, back_cols, *both_pieces)
+    dense_part = after(dense_part, up_sum)
     dense_sum = scatter_sum(dense_part.reshape(-1, dense_cols), "z")
     wide_sum = dense_sum[: local_count * shard_rows].reshape(2, 2, 1, shard_rows, dense_cols)
     wide_sum = jnp.broadcast_to(wide_sum, (2, 2, owners, shard_rows, dense_cols)).reshape(
@@ -972,15 +976,13 @@
     narrow_sum = narrow_sum[y, c, :, :narrow_len].reshape(owners, shard_rows, -1)
     narrow_sum = jnp.moveaxis(narrow_sum, 0, 1).reshape(shard_rows, narrow_cols).astype(f32)
 
-    up_sum = scatter_sum(after(up_part, dense_sum), "z")
-
     shares = run_kernel(
         functools.partial(mixture_kernel, capacity, groups),
         10,
         at,
-        (slots, down_w, after(gated[0], both_corner), *gated[1:]),
+        (slots, down_w, after(gated[0], both_pieces[3]), *gated[1:]),
         [((length, model_width), bf16)] * plane,
-        48,
+        24,
     )
     mixed = [over_core(near, far) for near, far in zip(shares[:4], shares[4:])]
     early = early_sums(mixed[1], mixed[2])

time: 614 us -> 547 us (0.89)
  waiting for transfers between devices: 277 us -> 235 us
  Pallas kernels: 111 us -> 87.6 us
  starting transfers between devices: 82.8 us -> 74.1 us
  local copies, waits for them, and re-layouts: 85.8 us -> 93.1 us
    reduce_scatter x4, waiting for transfers between devices: 91 us -> 16.5 us  [scatter_sum(): return lax.psum_scatter(block, axes, scatter_dimension=0, tiled=True)]
    ppermute x65, waiting for transfers between devices: 131 us -> 171 us  [swap(): return lax.ppermute(block, axis, [(0, 1), (1, 0)])]
    pallas_call x2 -> x0, Pallas kernels: 18.6 us -> none  [row_sums(): pl.pallas_call(functools.partial(row_sum_kernel, counts), out_shape=[jax....]
    ppermute x6, waiting for transfers between devices: 15.1 us -> 0.02 us  [shifts(): lax.ppermute(block, 'z', [(i, (i + k) % depth) for i in range(depth)])]
    all_to_all x7 -> x5, starting transfers between devices: 27.3 us -> 17.8 us  [exchange(): return lax.all_to_all(block, axes, split_axis=0, concat_axis=0, tiled=True)]
    all_to_all x7 -> x5, waiting for transfers between devices: 38.7 us -> 47.8 us  [exchange(): return lax.all_to_all(block, axes, split_axis=0, concat_axis=0, tiled=True)]
    unnamed x172 -> x247, local copies, waits for them, and re-layouts: 45 us -> 50.2 us
    pallas_call x9 -> x11, Pallas kernels: 84.1 us -> 81.7 us  [run_kernel(): pl.pallas_call(kernel, out_shape=[jax.ShapeDtypeStruct(shape, dtype) for...]
  transfers between devices with their start and end apart: 82 -> 80, of which waited for: 34 -> 37; matrix products, arithmetic and copies ran while one was open for 13% -> 13% of each run, Pallas kernels for 17% -> 14%
where the time goes in v2:
time: 547 us; the launch traced here: 541 us
  waiting for transfers between devices  235 us (43%)
  local copies, waits for them, and re-layouts  93.1 us (17%)
  Pallas kernels  87.6 us (16%)
  starting transfers between devices  74.1 us (14%)
  other arithmetic  34.7 us (6%)
  between operations  16.2 us (3%)
    ppermute x65, waiting for transfers between devices, swap(): return lax.ppermute(block, axis, [(0, 1), (1, 0)])  171 us
    pallas_call x11, Pallas kernels, run_kernel(): pl.pallas_call(kernel, out_shape=[jax.ShapeDtypeStruct(shape, dtype) for...  81.7 us
    unnamed x247, local copies, waits for them, and re-layouts  50.2 us
    all_to_all x5, waiting for transfers between devices, exchange(): return lax.all_to_all(block, axes, split_axis=0, concat_axis=0, tiled=True)  47.8 us
    ppermute x65, starting transfers between devices, swap(): return lax.ppermute(block, axis, [(0, 1), (1, 0)])  46 us
    all_to_all x5, starting transfers between devices, exchange(): return lax.all_to_all(block, axes, split_axis=0, concat_axis=0, tiled=True)  17.8 us
    reduce_scatter x4, waiting for transfers between devices, scatter_sum(): return lax.psum_scatter(block, axes, scatter_dimension=0, tiled=True)  16.5 us
  transfers between devices with their start and end apart: 80, of which 37 were waited for; matrix products, arithmetic and copies ran while one was open for 13% of the time, Pallas kernels for 14%

profile of v2, /device:TPU:0, one launch (start us, length us, event | category | flops | bytes accessed | tf_op | source)
XLA Modules:
  0.0 541.0 jit_solution(17995687098819719745)
XLA Ops:
  7.9 5.1 collective-permute-start.3
  16.6 2.8 collective-permute-start.2
  22.4 5.7 %dynamic-slice_bitcast_fusion.1 = (bf16[1536,768]{1,0:T(8,128)(2,1)}, bf16[1536,768]{1,0:T(8,128)(2,1)}) fusion(bf16[4,1536,768]{2,1,0:T(8,128)(2,1)} %param.23, s32[]{:T(128)S(6)} %select_n.73, bf16[4,1536,768]{2,1,0:T(8,128)(2,1)} %param.22), kind=kLoop, calls=%fused_computation.3 | loop fusion | bytes 9437188 | tf_op jit(solution)/shard_map/jit(dynamic_index_in_dim)/squeeze | solution.py:755
  35.3 12.6 %collective-permute-done.6 = bf16[4,1,1,96,10]{3,0,4,2,1:T(4,128)(2,1)S(1)} collective-permute-done((bf16[4,1,1,96,10]{3,0,4,2,1:T(4,128)(2,1)S(1)}, bf16[4,1,1,96,10]{3,0,4,2,1:T(4,128)(2,1)S(1)}, u32[]{:S(2)}, u32[]{:S(2)}) %collective-permute-start.6) | collective-permute-done | bytes 7712 | tf_op jit(solution)/shard_map/ppermute | solution.py:311
  49.5 2.1 collective-permute-done.9
  61.2 12.9 %collective-permute-done.12.refs_4_ = bf16[256,1536]{1,0:T(8,128)(2,1)S(1)} collective-permute-done((bf16[256,1536]{1,0:T(8,128)(2,1)}, bf16[256,1536]{1,0:T(8,128)(2,1)S(1)}, u32[]{:S(2)}, u32[]{:S(2)}) %collective-permute-start.12) | collective-permute-done | bytes 786464 | tf_op jit(solution)/shard_map/ppermute | solution.py:311
  80.9 4.5 collective-permute-done.13
  91.0 14.5 %collective-permute-done.16.refs_2_ = bf16[4,96,1024]{2,1,0:T(8,128)(2,1)} collective-permute-done((bf16[4,96,1024]{2,1,0:T(8,128)(2,1)}, bf16[4,96,1024]{2,1,0:T(8,128)(2,1)}, u32[]{:S(2)}, u32[]{:S(2)}) %collective-permute-start.16) | collective-permute-done | bytes 786464 | tf_op jit(solution)/shard_map/ppermute | solution.py:311
  110.9 4.9 collective-permute-done.17
  117.5 2.4 fusion
  127.8 8.6 %shard_map.229 = (bf16[256,1536]{1,0:T(8,128)(2,1)S(1)}, bf16[256,1536]{1,0:T(8,128)(2,1)S(1)}, bf16[256,256]{1,0:T(8,128)(2,1)S(1)}, bf16[256,256]{1,0:T(8,128)...) custom-call(s32[7]{0:T(128)S(1)} %copy-done.47, ...), custom_call_target="tpu_custom_call" | custom-call | flops 11000000512 | bytes 11000000 | tf_op jit(solution)/shard_map/pallas_call | solution.py:398
  136.4 2.7 copy-done.58
  142.1 7.2 %collective-permute-done.25 = bf16[2,96,768]{2,1,0:T(8,128)(2,1)S(1)} collective-permute-done((bf16[2,96,768]{2,1,0:T(8,128)(2,1)S(1)}, bf16[2,96,768]{2,1,0:T(8,128)(2,1)S(1)}, u32[]{:S(2)}, u32[]{:S(2)}) %collective-permute-start.25) | collective-permute-done | bytes 294944 | tf_op jit(solution)/shard_map/ppermute | solution.py:311
  151.8 3.3 shard_map.230
  156.3 2.2 copy-done.59
  167.6 9.9 %shard_map.231 = (bf16[384,1536]{1,0:T(8,128)(2,1)S(1)}, bf16[384,1536]{1,0:T(8,128)(2,1)S(1)}, bf16[384,768]{1,0:T(8,128)(2,1)S(1)}, bf16[384,768]{1,0:T(8,128)...) custom-call(s32[7]{0:T(128)S(1)} %copy-done.48, ...), custom_call_target="tpu_custom_call" | custom-call | flops 8000000000 | bytes 8000000 | tf_op jit(solution)/shard_map/pallas_call | solution.py:398
  184.8 9.2 %collective-permute-done.40 = bf16[128,1536]{1,0:T(8,128)(2,1)S(1)} collective-permute-done((bf16[128,1536]{1,0:T(8,128)(2,1)S(1)}, bf16[128,1536]{1,0:T(8,128)(2,1)S(1)}, u32[]{:S(2)}, u32[]{:S(2)}) %collective-permute-start.40) | collective-permute-done | bytes 393248 | tf_op jit(solution)/shard_map/ppermute | solution.py:311
  195.6 8.4 %collective-permute-done.41 = bf16[128,1536]{1,0:T(8,128)(2,1)S(1)} collective-permute-done((bf16[128,1536]{1,0:T(8,128)(2,1)S(1)}, bf16[128,1536]{1,0:T(8,128)(2,1)S(1)}, u32[]{:S(2)}, u32[]{:S(2)}) %collective-permute-start.41) | collective-permute-done | bytes 393248 | tf_op jit(solution)/shard_map/ppermute | solution.py:311
  204.2 18.3 %shard_map.232 = (bf16[768,1536]{1,0:T(8,128)(2,1)S(1)}, bf16[768,1536]{1,0:T(8,128)(2,1)S(1)}, bf16[768,768]{1,0:T(8,128)(2,1)S(1)}, bf16[768,768]{1,0:T(8,128)...) custom-call(s32[7]{0:T(128)S(1)} %copy-done.49, ...), custom_call_target="tpu_custom_call" | custom-call | flops 16000000000 | bytes 16000000 | tf_op jit(solution)/shard_map/pallas_call | solution.py:398
  225.1 8.2 %shard_map.233 = (bf16[384,1536]{1,0:T(8,128)(2,1)S(1)}, bf16[384,1536]{1,0:T(8,128)(2,1)S(1)}, bf16[384,768]{1,0:T(8,128)(2,1)S(1)}, bf16[384,768]{1,0:T(8,128)...) custom-call(s32[7]{0:T(128)S(1)} %copy-done.49, ...), custom_call_target="tpu_custom_call" | custom-call | flops 8000000000 | bytes 8000000 | tf_op jit(solution)/shard_map/pallas_call | solution.py:398
  237.7 4.6 shard_map.234
  248.2 9.7 %collective-permute-done.45 = bf16[128,1664]{1,0:T(8,128)(2,1)S(1)} collective-permute-done((bf16[128,1664]{1,0:T(8,128)(2,1)S(1)}, bf16[128,1664]{1,0:T(8,128)(2,1)S(1)}, u32[]{:S(2)}, u32[]{:S(2)}) %collective-permute-start.45) | collective-permute-done | bytes 426016 | tf_op jit(solution)/shard_map/ppermute | solution.py:311
  264.9 8.1 %shard_map.235 = (bf16[1536,768]{1,0:T(8,128)(2,1)S(1)}, bf16[1536,768]{1,0:T(8,128)(2,1)S(1)}) custom-call(s32[7]{0:T(128)S(1)} %copy-done.50, bf16[384,1536]{1,0:T(8,128)(2,1)S(1)} %copy-done.68, bf16[768,1536]{1,0:T(8,128)(2,1)S(1)} %copy-done.78, bf16[384,1536]{1,0:T(8,128)(2,1)S(1)} %copy-done.70, bf16[384,768]{1,0:T(8,128)(2,1)S(1)} %copy-done.80, ...), custom_call_target="tpu_custom_call" | custom-call | flops 12000000000 | bytes 12000000 | tf_op jit(solution)/shard_map/pallas_call | solution.py:398
  275.8 16.5 %reduce-scatter.5.cloned.1.call-done = bf16[384,768]{1,0:T(8,128)(2,1)} async-done(((bf16[1536,768]{1,0:T(8,128)(2,1)}), bf16[384,768]{1,0:T(8,128)(2,1)}) %reduce-scatter.5.cloned.1.call-update) | async-done | bytes 589840 | tf_op jit(solution)/shard_map/reduce_scatter | solution.py:65
  299.6 8.4 %collective-permute-done.50.first_y = bf16[128,1664]{1,0:T(8,128)(2,1)S(1)} collective-permute-done((bf16[128,1664]{1,0:T(8,128)(2,1)S(1)}, bf16[128,1664]{1,0:T(8,128)(2,1)S(1)}, u32[]{:S(2)}, u32[]{:S(2)}) %collective-permute-start.50) | collective-permute-done | bytes 426016 | tf_op jit(solution)/shard_map/ppermute | solution.py:311
  309.5 7.2 %collective-permute-done.51.last_y = bf16[128,1664]{1,0:T(8,128)(2,1)S(1)} collective-permute-done((bf16[128,1664]{1,0:T(8,128)(2,1)S(1)}, bf16[128,1664]{1,0:T(8,128)(2,1)S(1)}, u32[]{:S(2)}, u32[]{:S(2)}) %collective-permute-start.51) | collective-permute-done | bytes 426016 | tf_op jit(solution)/shard_map/ppermute | solution.py:311
  317.9 2.3 copy-done.60
  320.3 4.3 shard_map.236
  328.0 5.2 shard_map.238.back
  333.3 3.8 shard_map.239
  337.0 24.7 %collective-permute-done.53.refs_2_ = bf16[512,1536]{1,0:T(8,128)(2,1)S(1)} collective-permute-done((bf16[512,1536]{1,0:T(8,128)(2,1)S(1)}, bf16[512,1536]{1,0:T(8,128)(2,1)S(1)}, u32[]{:S(2)}, u32[]{:S(2)}) %collective-permute-start.53) | collective-permute-done | bytes 1572896 | tf_op jit(solution)/shard_map/ppermute | solution.py:311
  368.0 14.1 %collective-permute-done.55 = bf16[256,1536]{1,0:T(8,128)(2,1)} collective-permute-done((bf16[256,1536]{1,0:T(8,128)(2,1)}, bf16[256,1536]{1,0:T(8,128)(2,1)}, u32[]{:S(2)}, u32[]{:S(2)}) %collective-permute-start.55) | collective-permute-done | bytes 786464 | tf_op jit(solution)/shard_map/ppermute | solution.py:311
  382.1 2.2 constant_dynamic-update-slice_fusion.15
  384.2 2.2 constant_dynamic-update-slice_fusion.14.refs_3_
  386.4 7.4 %shard_map.237 = (bf16[256,1536]{1,0:T(8,128)(2,1)S(1)}, bf16[256,1536]{1,0:T(8,128)(2,1)S(1)}, bf16[256,1536]{1,0:T(8,128)(2,1)S(1)}, bf16[256,1536]{1,0:T(8,12...) custom-call(s32[7]{0:T(128)S(1)} %copy-done.50, ...), custom_call_target="tpu_custom_call" | custom-call | flops 10000000000 | bytes 10000000 | tf_op jit(solution)/shard_map/pallas_call | solution.py:398
  399.1 3.6 all-to-all-start
  412.9 17.3 %all-to-all-done.back = bf16[8,272,448]{2,1,0:T(8,128)(2,1)S(1)} async-done(((bf16[8,272,448]{2,1,0:T(8,128)(2,1)}), bf16[8,272,448]{2,1,0:T(8,128)(2,1)S(1)}, u32[]{:S(2)}, u32[]{:S(2)}) %all-to-all-start) | async-done | bytes 1949728 | tf_op jit(solution)/shard_map/all_to_all | solution.py:61
  434.4 5.9 %shard_map.240 = bf16[4,400,448]{2,1,0:T(8,128)(2,1)S(1)} custom-call(s32[7]{0:T(128)S(1)} %copy-done.50, bf16[8,272,448]{2,1,0:T(8,128)(2,1)S(1)} %all-to-all-done.back, bf16[512,1536]{1,0:T(8,128)(2,1)S(1)} %copy-done.35, bf16[512,1536]{1,0:T(8,128)(2,1)S(1)} %copy-done.33, bf16[512,1536]{1,0:T(8,128)(2,1)S(1)} %copy-done.31, ...), custom_call_target="tpu_custom_call" | custom-call | flops 8000000000 | bytes 8000000 | tf_op jit(solution)/shard_map/pallas_call | solution.py:947
  451.4 3.5 all-to-all-start.4
  454.8 13.0 %collective-permute-done.64 = bf16[128,1536]{1,0:T(8,128)(2,1)} collective-permute-done((bf16[128,1536]{1,0:T(8,128)(2,1)}, bf16[128,1536]{1,0:T(8,128)(2,1)}, u32[]{:S(2)}, u32[]{:S(2)}) %collective-permute-start.64) | collective-permute-done | bytes 393248 | tf_op jit(solution)/shard_map/ppermute | solution.py:311
  469.9 10.9 %all-to-all-done.4 = bf16[4,96,768]{2,1,0:T(8,128)(2,1)S(1)} async-done(((bf16[4,96,768]{2,1,0:T(8,128)(2,1)}), bf16[4,96,768]{2,1,0:T(8,128)(2,1)S(1)}, u32[]{:S(2)}, u32[]{:S(2)}) %all-to-all-start.4) | async-done | bytes 589856 | tf_op jit(solution)/shard_map/all_to_all | solution.py:61
  480.8 3.5 all-to-all-start.2
  486.3 7.5 %all-to-all-done.2 = bf16[4,96,768]{2,1,0:T(8,128)(2,1)S(1)} async-done(((bf16[4,96,768]{2,1,0:T(8,128)(2,1)}), bf16[4,96,768]{2,1,0:T(8,128)(2,1)S(1)}, u32[]{:S(2)}, u32[]{:S(2)}) %all-to-all-start.2) | async-done | bytes 589856 | tf_op jit(solution)/shard_map/all_to_all | solution.py:61
  493.8 3.5 all-to-all-start.3
  501.7 5.1 all-to-all-done.3
  507.6 3.7 all-to-all-start.1
  511.4 3.0 fusion.2
  517.8 7.0 %all-to-all-done.1 = bf16[8,112,448]{2,1,0:T(8,128)(2,1)S(1)} async-done(((bf16[8,112,448]{2,1,0:T(8,128)(2,1)}), bf16[8,112,448]{2,1,0:T(8,128)(2,1)S(1)}, u32[]{:S(2)}, u32[]{:S(2)}) %all-to-all-start.1) | async-done | bytes 802848 | tf_op jit(solution)/shard_map/all_to_all | solution.py:61
  (494 shorter events, 171.3 us)
Async XLA Ops:
  7.2 285.1 %reduce-scatter.5.cloned.1.call-start = ((), (), s32[]{:S(2)}) async-start(), calls=%async_computation.9 | async-start | bytes 2949120 | tf_op jit(solution)/shard_map/reduce_scatter | solution.py:65
  7.9 21.6 %collective-permute-start.3 = (bf16[96,10]{0,1:T(8,128)(2,1)S(1)}, bf16[96,10]{0,1:T(8,128)(2,1)S(1)}, u32[]{:S(2)}, u32[]{:S(2)}) collective-permute-start(bf16[96,10]{0,1:T(8,128)(2,1)S(1)} %pad_maximum_fusion.9), channel_id=1, source_target_pairs={{0,24},{8,0},{16,8},{24,16},{1,25},{9,1},{17,9},{25,17},{2,26},{10... | collective-permute-start | bytes 5768 | tf_op jit(solution)/shard_map/ppermute | solution.py:317
  13.0 16.5 %collective-permute-start.4 = (bf16[96,10]{0,1:T(8,128)(2,1)S(1)}, bf16[96,10]{0,1:T(8,128)(2,1)S(1)}, u32[]{:S(2)}, u32[]{:S(2)}) collective-permute-start(bf16[96,10]{0,1:T(8,128)(2,1)S(1)} %pad_maximum_fusion.9), channel_id=1, source_target_pairs={{0,16},{8,24},{16,0},{24,8},{1,17},{9,25},{17,1},{25,9},{2,18},{10... | collective-permute-start | bytes 5768 | tf_op jit(solution)/shard_map/ppermute | solution.py:317
  13.0 18.1 %collective-permute-start.5 = (bf16[96,10]{0,1:T(8,128)(2,1)S(1)}, bf16[96,10]{0,1:T(8,128)(2,1)S(1)}, u32[]{:S(2)}, u32[]{:S(2)}) collective-permute-start(bf16[96,10]{0,1:T(8,128)(2,1)S(1)} %pad_maximum_fusion.9), channel_id=1, source_target_pairs={{0,8},{8,16},{16,24},{24,0},{1,9},{9,17},{17,25},{25,1},{2,10},{10... | collective-permute-start | bytes 5768 | tf_op jit(solution)/shard_map/ppermute | solution.py:317
  16.6 39.9 %collective-permute-start.2 = (bf16[96,1792]{1,0:T(8,128)(2,1)}, bf16[96,1792]{1,0:T(8,128)(2,1)}, u32[]{:S(2)}, u32[]{:S(2)}) collective-permute-start(bf16[96,1792]{1,0:T(8,128)(2,1)} %pad_maximum_fusion.5), channel_id=1, source_target_pairs={{0,24},{8,0},{16,8},{24,16},{1,25},{9,1},{17,9},{25,17},{2,26},{10... | collective-permute-start | bytes 1032200 | tf_op jit(solution)/shard_map/ppermute | solution.py:317
  19.4 38.0 %collective-permute-start.1 = (bf16[96,1792]{1,0:T(8,128)(2,1)}, bf16[96,1792]{1,0:T(8,128)(2,1)}, u32[]{:S(2)}, u32[]{:S(2)}) collective-permute-start(bf16[96,1792]{1,0:T(8,128)(2,1)} %pad_maximum_fusion.5), channel_id=1, source_target_pairs={{0,16},{8,24},{16,0},{24,8},{1,17},{9,25},{17,1},{25,9},{2,18},{10... | collective-permute-start | bytes 1032200 | tf_op jit(solution)/shard_map/ppermute | solution.py:317
  29.5 28.8 %collective-permute-start = (bf16[96,1792]{1,0:T(8,128)(2,1)}, bf16[96,1792]{1,0:T(8,128)(2,1)}, u32[]{:S(2)}, u32[]{:S(2)}) collective-permute-start(bf16[96,1792]{1,0:T(8,128)(2,1)} %pad_maximum_fusion.5), channel_id=1, source_target_pairs={{0,8},{8,16},{16,24},{24,0},{1,9},{9,17},{17,25},{25,1},{2,10},{10... | collective-permute-start | bytes 1032200 | tf_op jit(solution)/shard_map/ppermute | solution.py:317
  29.5 31.6 %collective-permute-start.11 = (bf16[256,1536]{1,0:T(8,128)(2,1)}, bf16[256,1536]{1,0:T(8,128)(2,1)S(1)}, u32[]{:S(2)}, u32[]{:S(2)}) collective-permute-start(bf16[256,1536]{1,0:T(8,128)(2,1)} %cot.1), channel_id=1, source_target_pairs={{0,4},{4,0},{1,5},{5,1},{2,6},{6,2},{3,7},{7,3},{8,12},{12,8},{9,1... | collective-permute-start | bytes 2359304 | tf_op jit(solution)/shard_map/ppermute | solution.py:311
  34.8 13.1 %collective-permute-start.6 = (bf16[4,1,1,96,10]{3,0,4,2,1:T(4,128)(2,1)S(1)}, bf16[4,1,1,96,10]{3,0,4,2,1:T(4,128)(2,1)S(1)}, u32[]{:S(2)}, u32[]{:S(2)}) collective-permute-start(bf16[4,1,1,96,10]{3,0,4,2,1:T(4,128)(2,1)S(1)} %bitcast.111), channel_id=1, source_target_pairs={{0,4},{4,0},{1,5},{5,1},{2,6},{6,2},{3,7},{7,3},{8,12},{12,8},{9,1... | collective-permute-start | bytes 23048 | tf_op jit(solution)/shard_map/ppermute | solution.py:311
  54.3 19.8 %collective-permute-start.12 = (bf16[256,1536]{1,0:T(8,128)(2,1)}, bf16[256,1536]{1,0:T(8,128)(2,1)S(1)}, u32[]{:S(2)}, u32[]{:S(2)}) collective-permute-start(bf16[256,1536]{1,0:T(8,128)(2,1)} %cot.1), channel_id=1, source_target_pairs={{0,1},{1,0},{2,3},{3,2},{4,5},{5,4},{6,7},{7,6},{8,9},{9,8},{10,11... | collective-permute-start | bytes 2359304 | tf_op jit(solution)/shard_map/ppermute | solution.py:311
  87.6 17.9 %collective-permute-start.16 = (bf16[4,96,1024]{2,1,0:T(8,128)(2,1)}, bf16[4,96,1024]{2,1,0:T(8,128)(2,1)}, u32[]{:S(2)}, u32[]{:S(2)}) collective-permute-start(bf16[4,96,1024]{2,1,0:T(8,128)(2,1)} %pad_maximum_fusion.1.refs_0_), channel_id=1, source_target_pairs={{0,4},{4,0},{1,5},{5,1},{2,6},{6,2},{3,7},{7,3},{8,12},{12,8},{9,1... | collective-permute-start | bytes 2359304 | tf_op jit(solution)/shard_map/ppermute | solution.py:311
  89.1 17.6 %collective-permute-start.15 = (bf16[4,96,1024]{2,1,0:T(8,128)(2,1)}, bf16[4,96,1024]{2,1,0:T(8,128)(2,1)}, u32[]{:S(2)}, u32[]{:S(2)}) collective-permute-start(bf16[4,96,1024]{2,1,0:T(8,128)(2,1)} %pad_maximum_fusion.1.refs_0_), channel_id=1, source_target_pairs={{0,1},{1,0},{2,3},{3,2},{4,5},{5,4},{6,7},{7,6},{8,9},{9,8},{10,11... | collective-permute-start | bytes 2359304 | tf_op jit(solution)/shard_map/ppermute | solution.py:311
  90.9 32.6 %collective-permute-start.19 = (bf16[4,96,1024]{2,1,0:T(8,128)(2,1)}, bf16[4,96,1024]{2,1,0:T(8,128)(2,1)}, u32[]{:S(2)}, u32[]{:S(2)}) collective-permute-start(bf16[4,96,1024]{2,1,0:T(8,128)(2,1)} %pad_maximum_fusion.1.refs_0_), channel_id=1, source_target_pairs={{0,2},{2,0},{1,3},{3,1},{4,6},{6,4},{5,7},{7,5},{8,10},{10,8},{9,1... | collective-permute-start | bytes 2359304 | tf_op jit(solution)/shard_map/ppermute | solution.py:311
  110.3 14.7 %collective-permute-start.20 = (bf16[4,96,1024]{2,1,0:T(8,128)(2,1)}, bf16[4,96,1024]{2,1,0:T(8,128)(2,1)}, u32[]{:S(2)}, u32[]{:S(2)}) collective-permute-start(bf16[4,96,1024]{2,1,0:T(8,128)(2,1)} %collective-permute-done.15.refs_1_), channel_id=1, source_target_pairs={{0,2},{2,0},{1,3},{3,1},{4,6},{6,4},{5,7},{7,5},{8,10},{10,8},{9,1... | collective-permute-start | bytes 2359304 | tf_op jit(solution)/shard_map/ppermute | solution.py:311
  110.4 14.7 %collective-permute-start.21 = (bf16[4,96,1024]{2,1,0:T(8,128)(2,1)}, bf16[4,96,1024]{2,1,0:T(8,128)(2,1)}, u32[]{:S(2)}, u32[]{:S(2)}) collective-permute-start(bf16[4,96,1024]{2,1,0:T(8,128)(2,1)} %collective-permute-done.16.refs_2_), channel_id=1, source_target_pairs={{0,2},{2,0},{1,3},{3,1},{4,6},{6,4},{5,7},{7,5},{8,10},{10,8},{9,1... | collective-permute-start | bytes 2359304 | tf_op jit(solution)/shard_map/ppermute | solution.py:311
  122.1 18.3 %collective-permute-start.23 = (bf16[4,96,768]{2,1,0:T(8,128)(2,1)}, bf16[4,96,768]{2,1,0:T(8,128)(2,1)S(1)}, u32[]{:S(2)}, u32[]{:S(2)}) collective-permute-start(bf16[4,96,768]{2,1,0:T(8,128)(2,1)} %pad_maximum_fusion.4.refs_0_), channel_id=1, source_target_pairs={{0,1},{1,0},{2,3},{3,2},{4,5},{5,4},{6,7},{7,6},{8,9},{9,8},{10,11... | collective-permute-start | bytes 1769480 | tf_op jit(solution)/shard_map/ppermute | solution.py:311
  123.6 16.8 %collective-permute-start.24 = (bf16[4,96,768]{2,1,0:T(8,128)(2,1)}, bf16[4,96,768]{2,1,0:T(8,128)(2,1)S(1)}, u32[]{:S(2)}, u32[]{:S(2)}) collective-permute-start(bf16[4,96,768]{2,1,0:T(8,128)(2,1)} %pad_maximum_fusion.4.refs_0_), channel_id=1, source_target_pairs={{0,4},{4,0},{1,5},{5,1},{2,6},{6,2},{3,7},{7,3},{8,12},{12,8},{9,1... | collective-permute-start | bytes 1769480 | tf_op jit(solution)/shard_map/ppermute | solution.py:311
  158.6 21.2 %collective-permute-start.33 = (bf16[256,1536]{1,0:T(8,128)(2,1)}, bf16[256,1536]{1,0:T(8,128)(2,1)}, u32[]{:S(2)}, u32[]{:S(2)}) collective-permute-start(bf16[256,1536]{1,0:T(8,128)(2,1)} %get-tuple-element.124.refs_0_.second), channel_id=1, source_target_pairs={{0,1},{1,0},{2,3},{3,2},{4,5},{5,4},{6,7},{7,6},{8,9},{9,8},{10,11... | collective-permute-start | bytes 2359304 | tf_op jit(solution)/shard_map/ppermute | solution.py:311
  160.1 19.8 %collective-permute-start.34 = (bf16[256,1536]{1,0:T(8,128)(2,1)}, bf16[256,1536]{1,0:T(8,128)(2,1)}, u32[]{:S(2)}, u32[]{:S(2)}) collective-permute-start(bf16[256,1536]{1,0:T(8,128)(2,1)} %get-tuple-element.124.refs_0_.second), channel_id=1, source_target_pairs={{0,4},{4,0},{1,5},{5,1},{2,6},{6,2},{3,7},{7,3},{8,12},{12,8},{9,1... | collective-permute-start | bytes 2359304 | tf_op jit(solution)/shard_map/ppermute | solution.py:311
  183.8 20.3 %collective-permute-start.37 = (bf16[256,1536]{1,0:T(8,128)(2,1)S(1)}, bf16[256,1536]{1,0:T(8,128)(2,1)S(1)}, u32[]{:S(2)}, u32[]{:S(2)}) collective-permute-start(bf16[256,1536]{1,0:T(8,128)(2,1)S(1)} %copy-done.42), channel_id=1, source_target_pairs={{0,2},{2,0},{1,3},{3,1},{4,6},{6,4},{5,7},{7,5},{8,10},{10,8},{9,1... | collective-permute-start | bytes 2359304 | tf_op jit(solution)/shard_map/ppermute | solution.py:311
  183.8 20.3 %collective-permute-start.38 = (bf16[256,1536]{1,0:T(8,128)(2,1)S(1)}, bf16[256,1536]{1,0:T(8,128)(2,1)S(1)}, u32[]{:S(2)}, u32[]{:S(2)}) collective-permute-start(bf16[256,1536]{1,0:T(8,128)(2,1)S(1)} %copy-done.40), channel_id=1, source_target_pairs={{0,2},{2,0},{1,3},{3,1},{4,6},{6,4},{5,7},{7,5},{8,10},{10,8},{9,1... | collective-permute-start | bytes 2359304 | tf_op jit(solution)/shard_map/ppermute | solution.py:311
  184.3 19.8 %collective-permute-start.35 = (bf16[256,1536]{1,0:T(8,128)(2,1)}, bf16[256,1536]{1,0:T(8,128)(2,1)S(1)}, u32[]{:S(2)}, u32[]{:S(2)}) collective-permute-start(bf16[256,1536]{1,0:T(8,128)(2,1)} %collective-permute-done.33.refs_0_), channel_id=1, source_target_pairs={{0,2},{2,0},{1,3},{3,1},{4,6},{6,4},{5,7},{7,5},{8,10},{10,8},{9,1... | collective-permute-start | bytes 2359304 | tf_op jit(solution)/shard_map/ppermute | solution.py:311
  184.4 19.7 %collective-permute-start.36 = (bf16[256,1536]{1,0:T(8,128)(2,1)}, bf16[256,1536]{1,0:T(8,128)(2,1)S(1)}, u32[]{:S(2)}, u32[]{:S(2)}) collective-permute-start(bf16[256,1536]{1,0:T(8,128)(2,1)} %collective-permute-done.34.refs_2_), channel_id=1, source_target_pairs={{0,2},{2,0},{1,3},{3,1},{4,6},{6,4},{5,7},{7,5},{8,10},{10,8},{9,1... | collective-permute-start | bytes 2359304 | tf_op jit(solution)/shard_map/ppermute | solution.py:311
  204.0 19.1 %collective-permute-start.43 = (bf16[256,1536]{1,0:T(8,128)(2,1)S(1)}, bf16[256,1536]{1,0:T(8,128)(2,1)S(1)}, u32[]{:S(2)}, u32[]{:S(2)}) collective-permute-start(bf16[256,1536]{1,0:T(8,128)(2,1)S(1)} %copy-done.23), channel_id=1, source_target_pairs={{0,2},{2,0},{1,3},{3,1},{4,6},{6,4},{5,7},{7,5},{8,10},{10,8},{9,1... | collective-permute-start | bytes 2359304 | tf_op jit(solution)/shard_map/ppermute | solution.py:311
  243.7 122.4 %reduce-scatter.7.cloned.1.call-start = ((), (), s32[]{:S(2)}) async-start(), calls=%async_computation.10 | async-start | bytes 2949120 | tf_op jit(solution)/shard_map/reduce_scatter | solution.py:65
  244.2 49.5 %collective-permute-start.49 = (bf16[256,1664]{1,0:T(8,128)(2,1)}, bf16[256,1664]{1,0:T(8,128)(2,1)}, u32[]{:S(2)}, u32[]{:S(2)}) collective-permute-start(bf16[256,1664]{1,0:T(8,128)(2,1)} %copy-done.52), channel_id=1, source_target_pairs={{0,2},{2,0},{1,3},{3,1},{4,6},{6,4},{5,7},{7,5},{8,10},{10,8},{9,1... | collective-permute-start | bytes 2555912 | tf_op jit(solution)/shard_map/ppermute | solution.py:311
  292.3 149.2 %reduce-scatter.9.cloned.1.call-start = ((), (), s32[]{:S(2)}) async-start(), calls=%async_computation.11 | async-start | bytes 2949120 | tf_op jit(solution)/shard_map/reduce_scatter | solution.py:65
  298.4 18.3 %collective-permute-start.51 = (bf16[128,1664]{1,0:T(8,128)(2,1)S(1)}, bf16[128,1664]{1,0:T(8,128)(2,1)S(1)}, u32[]{:S(2)}, u32[]{:S(2)}) collective-permute-start(bf16[128,1664]{1,0:T(8,128)(2,1)S(1)} %reduce-precision_convert_fusion.7), channel_id=1, source_target_pairs={{0,4},{4,0},{1,5},{5,1},{2,6},{6,2},{3,7},{7,3},{8,12},{12,8},{9,1... | collective-permute-start | bytes 1277960 | tf_op jit(solution)/shard_map/ppermute | solution.py:311
  299.0 18.9 %collective-permute-start.52 = (bf16[128,1664]{1,0:T(8,128)(2,1)S(1)}, bf16[128,1664]{1,0:T(8,128)(2,1)S(1)}, u32[]{:S(2)}, u32[]{:S(2)}) collective-permute-start(bf16[128,1664]{1,0:T(8,128)(2,1)S(1)} %copy-done.106), channel_id=1, source_target_pairs={{0,1},{1,0},{2,3},{3,2},{4,5},{5,4},{6,7},{7,6},{8,9},{9,8},{10,11... | collective-permute-start | bytes 1277960 | tf_op jit(solution)/shard_map/ppermute | solution.py:311
  325.8 35.9 %collective-permute-start.53 = (bf16[512,1536]{1,0:T(8,128)(2,1)S(1)}, bf16[512,1536]{1,0:T(8,128)(2,1)S(1)}, u32[]{:S(2)}, u32[]{:S(2)}) collective-permute-start(bf16[512,1536]{1,0:T(8,128)(2,1)S(1)} %constant_dynamic-update-slice_fusion.12.refs_0_), channel_id=1, source_target_pairs={{0,4},{4,0},{1,5},{5,1},{2,6},{6,2},{3,7},{7,3},{8,12},{12,8},{9,1... | collective-permute-start | bytes 4718600 | tf_op jit(solution)/shard_map/ppermute | solution.py:311
  326.5 36.2 %collective-permute-start.54 = (bf16[512,1536]{1,0:T(8,128)(2,1)S(1)}, bf16[512,1536]{1,0:T(8,128)(2,1)S(1)}, u32[]{:S(2)}, u32[]{:S(2)}) collective-permute-start(bf16[512,1536]{1,0:T(8,128)(2,1)S(1)} %constant_dynamic-update-slice_fusion.12.refs_0_), channel_id=1, source_target_pairs={{0,1},{1,0},{2,3},{3,2},{4,5},{5,4},{6,7},{7,6},{8,9},{9,8},{10,11... | collective-permute-start | bytes 4718600 | tf_op jit(solution)/shard_map/ppermute | solution.py:311
  363.7 18.3 %collective-permute-start.55 = (bf16[256,1536]{1,0:T(8,128)(2,1)}, bf16[256,1536]{1,0:T(8,128)(2,1)}, u32[]{:S(2)}, u32[]{:S(2)}) collective-permute-start(bf16[256,1536]{1,0:T(8,128)(2,1)} %slice.203), channel_id=1, source_target_pairs={{0,1},{1,0},{2,3},{3,2},{4,5},{5,4},{6,7},{7,6},{8,9},{9,8},{10,11... | collective-permute-start | bytes 2359304 | tf_op jit(solution)/shard_map/ppermute | solution.py:311
  365.4 18.8 %collective-permute-start.56 = (bf16[256,1536]{1,0:T(8,128)(2,1)}, bf16[256,1536]{1,0:T(8,128)(2,1)}, u32[]{:S(2)}, u32[]{:S(2)}) collective-permute-start(bf16[256,1536]{1,0:T(8,128)(2,1)} %slice.204), channel_id=1, source_target_pairs={{0,4},{4,0},{1,5},{5,1},{2,6},{6,2},{3,7},{7,3},{8,12},{12,8},{9,1... | collective-permute-start | bytes 2359304 | tf_op jit(solution)/shard_map/ppermute | solution.py:311
  399.1 31.1 %all-to-all-start = ((bf16[8,272,448]{2,1,0:T(8,128)(2,1)}), bf16[8,272,448]{2,1,0:T(8,128)(2,1)S(1)}, u32[]{:S(2)}, u32[]{:S(2)}) async-start(bf16[8,272,448]{2,1,0:T(8,128)(2,1)} %pad_maximum_fusion), calls=%async_computation | async-start | bytes 4456448 | tf_op jit(solution)/shard_map/all_to_all | solution.py:61
  402.7 96.6 %reduce-scatter.11.cloned.1.call-start = ((), (), s32[]{:S(2)}) async-start(), calls=%async_computation.12 | async-start | bytes 2048000 | tf_op jit(solution)/shard_map/reduce_scatter | solution.py:65
  403.8 26.4 %collective-permute-start.70 = (bf16[512,1536]{1,0:T(8,128)(2,1)}, bf16[512,1536]{1,0:T(8,128)(2,1)}, u32[]{:S(2)}, u32[]{:S(2)}) collective-permute-start(bf16[512,1536]{1,0:T(8,128)(2,1)} %constant_dynamic-update-slice_fusion.14.refs_3_), channel_id=1, source_target_pairs={{0,2},{2,0},{1,3},{3,1},{4,6},{6,4},{5,7},{7,5},{8,10},{10,8},{9,1... | collective-permute-start | bytes 4718600 | tf_op jit(solution)/shard_map/ppermute | solution.py:311
  404.0 37.6 %collective-permute-start.57 = (bf16[256,1536]{1,0:T(8,128)(2,1)}, bf16[256,1536]{1,0:T(8,128)(2,1)}, u32[]{:S(2)}, u32[]{:S(2)}) collective-permute-start(bf16[256,1536]{1,0:T(8,128)(2,1)} %copy-done.57), channel_id=1, source_target_pairs={{0,2},{2,0},{1,3},{3,1},{4,6},{6,4},{5,7},{7,5},{8,10},{10,8},{9,1... | collective-permute-start | bytes 2359304 | tf_op jit(solution)/shard_map/ppermute | solution.py:311
  406.9 38.8 %collective-permute-start.59 = (bf16[256,1536]{1,0:T(8,128)(2,1)}, bf16[256,1536]{1,0:T(8,128)(2,1)}, u32[]{:S(2)}, u32[]{:S(2)}) collective-permute-start(bf16[256,1536]{1,0:T(8,128)(2,1)} %get-tuple-element.172), channel_id=1, source_target_pairs={{0,2},{2,0},{1,3},{3,1},{4,6},{6,4},{5,7},{7,5},{8,10},{10,8},{9,1... | collective-permute-start | bytes 2359304 | tf_op jit(solution)/shard_map/ppermute | solution.py:311
  409.0 102.3 %collective-permute-start.66 = (bf16[256,1536]{1,0:T(8,128)(2,1)}, bf16[256,1536]{1,0:T(8,128)(2,1)}, u32[]{:S(2)}, u32[]{:S(2)}) collective-permute-start(bf16[256,1536]{1,0:T(8,128)(2,1)} %get-tuple-element.176), channel_id=1, source_target_pairs={{0,2},{2,0},{1,3},{3,1},{4,6},{6,4},{5,7},{7,5},{8,10},{10,8},{9,1... | collective-permute-start | bytes 2359304 | tf_op jit(solution)/shard_map/ppermute | solution.py:311
  411.3 38.0 %collective-permute-start.61 = (bf16[128,1536]{1,0:T(8,128)(2,1)}, bf16[128,1536]{1,0:T(8,128)(2,1)}, u32[]{:S(2)}, u32[]{:S(2)}) collective-permute-start(bf16[128,1536]{1,0:T(8,128)(2,1)} %get-tuple-element.196), channel_id=1, source_target_pairs={{0,1},{1,0},{2,3},{3,2},{4,5},{5,4},{6,7},{7,6},{8,9},{9,8},{10,11... | collective-permute-start | bytes 1179656 | tf_op jit(solution)/shard_map/ppermute | solution.py:311
  444.7 39.6 %collective-permute-start.58 = (bf16[128,1536]{1,0:T(8,128)(2,1)}, bf16[128,1536]{1,0:T(8,128)(2,1)}, u32[]{:S(2)}, u32[]{:S(2)}) collective-permute-start(bf16[128,1536]{1,0:T(8,128)(2,1)} %slice.205), channel_id=1, source_target_pairs={{0,1},{1,0},{2,3},{3,2},{4,5},{5,4},{6,7},{7,6},{8,9},{9,8},{10,11... | collective-permute-start | bytes 1179656 | tf_op jit(solution)/shard_map/ppermute | solution.py:311
  447.2 50.1 %collective-permute-start.63 = (bf16[128,1536]{1,0:T(8,128)(2,1)S(1)}, bf16[128,1536]{1,0:T(8,128)(2,1)}, u32[]{:S(2)}, u32[]{:S(2)}) collective-permute-start(bf16[128,1536]{1,0:T(8,128)(2,1)S(1)} %slice.208), channel_id=1, source_target_pairs={{0,4},{4,0},{1,5},{5,1},{2,6},{6,2},{3,7},{7,3},{8,12},{12,8},{9,1... | collective-permute-start | bytes 1179656 | tf_op jit(solution)/shard_map/ppermute | solution.py:311
  448.2 19.7 %collective-permute-start.64 = (bf16[128,1536]{1,0:T(8,128)(2,1)}, bf16[128,1536]{1,0:T(8,128)(2,1)}, u32[]{:S(2)}, u32[]{:S(2)}) collective-permute-start(bf16[128,1536]{1,0:T(8,128)(2,1)} %get-tuple-element.197), channel_id=1, source_target_pairs={{0,4},{4,0},{1,5},{5,1},{2,6},{6,2},{3,7},{7,3},{8,12},{12,8},{9,1... | collective-permute-start | bytes 1179656 | tf_op jit(solution)/shard_map/ppermute | solution.py:311
  450.4 33.9 %collective-permute-start.62 = (bf16[128,1536]{1,0:T(8,128)(2,1)S(1)}, bf16[128,1536]{1,0:T(8,128)(2,1)S(1)}, u32[]{:S(2)}, u32[]{:S(2)}) collective-permute-start(bf16[128,1536]{1,0:T(8,128)(2,1)S(1)} %reduce-precision_convert_fusion.10), channel_id=1, source_target_pairs={{0,4},{4,0},{1,5},{5,1},{2,6},{6,2},{3,7},{7,3},{8,12},{12,8},{9,1... | collective-permute-start | bytes 1179656 | tf_op jit(solution)/shard_map/ppermute | solution.py:311
  451.4 29.4 %all-to-all-start.4 = ((bf16[4,96,768]{2,1,0:T(8,128)(2,1)}), bf16[4,96,768]{2,1,0:T(8,128)(2,1)S(1)}, u32[]{:S(2)}, u32[]{:S(2)}) async-start(bf16[4,96,768]{2,1,0:T(8,128)(2,1)} %bitcast.42), calls=%async_computation.8 | async-start | bytes 1179648 | tf_op jit(solution)/shard_map/all_to_all | solution.py:61
  468.9 28.4 %collective-permute-start.65 = (bf16[128,1536]{1,0:T(8,128)(2,1)S(1)}, bf16[128,1536]{1,0:T(8,128)(2,1)S(1)}, u32[]{:S(2)}, u32[]{:S(2)}) collective-permute-start(bf16[128,1536]{1,0:T(8,128)(2,1)S(1)} %reduce-precision_convert_fusion.9), channel_id=1, source_target_pairs={{0,1},{1,0},{2,3},{3,2},{4,5},{5,4},{6,7},{7,6},{8,9},{9,8},{10,11... | collective-permute-start | bytes 1179656 | tf_op jit(solution)/shard_map/ppermute | solution.py:311
  493.8 13.0 %all-to-all-start.3 = ((bf16[4,96,768]{2,1,0:T(8,128)(2,1)}), bf16[4,96,768]{2,1,0:T(8,128)(2,1)S(1)}, u32[]{:S(2)}, u32[]{:S(2)}) async-start(bf16[4,96,768]{2,1,0:T(8,128)(2,1)} %bitcast.41), calls=%async_computation.7 | async-start | bytes 1179648 | tf_op jit(solution)/shard_map/all_to_all | solution.py:61
  507.6 17.2 %all-to-all-start.1 = ((bf16[8,112,448]{2,1,0:T(8,128)(2,1)}), bf16[8,112,448]{2,1,0:T(8,128)(2,1)S(1)}, u32[]{:S(2)}, u32[]{:S(2)}) async-start(bf16[8,112,448]{2,1,0:T(8,128)(2,1)} %maximum_maximum_fusion), calls=%async_computation.5 | async-start | bytes 1835008 | tf_op jit(solution)/shard_map/all_to_all | solution.py:61
  (151 other events, 1417.5 us)
Sparse Core Ops, SparseCore 0:
  243.9 48.3 reduce-scatter.4
  294.6 47.5 reduce-scatter.6
  366.3 46.4 reduce-scatter.8
  441.6 34.8 reduce-scatter.10

commit v3 on v2

--- a/solution.py
+++ b/solution.py
@@ -391,15 +391,16 @@
 
 
 WHOLE = pl.BlockSpec(memory_space=pltpu.VMEM)
+IN_HBM = pl.BlockSpec(memory_space=pltpu.HBM)
 SCALARS = pl.BlockSpec(memory_space=pltpu.SMEM)
 
 
-def run_kernel(kernel, micros, at, operands, outs, megabytes=16, scratch=()):
+def run_kernel(kernel, micros, at, operands, outs, megabytes=16, scratch=(), hbm_in=0, hbm_out=0):
     return pl.pallas_call(
         kernel,
         out_shape=[jax.ShapeDtypeStruct(shape, dtype) for shape, dtype in outs],
-        in_specs=[SCALARS] + [WHOLE] * len(operands),
-        out_specs=[WHOLE] * len(outs),
+        in_specs=[SCALARS] + [WHOLE] * (len(operands) - hbm_in) + [IN_HBM] * hbm_in,
+        out_specs=[WHOLE] * (len(outs) - hbm_out) + [IN_HBM] * hbm_out,
         scratch_shapes=scratch,
         cost_estimate=cost(micros),
         compiler_params=pltpu.CompilerParams(vmem_limit_bytes=megabytes * 2**20),
@@ -434,8 +435,11 @@
 
 
 def attend_kernel(at, tokens, gain, cosine, sine, *refs):
-    first_ref, query_ref, key_ref, value_ref, prob_ref, out_ref, weight = refs[8:]
+    first_ref, query_ref, key_ref, value_ref, out_ref = refs[8:13]
+    prob_out, weight_out, prob_ref, weight, sems = refs[13:]
     place_pieces(at, refs[:8], weight)
+    copies = [pltpu.make_async_copy(weight, weight_out, sems.at[HK])]
+    copies[0].start()
     length = tokens.shape[0]
     first_in = rms_kernel(tokens[...].astype(jnp.float32), gain[...])
     first_ref[...] = first_in
@@ -465,16 +469,26 @@
             prob = prob.astype(jnp.bfloat16)
             prob_ref[head] = prob
             out_ref[:, here] = dot(prob, value).astype(jnp.bfloat16)
+        here = pl.ds(group * group_size, group_size)
+        copies.append(
+            pltpu.make_async_copy(prob_ref.at[here], prob_out.at[here], sems.at[group])
+        )
+        copies[-1].start()
+    for copy in copies:
+        copy.wait()
 
 
 def project_kernel(at, tokens, gain, attended, *refs):
-    resid_ref, second_ref, weight = refs[8:]
+    resid_ref, second_ref, weight_out, weight, sem = refs[8:]
     place_pieces(at, refs[:8], weight)
+    copy = pltpu.make_async_copy(weight, weight_out, sem)
+    copy.start()
     heads = attended[...]
     halves = [dot(heads, weight[half].reshape(heads.shape[1], -1)) for half in range(2)]
     resid = tokens[...].astype(jnp.float32) + jnp.concatenate(halves, axis=1)
     resid_ref[...] = resid
     second_ref[...] = rms_kernel(resid, gain[...])
+    copy.wait()
 
 
 def one_hot(slots, capacity, dtype):
@@ -482,47 +496,74 @@
     return (slots == lax.broadcasted_iota(jnp.int32, shape, 0)).astype(jnp.float32).astype(dtype)
 
 
-def spread(slots, pieces, capacity, rows, outs):
+def slots_of(ids, expert, start, rows):
+    named = jnp.any(ids[:, start : start + rows] == expert, axis=0, keepdims=True)
+    named = named.astype(jnp.float32)
+    before = lax.broadcasted_iota(jnp.int32, (rows, rows), 0)
+    upto = lax.broadcasted_iota(jnp.int32, (rows, rows), 1)
+    counts = dot(named.astype(jnp.bfloat16), (before <= upto).astype(jnp.float32).astype(jnp.bfloat16))
+    return jnp.where(named > 0.0, counts - 1.0, -1.0).astype(jnp.int32)
+
+
+def spread(picks, capacity, rows, outs):
     rows = rows.astype(jnp.bfloat16)
-    block = slots.shape[1]
-    for n, piece in enumerate(pieces):
+    block = picks[0].shape[1]
+    for n in range(len(picks) // 2):
         for part in range(2):
-            pick = one_hot(slots[2 * piece + part : 2 * piece + part + 1], capacity, jnp.bfloat16)
+            pick = picks[2 * n + part]
             at_row = (2 * n + part) * capacity
             tokens = dot(pick, rows[at_row : at_row + capacity], ((0,), (0,)))
             outs[n][part * block : (part + 1) * block] = tokens.astype(jnp.bfloat16)
 
 
-def expert_kernel(capacity, pieces, at, slots, bias, router, gate_w, up_w, down_w, *refs):
+def expert_kernel(capacity, pieces, at, ids, ids_turned, router, *refs):
     count = len(pieces)
     second, cot = refs[:count], refs[count : 2 * count]
-    rows_in, rows_cot, gated_ref, gate_back, up_back, gates_ref = refs[2 * count : 2 * count + 6]
-    backs = refs[2 * count + 6 : -1]
-    gate_rows = refs[-1]
+    sources = refs[2 * count : 2 * count + 3]
+    rows_in, rows_cot, gated_ref, gate_back, up_back, gates_ref = refs[2 * count + 3 : 2 * count + 9]
+    backs = refs[2 * count + 9 : -5]
+    gate_w, up_w, down_w, gate_rows, sems = refs[-5:]
+    copies = [
+        pltpu.make_async_copy(source.at[at[6]], target, sems.at[n])
+        for n, (source, target) in enumerate(zip(sources, (gate_w, up_w, down_w)))
+    ]
+    for copy in copies:
+        copy.start()
     f32, bf16 = jnp.float32, jnp.bfloat16
-    length = second[0].shape[0]
+    length, width = second[0].shape
+    wide = router.shape[1]
     half = length // 2
+    picks = []
     for n, piece in enumerate(pieces):
         tokens = second[n][...]
-        logits = dot(tokens, router[...]) + bias[piece * length : (piece + 1) * length]
+        experts = lax.broadcasted_iota(jnp.int32, (length, wide), 1)
+        named = ids[piece * length : (piece + 1) * length]
+        chosen = functools.reduce(
+            jnp.logical_or, [named[:, k : k + 1] == experts for k in range(named.shape[1])]
+        )
+        logits = jnp.where(chosen, dot(tokens, router[...]), -1e30)
         weights = jnp.exp(logits - jnp.max(logits, axis=-1, keepdims=True))
         gates = weights * (1.0 / jnp.sum(weights, axis=-1, keepdims=True))
         if n == 0:
             gates_ref[...] = gates
-        lanes = lax.broadcasted_iota(jnp.int32, (capacity, gates.shape[1]), 1)
+        lanes = lax.broadcasted_iota(jnp.int32, (capacity, wide), 1)
         for part in range(2):
-            block = 2 * piece + part
             here = slice(part * half, (part + 1) * half)
             place = slice((2 * n + part) * capacity, (2 * n + part + 1) * capacity)
-            pick = one_hot(slots[block : block + 1], capacity, f32)
-            rows_in[place] = dot(pick.astype(bf16), tokens[here]).astype(bf16)
-            rows_cot[place] = dot(pick.astype(bf16), cot[n][here]).astype(bf16)
+            slots = slots_of(ids_turned, at[5], piece * length + part * half, half)
+            pick = one_hot(slots, capacity, f32)
+            picks.append(pick.astype(bf16))
+            rows_in[place] = dot(picks[-1], tokens[here]).astype(bf16)
+            rows_cot[place] = dot(picks[-1], cot[n][here]).astype(bf16)
             picked = dot(pick, gates[here], precision=lax.Precision.HIGHEST)
             picked = jnp.where(lanes == at[5], picked, 0.0)
             gate_rows[place] = jnp.sum(picked, axis=1, keepdims=True)
     gate = gate_rows[...]
+    copies[0].wait()
     gate_pre = dot(rows_in[...], gate_w[...])
+    copies[1].wait()
     up_pre = dot(rows_in[...], up_w[...])
+    copies[2].wait()
     cot_hidden = dot(rows_cot[...], down_w[...], ((1,), (1,)))
     scale = math.sqrt(2.0 / math.pi)
     square = gate_pre * gate_pre
@@ -540,55 +581,72 @@
     up_back[...] = (back * active).astype(bf16)
     high = signal.astype(bf16)
     low = (signal - high.astype(f32)).astype(bf16)
-    lanes = lax.broadcasted_iota(jnp.int32, (signal.shape[0], bias.shape[1]), 1)
+    lanes = lax.broadcasted_iota(jnp.int32, (signal.shape[0], wide), 1)
     signal = jnp.where(lanes == at[5], high.astype(f32), 0.0)
-    signal = jnp.where(lanes == at[5] + bias.shape[1] // 2, low.astype(f32), signal)
+    signal = jnp.where(lanes == at[5] + wide // 2, low.astype(f32), signal)
     by_rows = ((1,), (1,))
     rows = dot(gate_back[...], gate_w[...], by_rows) + dot(up_back[...], up_w[...], by_rows)
-    spread(slots, pieces, capacity, jnp.concatenate([rows, signal], axis=1), backs)
-
-
-def run_expert(pieces, at, slots, bias, router, weights, second, cot, capacity):
+    spread(picks, capacity, jnp.concatenate([rows, signal], axis=1), backs)
+
+
+def run_expert(pieces, at, ids, ids_turned, router, weights, second, cot, capacity):
     count = len(pieces)
-    rows = 2 * count * capacity
-    (length, width), hidden = second[0].shape, weights[0].shape[1]
+    rows, wide = 2 * count * capacity, router.shape[1]
+    (length, width), hidden = second[0].shape, weights[0].shape[2]
     bf16, f32 = jnp.bfloat16, jnp.float32
     outs = [(rows, width)] * 2 + [(rows, hidden)] * 3
-    outs = [(shape, bf16) for shape in outs] + [((length, bias.shape[1]), f32)]
-    outs = outs + [((length, width + bias.shape[1]), bf16)] * count
+    outs = [(shape, bf16) for shape in outs] + [((length, wide), f32)]
+    outs = outs + [((length, width + wide), bf16)] * count
     return run_kernel(
         functools.partial(expert_kernel, capacity, pieces),
         4 * count,
         at,
-        (slots, bias, router, *weights, *second, *cot),
+        (ids, ids_turned, router, *second, *cot, *weights),
         outs,
-        8 + 6 * count,
-        [pltpu.VMEM((rows, 1), f32)],
-    )
-
-
-def mixture_kernel(capacity, groups, at, slots, down_w, *refs):
-    outs = refs[len(groups) :]
-    for pieces, gated in zip(groups, refs):
-        rows = dot(gated[...], down_w[...])
-        spread(slots, pieces, capacity, rows, [outs[piece] for piece in pieces])
+        15 + 6 * count,
+        [pltpu.VMEM(weight.shape[1:], bf16) for weight in weights]
+        + [pltpu.VMEM((rows, 1), f32), pltpu.SemaphoreType.DMA((3,))],
+        hbm_in=3,
+    )
+
+
+def mixture_kernel(capacity, groups, at, ids_turned, *refs):
+    gated, source, down_w, sem = refs[: len(groups)], refs[len(groups)], refs[-2], refs[-1]
+    outs = refs[len(groups) + 1 : -2]
+    copy = pltpu.make_async_copy(source.at[at[6]], down_w, sem)
+    copy.start()
+    copy.wait()
+    length = outs[0].shape[0]
+    for pieces, rows in zip(groups, gated):
+        picks = []
+        for piece in pieces:
+            for part in range(2):
+                start = piece * length + part * length // 2
+                slots = slots_of(ids_turned, at[5], start, length // 2)
+                picks.append(one_hot(slots, capacity, jnp.bfloat16))
+        spread(picks, capacity, dot(rows[...], down_w[...]), [outs[piece] for piece in pieces])
 
 
 def row_sum_kernel(parts, at, *refs):
     arrays = [
         jnp.concatenate([ref[...] for ref in refs[n : n + parts]], axis=0)
-        for n in range(0, len(refs) - len(refs) // (parts + 1), parts)
+        for n in range(0, len(refs) - 1, parts)
     ]
-    outs = refs[len(arrays) * parts :]
-    for out, right in zip(outs, arrays[1:]):
-        out[...] = dot(arrays[0], right, ((0,), (0,))).astype(jnp.bfloat16)
-
-
-def row_sums(at, left, *rights):
+    out = refs[-1]
+    rows = out.shape[2]
+    for n, right in enumerate(arrays[1:]):
+        total = dot(arrays[0], right, ((0,), (0,))).astype(jnp.bfloat16)
+        for owner in range(out.shape[0]):
+            out[owner, n] = total[owner * rows : (owner + 1) * rows]
+
+
+def row_sums(at, shard_rows, left, *rights):
     operands = [part for parts in (left, *rights) for part in parts]
-    outs = [((left[0].shape[1], right[0].shape[1]), jnp.bfloat16) for right in rights]
+    rows, cols = left[0].shape[1], rights[0][0].shape[1]
+    shape = (rows // shard_rows, len(rights), shard_rows, cols)
     kernel = functools.partial(row_sum_kernel, len(left))
-    return run_kernel(kernel, 6 * len(rights), at, operands, outs, 24)
+    (total,) = run_kernel(kernel, 4 * len(rights), at, operands, [(shape, jnp.bfloat16)], 24)
+    return total
 
 
 def branch_back_kernel(
@@ -749,42 +807,29 @@
     narrow = small_group_gather(narrow)
     ids_all = small_gather(expert_ids)
     column = [own_half] + shifts(own_half)
-    cot_sides = plane_sides(out_grad)
-    cot_corner = plane_corner(cot_sides)
-    gate_w, up_w, down_w = (
-        lax.dynamic_index_in_dim(weight, own_local, 0, keepdims=False)
-        for weight in (w_gate, w_up, w_down)
-    )
+    cot_sides = plane_sides(after(out_grad, narrow, ids_all))
     qkv_half = qkv_cols // 2
     qkv_column = jnp.stack([part[:, :qkv_half] for part in column])
     out_column = jnp.stack([part[:, qkv_half:] for part in column])
-    qkv_column, out_column, narrow, ids_all, cot_corner, gate_w, up_w, down_w = (
-        lax.optimization_barrier(
-            (qkv_column, out_column, narrow, ids_all, cot_corner, gate_w, up_w, down_w)
-        )
-    )
+    qkv_column, out_column = lax.optimization_barrier((qkv_column, out_column, *cot_sides))[:2]
     qkv_sides = plane_sides(qkv_column)
     qkv_corner = plane_corner(qkv_sides)
     out_sides = plane_sides(after(out_column, qkv_corner))
     qkv_pieces = plane_pieces(qkv_column, qkv_sides, qkv_corner)
-    cot_pieces = plane_pieces(out_grad, cot_sides, cot_corner)
     router_w = jnp.pad(narrow[:, :experts_all], ((0, 0), (0, 128 - experts_all)))
     gains = narrow[:, experts_all : experts_all + 2].T.astype(f32)
     gain_one, gain_two = gains[:1], gains[1:]
 
-    expert_range = jnp.arange(128, dtype=jnp.int32)
-    chosen_mask = jnp.any(ids_all[:, :, None] == expert_range[None, None, :], axis=1)
-    bias = jnp.where(chosen_mask, 0.0, -1e30).astype(f32)
-    own_mask = jnp.any(ids_all == own_expert, axis=1).reshape(blocks, block_rows)
-    place = jnp.cumsum(own_mask.astype(jnp.int32), axis=1) - 1
-    slots = jnp.where(own_mask, place, -1)
-    gain_one, bias, slots, router_w = lax.optimization_barrier((gain_one, bias, slots, router_w))
+    ids_turned = ids_all.T
+    gain_one, ids_all, ids_turned, router_w = lax.optimization_barrier(
+        (gain_one, ids_all, ids_turned, router_w)
+    )
 
     cosine_tab, sine_tab = angles(length, HD)
     cosine_all = jnp.concatenate([cosine_tab, cosine_tab], axis=2)[:, 0]
     sine_all = jnp.concatenate([-sine_tab, sine_tab], axis=2)[:, 0]
     weight_lead = (2, depth, 2, 2, shard_rows)
-    first_in, queries, keys_rot, values_b, probs, attended, qkv_w = run_kernel(
+    first_in, queries, keys_rot, values_b, attended, probs, qkv_w = run_kernel(
         attend_kernel,
         11,
         at,
@@ -794,24 +839,36 @@
             ((length, q_cols), bf16),
             ((length, kv_cols), bf16),
             ((length, kv_cols), bf16),
+            ((length, q_cols), bf16),
             ((HQ, length, length), bf16),
-            ((length, q_cols), bf16),
             (weight_lead + (qkv_half,), bf16),
         ],
+        28,
+        [
+            pltpu.VMEM((HQ, length, length), bf16),
+            pltpu.VMEM(weight_lead + (qkv_half,), bf16),
+            pltpu.SemaphoreType.DMA((HK + 1,)),
+        ],
+        hbm_out=2,
     )
     out_sides = lax.optimization_barrier((*out_sides, attended))[:2]
     out_corner = plane_corner(out_sides)
+    cot_corner = plane_corner(cot_sides, (out_corner,))
     out_pieces = plane_pieces(out_column, out_sides, out_corner)
+    cot_pieces = plane_pieces(out_grad, cot_sides, cot_corner)
     resid, second_in, output_w = run_kernel(
         project_kernel,
         4,
         at,
-        (tokens, gain_two, attended, *out_pieces),
+        (tokens, after(gain_two, cot_corner), attended, *out_pieces),
         [
             ((length, model_width), f32),
             ((length, model_width), bf16),
             (weight_lead + (out_half,), bf16),
         ],
+        20,
+        [pltpu.VMEM(weight_lead + (out_half,), bf16), pltpu.SemaphoreType.DMA],
+        hbm_out=1,
     )
     qkv_w = qkv_w.reshape(HK, model_width, qkv_half)
     output_w = output_w.reshape(2, q_cols, out_half)
@@ -819,10 +876,10 @@
     expert = functools.partial(
         run_expert,
         at=at,
-        slots=slots,
-        bias=bias,
+        ids=ids_all,
+        ids_turned=ids_turned,
         router=router_w,
-        weights=(gate_w, up_w, down_w),
+        weights=(w_gate, w_up, w_down),
         capacity=capacity,
     )
     second_sides = plane_sides(second_in)
@@ -855,16 +912,15 @@
     stages = (stage_own, stage_sides, stage_corner)
     rows_in, rows_cot, gated, gate_back, up_back = ([stage[n] for stage in stages] for n in range(5))
     gates = stage_own[5]
-    (down_part,) = row_sums(at, [after(rows_cot[0], corner)] + rows_cot[1:], gated)
+    down_part = row_sums(at, shard_rows, [after(rows_cot[0], corner)] + rows_cot[1:], gated)
     down_sum = scatter_sum(down_part, "z")
     passed = lax.optimization_barrier((*passed, down_part))[:2]
     last_y, last_x, sent = corner_last(back_x, back_y, passed)
-    gate_part, up_part = row_sums(
-        at, [after(rows_in[0], sent)] + rows_in[1:], gate_back, up_back
-    )
-    gate_sum = scatter_sum(after(gate_part, down_sum), "z")
-    up_sum = scatter_sum(after(up_part, gate_sum), "z")
-    own_near = after(own_near, gate_part)
+    gate_up_part = row_sums(
+        at, shard_rows, [after(rows_in[0], sent)] + rows_in[1:], gate_back, up_back
+    )
+    gate_up_sum = scatter_sum(gate_up_part, "z")
+    own_near = after(own_near, gate_up_part)
 
     resid_grad, branch_grad, attended_grad, router_acc, gain_two_grad = run_kernel(
         branch_back_kernel,
@@ -923,7 +979,7 @@
     both = jnp.concatenate(
         lax.optimization_barrier((attended, first_in, resid_grad))[:2], axis=0
     )
-    both_pieces = plane_pieces(both)
+    both_sides = plane_sides(both)
     narrow_part = jnp.concatenate(
         [router_acc[:, :experts_all], gain_one_grad.T, gain_two_grad.T], axis=1
     )
@@ -940,14 +996,15 @@
         narrow_part, ((0, 0), (0, 0), (0, each_rows * dense_cols - narrow_len))
     ).reshape(plane, depth * each_rows, dense_cols)
     back_cols = exchange(jnp.concatenate([back_cols, narrow_part.astype(bf16)], axis=1), PLANE)
+    both_corner = plane_corner(both_sides, (back_cols,))
+    both_pieces = plane_pieces(both, both_sides, both_corner)
     kept_rows = -(-narrow_rows // 16) * 16
     wide_rows = local_count * shard_rows
     dense_shape = (depth, wide_rows + kept_rows, dense_cols)
-    anywhere = pl.BlockSpec(memory_space=pl.ANY)
     dense_part = pl.pallas_call(
         dense_grad_kernel,
         out_shape=jax.ShapeDtypeStruct(dense_shape, bf16),
-        in_specs=[SCALARS, WHOLE] + [anywhere] * 8,
+        in_specs=[SCALARS, WHOLE] + [IN_HBM] * 8,
         out_specs=WHOLE,
         scratch_shapes=[
             pltpu.VMEM((plane, 2 * length, model_width), bf16),
@@ -956,7 +1013,6 @@
         cost_estimate=cost(8),
         compiler_params=pltpu.CompilerParams(vmem_limit_bytes=32 * 2**20),
     )(at, back_cols, *both_pieces)
-    dense_part = after(dense_part, up_sum)
     dense_sum = scatter_sum(dense_part.reshape(-1, dense_cols), "z")
     wide_sum = dense_sum[: local_count * shard_rows].reshape(2, 2, 1, shard_rows, dense_cols)
     wide_sum = jnp.broadcast_to(wide_sum, (2, 2, owners, shard_rows, dense_cols)).reshape(
@@ -980,9 +1036,11 @@
         functools.partial(mixture_kernel, capacity, groups),
         10,
         at,
-        (slots, down_w, after(gated[0], both_pieces[3]), *gated[1:]),
+        (ids_turned, after(gated[0], both_corner), *gated[1:], w_down),
         [((length, model_width), bf16)] * plane,
         24,
+        [pltpu.VMEM(w_down.shape[1:], bf16), pltpu.SemaphoreType.DMA],
+        hbm_in=1,
     )
     mixed = [over_core(near, far) for near, far in zip(shares[:4], shares[4:])]
     early = early_sums(mixed[1], mixed[2])
@@ -992,9 +1050,8 @@
     )
     block_out = (resid + (mixture + mixed[0].astype(f32))).astype(bf16)
 
-    def placed(total):
-        total = exchange(total, ("y", "c"))
-        return total.reshape(local_count, shard_rows, hidden_width).astype(f32)
+    down_grad = exchange(down_sum, ("y", "c"))[:, 0].astype(f32)
+    gate_up_grad = exchange(gate_up_sum, ("y", "c")).astype(f32)
 
     return (
         block_out,
@@ -1006,9 +1063,9 @@
         output_sum,
         narrow_sum[:, experts_all + 1],
         narrow_sum[:, :experts_all],
-        placed(gate_sum),
-        placed(up_sum),
-        jnp.swapaxes(placed(down_sum), 1, 2),
+        gate_up_grad[:, 0],
+        gate_up_grad[:, 1],
+        jnp.swapaxes(down_grad, 1, 2),
     )
 
 

time: 547 us -> 558 us (1.020)
  other arithmetic: 34.7 us -> 18.4 us
  waiting for transfers between devices: 235 us -> 250 us
  Pallas kernels: 87.6 us -> 100 us
  starting transfers between devices: 74.1 us -> 67.7 us
    all_to_all x5 -> x4, waiting for transfers between devices: 47.8 us -> 18.2 us  [exchange(): return lax.all_to_all(block, axes, split_axis=0, concat_axis=0, tiled=True)]
    reduce_scatter x4 -> x3, waiting for transfers between devices: 16.5 us -> 44.1 us  [scatter_sum(): return lax.psum_scatter(block, axes, scatter_dimension=0, tiled=True)]
    ppermute x6, waiting for transfers between devices: 0.02 us -> 20.2 us  [shifts(): lax.ppermute(block, 'z', [(i, (i + k) % depth) for i in range(depth)])]
    unnamed x247 -> x229, local copies, waits for them, and re-layouts: 50.2 us -> 65.5 us
    pallas_call x11, Pallas kernels: 81.7 us -> 93.1 us  [run_kernel(): pl.pallas_call(kernel, out_shape=[jax.ShapeDtypeStruct(shape, dtype) for...]
    squeeze x2 -> x1, local copies, waits for them, and re-layouts: 7.56 us -> 1.56 us  [local_pairs(): gate_up_grad[:, 1]]
    all_to_all x5 -> x4, starting transfers between devices: 17.8 us -> 15.5 us  [exchange(): return lax.all_to_all(block, axes, split_axis=0, concat_axis=0, tiled=True)]
  transfers between devices with their start and end apart: 80 -> 78, of which waited for: 37 -> 32; matrix products, arithmetic and copies ran while one was open for 13% -> 8% of each run, Pallas kernels for 14% -> 16%
where the time goes in v3:
time: 558 us; the launch traced here: 547 us
  waiting for transfers between devices  250 us (45%)
  Pallas kernels  100 us (18%)
  local copies, waits for them, and re-layouts  94.2 us (17%)
  starting transfers between devices  67.7 us (12%)
  other arithmetic  18.4 us (3%)
  between operations  16.4 us (3%)
    ppermute x65, waiting for transfers between devices, swap(): return lax.ppermute(block, axis, [(0, 1), (1, 0)])  167 us
    pallas_call x11, Pallas kernels, run_kernel(): pl.pallas_call(kernel, out_shape=[jax.ShapeDtypeStruct(shape, dtype) for...  93.1 us
    unnamed x229, local copies, waits for them, and re-layouts  65.5 us
    reduce_scatter x3, waiting for transfers between devices, scatter_sum(): return lax.psum_scatter(block, axes, scatter_dimension=0, tiled=True)  44.1 us
    ppermute x65, starting transfers between devices, swap(): return lax.ppermute(block, axis, [(0, 1), (1, 0)])  41.9 us
    ppermute x6, waiting for transfers between devices, shifts(): lax.ppermute(block, 'z', [(i, (i + k) % depth) for i in range(depth)])  20.2 us
    all_to_all x4, waiting for transfers between devices, exchange(): return lax.all_to_all(block, axes, split_axis=0, concat_axis=0, tiled=True)  18.2 us
    all_to_all x4, starting transfers between devices, exchange(): return lax.all_to_all(block, axes, split_axis=0, concat_axis=0, tiled=True)  15.5 us
  transfers between devices with their start and end apart: 78, of which 32 were waited for; matrix products, arithmetic and copies ran while one was open for 8% of the time, Pallas kernels for 16%

profile of v3, /device:TPU:0, one launch (start us, length us, event | category | flops | bytes accessed | tf_op | source)
XLA Modules:
  0.0 547.4 jit_solution(16837518878241499069)
XLA Ops:
  8.0 5.1 collective-permute-start
  17.4 2.9 collective-permute-start.12
  30.0 20.2 %collective-permute-done.11 = bf16[96,1792]{1,0:T(8,128)(2,1)S(1)} collective-permute-done((bf16[96,1792]{1,0:T(8,128)(2,1)S(1)}, bf16[96,1792]{1,0:T(8,128)(2,1)S(1)}, u32[]{:S(2)}, u32[]{:S(2)}) %collective-permute-start.11) | collective-permute-done | bytes 344096 | tf_op jit(solution)/shard_map/ppermute | solution.py:317
  55.5 15.2 %collective-permute-done.13.refs_2_ = bf16[4,96,1024]{2,1,0:T(8,128)(2,1)S(1)} collective-permute-done((bf16[4,96,1024]{2,1,0:T(8,128)(2,1)S(1)}, bf16[4,96,1024]{2,1,0:T(8,128)(2,1)S(1)}, u32[]{:S(2)}, u32[]{:S(2)}) %collective-permute-start.13) | collective-permute-done | bytes 786464 | tf_op jit(solution)/shard_map/ppermute | solution.py:311
  77.6 4.3 collective-permute-done.15
  85.9 7.4 %shard_map.229 = (bf16[256,1536]{1,0:T(8,128)(2,1)S(1)}, bf16[256,1536]{1,0:T(8,128)(2,1)S(1)}, bf16[256,256]{1,0:T(8,128)(2,1)S(1)}, bf16[256,256]{1,0:T(8,128)...) custom-call(s32[7]{0:T(128)S(1)} %stack.76.at, ...), custom_call_target="tpu_custom_call" | custom-call | flops 11000000512 | bytes 11000000 | tf_op jit(solution)/shard_map/pallas_call | solution.py:399
  93.3 2.7 copy-done.71
  102.1 6.7 %collective-permute-done.23 = bf16[2,96,768]{2,1,0:T(8,128)(2,1)S(1)} collective-permute-done((bf16[2,96,768]{2,1,0:T(8,128)(2,1)S(1)}, bf16[2,96,768]{2,1,0:T(8,128)(2,1)S(1)}, u32[]{:S(2)}, u32[]{:S(2)}) %collective-permute-start.23) | collective-permute-done | bytes 294944 | tf_op jit(solution)/shard_map/ppermute | solution.py:311
  112.1 6.3 %collective-permute-done.25 = bf16[128,1536]{1,0:T(8,128)(2,1)S(1)} collective-permute-done((bf16[128,1536]{1,0:T(8,128)(2,1)S(1)}, bf16[128,1536]{1,0:T(8,128)(2,1)S(1)}, u32[]{:S(2)}, u32[]{:S(2)}) %collective-permute-start.25) | collective-permute-done | bytes 393248 | tf_op jit(solution)/shard_map/ppermute | solution.py:311
  120.6 2.8 shard_map.230
  124.5 2.2 copy-done.72
  129.8 3.7 copy-done
  133.4 12.3 %shard_map.231 = (bf16[384,1536]{1,0:T(8,128)(2,1)S(1)}, bf16[384,1536]{1,0:T(8,128)(2,1)S(1)}, bf16[384,768]{1,0:T(8,128)(2,1)S(1)}, bf16[384,768]{1,0:T(8,128)...) custom-call(s32[7]{0:T(128)S(1)} %stack.76.at, ...), custom_call_target="tpu_custom_call" | custom-call | flops 8000000000 | bytes 8000000 | tf_op jit(solution)/shard_map/pallas_call | solution.py:399
  154.0 9.0 %collective-permute-done.40 = bf16[128,1536]{1,0:T(8,128)(2,1)S(1)} collective-permute-done((bf16[128,1536]{1,0:T(8,128)(2,1)S(1)}, bf16[128,1536]{1,0:T(8,128)(2,1)S(1)}, u32[]{:S(2)}, u32[]{:S(2)}) %collective-permute-start.40) | collective-permute-done | bytes 393248 | tf_op jit(solution)/shard_map/ppermute | solution.py:311
  164.0 9.1 %collective-permute-done.41 = bf16[128,1536]{1,0:T(8,128)(2,1)S(1)} collective-permute-done((bf16[128,1536]{1,0:T(8,128)(2,1)S(1)}, bf16[128,1536]{1,0:T(8,128)(2,1)S(1)}, u32[]{:S(2)}, u32[]{:S(2)}) %collective-permute-start.41) | collective-permute-done | bytes 393248 | tf_op jit(solution)/shard_map/ppermute | solution.py:311
  181.5 23.3 %shard_map.232 = (bf16[768,1536]{1,0:T(8,128)(2,1)}, bf16[768,1536]{1,0:T(8,128)(2,1)}, bf16[768,768]{1,0:T(8,128)(2,1)S(1)}, bf16[768,768]{1,0:T(8,128)(2,1)S(1...) custom-call(s32[7]{0:T(128)S(1)} %stack.76.at, ...), custom_call_target="tpu_custom_call" | custom-call | flops 16000000000 | bytes 16000000 | tf_op jit(solution)/shard_map/pallas_call | solution.py:399
  208.5 2.9 collective-permute-done.42.refs_1_
  211.4 11.7 %shard_map.233 = (bf16[384,1536]{1,0:T(8,128)(2,1)S(1)}, bf16[384,1536]{1,0:T(8,128)(2,1)S(1)}, bf16[384,768]{1,0:T(8,128)(2,1)S(1)}, bf16[384,768]{1,0:T(8,128)...) custom-call(s32[7]{0:T(128)S(1)} %stack.76.at, ...), custom_call_target="tpu_custom_call" | custom-call | flops 8000000000 | bytes 8000000 | tf_op jit(solution)/shard_map/pallas_call | solution.py:399
  231.3 6.0 %shard_map.234 = bf16[16,1,96,768]{3,2,1,0:T(8,128)(2,1)} custom-call(s32[7]{0:T(128)S(1)} %stack.76.at, bf16[384,1536]{1,0:T(8,128)(2,1)S(1)} %copy-done.36, bf16[768,1536]{1,0:T(8,128)(2,1)S(1)} %copy-done.74, bf16[384,1536]{1,0:T(8,128)(2,1)S(1)} %get-tuple-element.130.refs_2_, bf16[384,768]{1,0:T(8,128)(2,1)S(1)} %copy-done.57, ...), custom_call_target="tpu_custom_call" | custom-call | flops 4000000000 | bytes 4000000 | tf_op jit(solution)/shard_map/pallas_call | solution.py:399
  237.4 2.8 collective-permute-done.45
  240.2 6.2 %collective-permute-done.46 = bf16[128,1664]{1,0:T(8,128)(2,1)S(1)} collective-permute-done((bf16[128,1664]{1,0:T(8,128)(2,1)S(1)}, bf16[128,1664]{1,0:T(8,128)(2,1)S(1)}, u32[]{:S(2)}, u32[]{:S(2)}) %collective-permute-start.46) | collective-permute-done | bytes 426016 | tf_op jit(solution)/shard_map/ppermute | solution.py:311
  261.2 8.1 %shard_map.235 = bf16[16,2,96,768]{3,2,1,0:T(8,128)(2,1)S(1)} custom-call(s32[7]{0:T(128)S(1)} %stack.76.at, bf16[384,1536]{1,0:T(8,128)(2,1)S(1)} %copy-done.34, bf16[768,1536]{1,0:T(8,128)(2,1)S(1)} %copy-done.78, bf16[384,1536]{1,0:T(8,128)(2,1)S(1)} %copy-done.38, bf16[384,768]{1,0:T(8,128)(2,1)S(1)} %copy-done.62, bf16[768,768]{1,0:T(8,128)(2,1)S(1)} %copy-done.82, ...), custom_call_target="tpu_custom_call" | custom-call | flops 8000000000 | bytes 8000000 | tf_op jit(solution)/shard_map/pallas_call | solution.py:399
  269.3 2.1 copy-done.2
  274.9 2.3 copy-done.73
  277.2 4.7 shard_map.236
  282.0 5.4 shard_map.237.back
  287.5 3.8 shard_map.238
  295.0 3.6 all-to-all-start
  298.6 2.2 constant_dynamic-update-slice_fusion.19
  301.8 1.9 collective-permute-start.53
  305.2 54.2 %collective-permute-done.53.refs_2_ = bf16[512,1536]{1,0:T(8,128)(2,1)} collective-permute-done((bf16[512,1536]{1,0:T(8,128)(2,1)}, bf16[512,1536]{1,0:T(8,128)(2,1)}, u32[]{:S(2)}, u32[]{:S(2)}) %collective-permute-start.53) | collective-permute-done | bytes 1572896 | tf_op jit(solution)/shard_map/ppermute | solution.py:311
  359.4 2.1 slice.213
  365.3 16.8 %collective-permute-done.55 = bf16[256,1536]{1,0:T(8,128)(2,1)S(1)} collective-permute-done((bf16[256,1536]{1,0:T(8,128)(2,1)}, bf16[256,1536]{1,0:T(8,128)(2,1)S(1)}, u32[]{:S(2)}, u32[]{:S(2)}) %collective-permute-start.55) | collective-permute-done | bytes 786464 | tf_op jit(solution)/shard_map/ppermute | solution.py:311
  383.2 3.4 collective-permute-done.70.refs_7_
  386.5 7.3 %shard_map.240 = bf16[4,400,448]{2,1,0:T(8,128)(2,1)S(1)} custom-call(s32[7]{0:T(128)S(1)} %copy-done.32, bf16[8,272,448]{2,1,0:T(8,128)(2,1)S(1)} %all-to-all-done.back, bf16[512,1536]{1,0:T(8,128)(2,1)} %constant_dynamic-update-slice_fusion.18.refs_0_, bf16[512,1536]{1,0:T(8,128)(2,1)} %collective-permute-done.54.refs_1_, ...), custom_call_target="tpu_custom_call" | custom-call | flops 8000000000 | bytes 8000000 | tf_op jit(solution)/shard_map/pallas_call | solution.py:1004
  395.8 3.7 copy-done.1
  403.0 7.5 %shard_map.239 = (bf16[256,1536]{1,0:T(8,128)(2,1)S(1)}, bf16[256,1536]{1,0:T(8,128)(2,1)S(1)}, bf16[256,1536]{1,0:T(8,128)(2,1)S(1)}, bf16[256,1536]{1,0:T(8,12...) custom-call(s32[7]{0:T(128)S(1)} %copy-done.32, ...), custom_call_target="tpu_custom_call" | custom-call | flops 10000000000 | bytes 10000000 | tf_op jit(solution)/shard_map/pallas_call | solution.py:399
  422.8 6.4 %collective-permute-done.61 = bf16[128,1536]{1,0:T(8,128)(2,1)S(1)} collective-permute-done((bf16[128,1536]{1,0:T(8,128)(2,1)S(1)}, bf16[128,1536]{1,0:T(8,128)(2,1)S(1)}, u32[]{:S(2)}, u32[]{:S(2)}) %collective-permute-start.61) | collective-permute-done | bytes 393248 | tf_op jit(solution)/shard_map/ppermute | solution.py:311
  430.0 11.2 %collective-permute-done.64 = bf16[128,1536]{1,0:T(8,128)(2,1)S(1)} collective-permute-done((bf16[128,1536]{1,0:T(8,128)(2,1)S(1)}, bf16[128,1536]{1,0:T(8,128)(2,1)S(1)}, u32[]{:S(2)}, u32[]{:S(2)}) %collective-permute-start.64) | collective-permute-done | bytes 393248 | tf_op jit(solution)/shard_map/ppermute | solution.py:311
  443.6 4.2 all-to-all-start.3
  452.0 5.4 all-to-all-done.3
  457.4 4.2 all-to-all-start.1
  462.9 2.5 fusion.1
  465.4 9.8 %all-to-all-done.1 = bf16[8,112,448]{2,1,0:T(8,128)(2,1)} async-done(((bf16[8,112,448]{2,1,0:T(8,128)(2,1)}), bf16[8,112,448]{2,1,0:T(8,128)(2,1)}, u32[]{:S(2)}, u32[]{:S(2)}) %all-to-all-start.1) | async-done | bytes 802848 | tf_op jit(solution)/shard_map/all_to_all | solution.py:61
  475.2 44.1 %reduce-scatter.6.cloned.1.call-done = bf16[4,2,96,768]{3,2,1,0:T(8,128)(2,1)} async-done(((bf16[16,2,96,768]{3,2,1,0:T(8,128)(2,1)}), bf16[4,2,96,768]{3,2,1,0:T(8,128)(2,1)}) %reduce-scatter.6.cloned.1.call-update) | async-done | bytes 1179664 | tf_op jit(solution)/shard_map/reduce_scatter | solution.py:65
  519.3 3.5 all-to-all-start.2
  522.8 2.2 convert_bitcast_fusion.1
  535.5 3.1 all-to-all-done.2
  (464 shorter events, 142.6 us)
Async XLA Ops:
  8.0 12.3 %collective-permute-start = (bf16[96,10]{0,1:T(8,128)(2,1)S(1)}, bf16[96,10]{0,1:T(8,128)(2,1)S(1)}, u32[]{:S(2)}, u32[]{:S(2)}) collective-permute-start(bf16[96,10]{0,1:T(8,128)(2,1)S(1)} %pad_maximum_fusion.8), channel_id=1, source_target_pairs={{0,24},{8,0},{16,8},{24,16},{1,25},{9,1},{17,9},{25,17},{2,26},{10... | collective-permute-start | bytes 5768 | tf_op jit(solution)/shard_map/ppermute | solution.py:317
  17.4 11.9 %collective-permute-start.12 = (bf16[96,1792]{1,0:T(8,128)(2,1)S(1)}, bf16[96,1792]{1,0:T(8,128)(2,1)S(1)}, u32[]{:S(2)}, u32[]{:S(2)}) collective-permute-start(bf16[96,1792]{1,0:T(8,128)(2,1)S(1)} %pad_maximum_fusion.4), channel_id=1, source_target_pairs={{0,24},{8,0},{16,8},{24,16},{1,25},{9,1},{17,9},{25,17},{2,26},{10... | collective-permute-start | bytes 1032200 | tf_op jit(solution)/shard_map/ppermute | solution.py:317
  20.4 29.8 %collective-permute-start.11 = (bf16[96,1792]{1,0:T(8,128)(2,1)S(1)}, bf16[96,1792]{1,0:T(8,128)(2,1)S(1)}, u32[]{:S(2)}, u32[]{:S(2)}) collective-permute-start(bf16[96,1792]{1,0:T(8,128)(2,1)S(1)} %pad_maximum_fusion.4), channel_id=1, source_target_pairs={{0,16},{8,24},{16,0},{24,8},{1,17},{9,25},{17,1},{25,9},{2,18},{10... | collective-permute-start | bytes 1032200 | tf_op jit(solution)/shard_map/ppermute | solution.py:317
  21.5 28.7 %collective-permute-start.10 = (bf16[96,1792]{1,0:T(8,128)(2,1)S(1)}, bf16[96,1792]{1,0:T(8,128)(2,1)}, u32[]{:S(2)}, u32[]{:S(2)}) collective-permute-start(bf16[96,1792]{1,0:T(8,128)(2,1)S(1)} %pad_maximum_fusion.4), channel_id=1, source_target_pairs={{0,8},{8,16},{16,24},{24,0},{1,9},{9,17},{17,25},{25,1},{2,10},{10... | collective-permute-start | bytes 1032200 | tf_op jit(solution)/shard_map/ppermute | solution.py:317
  28.2 25.2 %collective-permute-start.8 = (bf16[256,1536]{1,0:T(8,128)(2,1)S(1)}, bf16[256,1536]{1,0:T(8,128)(2,1)S(1)}, u32[]{:S(2)}, u32[]{:S(2)}) collective-permute-start(bf16[256,1536]{1,0:T(8,128)(2,1)S(1)} %copy-done.10), channel_id=1, source_target_pairs={{0,4},{4,0},{1,5},{5,1},{2,6},{6,2},{3,7},{7,3},{8,12},{12,8},{9,1... | collective-permute-start | bytes 2359304 | tf_op jit(solution)/shard_map/ppermute | solution.py:311
  28.7 24.6 %collective-permute-start.9 = (bf16[256,1536]{1,0:T(8,128)(2,1)S(1)}, bf16[256,1536]{1,0:T(8,128)(2,1)S(1)}, u32[]{:S(2)}, u32[]{:S(2)}) collective-permute-start(bf16[256,1536]{1,0:T(8,128)(2,1)S(1)} %copy-done.10), channel_id=1, source_target_pairs={{0,1},{1,0},{2,3},{3,2},{4,5},{5,4},{6,7},{7,6},{8,9},{9,8},{10,11... | collective-permute-start | bytes 2359304 | tf_op jit(solution)/shard_map/ppermute | solution.py:311
  53.4 17.3 %collective-permute-start.13 = (bf16[4,96,1024]{2,1,0:T(8,128)(2,1)S(1)}, bf16[4,96,1024]{2,1,0:T(8,128)(2,1)S(1)}, u32[]{:S(2)}, u32[]{:S(2)}) collective-permute-start(bf16[4,96,1024]{2,1,0:T(8,128)(2,1)S(1)} %pad_maximum_fusion.1.refs_0_), channel_id=1, source_target_pairs={{0,4},{4,0},{1,5},{5,1},{2,6},{6,2},{3,7},{7,3},{8,12},{12,8},{9,1... | collective-permute-start | bytes 2359304 | tf_op jit(solution)/shard_map/ppermute | solution.py:311
  55.0 17.1 %collective-permute-start.14 = (bf16[4,96,1024]{2,1,0:T(8,128)(2,1)S(1)}, bf16[4,96,1024]{2,1,0:T(8,128)(2,1)}, u32[]{:S(2)}, u32[]{:S(2)}) collective-permute-start(bf16[4,96,1024]{2,1,0:T(8,128)(2,1)S(1)} %pad_maximum_fusion.1.refs_0_), channel_id=1, source_target_pairs={{0,1},{1,0},{2,3},{3,2},{4,5},{5,4},{6,7},{7,6},{8,9},{9,8},{10,11... | collective-permute-start | bytes 2359304 | tf_op jit(solution)/shard_map/ppermute | solution.py:311
  83.3 15.8 %collective-permute-start.17 = (bf16[4,96,768]{2,1,0:T(8,128)(2,1)S(1)}, bf16[4,96,768]{2,1,0:T(8,128)(2,1)S(1)}, u32[]{:S(2)}, u32[]{:S(2)}) collective-permute-start(bf16[4,96,768]{2,1,0:T(8,128)(2,1)S(1)} %pad_maximum_fusion.3.refs_0_), channel_id=1, source_target_pairs={{0,1},{1,0},{2,3},{3,2},{4,5},{5,4},{6,7},{7,6},{8,9},{9,8},{10,11... | collective-permute-start | bytes 1769480 | tf_op jit(solution)/shard_map/ppermute | solution.py:311
  84.9 15.4 %collective-permute-start.18 = (bf16[4,96,768]{2,1,0:T(8,128)(2,1)S(1)}, bf16[4,96,768]{2,1,0:T(8,128)(2,1)S(1)}, u32[]{:S(2)}, u32[]{:S(2)}) collective-permute-start(bf16[4,96,768]{2,1,0:T(8,128)(2,1)S(1)} %pad_maximum_fusion.3.refs_0_), channel_id=1, source_target_pairs={{0,4},{4,0},{1,5},{5,1},{2,6},{6,2},{3,7},{7,3},{8,12},{12,8},{9,1... | collective-permute-start | bytes 1769480 | tf_op jit(solution)/shard_map/ppermute | solution.py:311
  119.5 10.2 %collective-permute-start.32 = (bf16[256,1536]{1,0:T(8,128)(2,1)S(1)}, bf16[256,1536]{1,0:T(8,128)(2,1)}, u32[]{:S(2)}, u32[]{:S(2)}) collective-permute-start(bf16[256,1536]{1,0:T(8,128)(2,1)S(1)} %copy-done.10), channel_id=1, source_target_pairs={{0,2},{2,0},{1,3},{3,1},{4,6},{6,4},{5,7},{7,5},{8,10},{10,8},{9,1... | collective-permute-start | bytes 2359304 | tf_op jit(solution)/shard_map/ppermute | solution.py:311
  127.1 22.2 %collective-permute-start.33 = (bf16[256,1536]{1,0:T(8,128)(2,1)S(1)}, bf16[256,1536]{1,0:T(8,128)(2,1)}, u32[]{:S(2)}, u32[]{:S(2)}) collective-permute-start(bf16[256,1536]{1,0:T(8,128)(2,1)S(1)} %get-tuple-element.112.refs_0_.second), channel_id=1, source_target_pairs={{0,1},{1,0},{2,3},{3,2},{4,5},{5,4},{6,7},{7,6},{8,9},{9,8},{10,11... | collective-permute-start | bytes 2359304 | tf_op jit(solution)/shard_map/ppermute | solution.py:311
  128.1 21.1 %collective-permute-start.34 = (bf16[256,1536]{1,0:T(8,128)(2,1)S(1)}, bf16[256,1536]{1,0:T(8,128)(2,1)}, u32[]{:S(2)}, u32[]{:S(2)}) collective-permute-start(bf16[256,1536]{1,0:T(8,128)(2,1)S(1)} %get-tuple-element.112.refs_0_.second), channel_id=1, source_target_pairs={{0,4},{4,0},{1,5},{5,1},{2,6},{6,2},{3,7},{7,3},{8,12},{12,8},{9,1... | collective-permute-start | bytes 2359304 | tf_op jit(solution)/shard_map/ppermute | solution.py:311
  152.0 11.0 %collective-permute-start.40 = (bf16[128,1536]{1,0:T(8,128)(2,1)S(1)}, bf16[128,1536]{1,0:T(8,128)(2,1)S(1)}, u32[]{:S(2)}, u32[]{:S(2)}) collective-permute-start(bf16[128,1536]{1,0:T(8,128)(2,1)S(1)} %slice.163), channel_id=1, source_target_pairs={{0,1},{1,0},{2,3},{3,2},{4,5},{5,4},{6,7},{7,6},{8,9},{9,8},{10,11... | collective-permute-start | bytes 1179656 | tf_op jit(solution)/shard_map/ppermute | solution.py:311
  153.0 20.3 %collective-permute-start.37 = (bf16[256,1536]{1,0:T(8,128)(2,1)S(1)}, bf16[256,1536]{1,0:T(8,128)(2,1)S(1)}, u32[]{:S(2)}, u32[]{:S(2)}) collective-permute-start(bf16[256,1536]{1,0:T(8,128)(2,1)S(1)} %copy-done.20), channel_id=1, source_target_pairs={{0,2},{2,0},{1,3},{3,1},{4,6},{6,4},{5,7},{7,5},{8,10},{10,8},{9,1... | collective-permute-start | bytes 2359304 | tf_op jit(solution)/shard_map/ppermute | solution.py:311
  153.0 21.1 %collective-permute-start.38 = (bf16[256,1536]{1,0:T(8,128)(2,1)S(1)}, bf16[256,1536]{1,0:T(8,128)(2,1)S(1)}, u32[]{:S(2)}, u32[]{:S(2)}) collective-permute-start(bf16[256,1536]{1,0:T(8,128)(2,1)S(1)} %copy-done.17), channel_id=1, source_target_pairs={{0,2},{2,0},{1,3},{3,1},{4,6},{6,4},{5,7},{7,5},{8,10},{10,8},{9,1... | collective-permute-start | bytes 2359304 | tf_op jit(solution)/shard_map/ppermute | solution.py:311
  153.5 21.5 %collective-permute-start.35 = (bf16[256,1536]{1,0:T(8,128)(2,1)}, bf16[256,1536]{1,0:T(8,128)(2,1)S(1)}, u32[]{:S(2)}, u32[]{:S(2)}) collective-permute-start(bf16[256,1536]{1,0:T(8,128)(2,1)} %collective-permute-done.33.refs_0_), channel_id=1, source_target_pairs={{0,2},{2,0},{1,3},{3,1},{4,6},{6,4},{5,7},{7,5},{8,10},{10,8},{9,1... | collective-permute-start | bytes 2359304 | tf_op jit(solution)/shard_map/ppermute | solution.py:311
  153.5 22.4 %collective-permute-start.36 = (bf16[256,1536]{1,0:T(8,128)(2,1)}, bf16[256,1536]{1,0:T(8,128)(2,1)S(1)}, u32[]{:S(2)}, u32[]{:S(2)}) collective-permute-start(bf16[256,1536]{1,0:T(8,128)(2,1)} %collective-permute-done.34.refs_2_), channel_id=1, source_target_pairs={{0,2},{2,0},{1,3},{3,1},{4,6},{6,4},{5,7},{7,5},{8,10},{10,8},{9,1... | collective-permute-start | bytes 2359304 | tf_op jit(solution)/shard_map/ppermute | solution.py:311
  173.1 35.4 %collective-permute-start.43 = (bf16[256,1536]{1,0:T(8,128)(2,1)}, bf16[256,1536]{1,0:T(8,128)(2,1)}, u32[]{:S(2)}, u32[]{:S(2)}) collective-permute-start(bf16[256,1536]{1,0:T(8,128)(2,1)} %constant_dynamic-update-slice_fusion.16.refs_2_), channel_id=1, source_target_pairs={{0,2},{2,0},{1,3},{3,1},{4,6},{6,4},{5,7},{7,5},{8,10},{10,8},{9,1... | collective-permute-start | bytes 2359304 | tf_op jit(solution)/shard_map/ppermute | solution.py:311
  208.5 15.7 %collective-permute-start.49 = (bf16[256,1664]{1,0:T(8,128)(2,1)}, bf16[256,1664]{1,0:T(8,128)(2,1)S(1)}, u32[]{:S(2)}, u32[]{:S(2)}) collective-permute-start(bf16[256,1664]{1,0:T(8,128)(2,1)} %get-tuple-element.145), channel_id=1, source_target_pairs={{0,2},{2,0},{1,3},{3,1},{4,6},{6,4},{5,7},{7,5},{8,10},{10,8},{9,1... | collective-permute-start | bytes 2555912 | tf_op jit(solution)/shard_map/ppermute | solution.py:311
  223.6 47.8 %collective-permute-start.47 = (bf16[256,1664]{1,0:T(8,128)(2,1)}, bf16[256,1664]{1,0:T(8,128)(2,1)}, u32[]{:S(2)}, u32[]{:S(2)}) collective-permute-start(bf16[256,1664]{1,0:T(8,128)(2,1)} %get-tuple-element.143), channel_id=1, source_target_pairs={{0,2},{2,0},{1,3},{3,1},{4,6},{6,4},{5,7},{7,5},{8,10},{10,8},{9,1... | collective-permute-start | bytes 2555912 | tf_op jit(solution)/shard_map/ppermute | solution.py:311
  225.1 46.3 %collective-permute-start.50 = (bf16[128,1664]{1,0:T(8,128)(2,1)}, bf16[128,1664]{1,0:T(8,128)(2,1)}, u32[]{:S(2)}, u32[]{:S(2)}) collective-permute-start(bf16[128,1664]{1,0:T(8,128)(2,1)} %slice.211), channel_id=1, source_target_pairs={{0,4},{4,0},{1,5},{5,1},{2,6},{6,2},{3,7},{7,3},{8,12},{12,8},{9,1... | collective-permute-start | bytes 1277960 | tf_op jit(solution)/shard_map/ppermute | solution.py:311
  227.3 12.9 %collective-permute-start.45 = (bf16[128,1664]{1,0:T(8,128)(2,1)}, bf16[128,1664]{1,0:T(8,128)(2,1)S(1)}, u32[]{:S(2)}, u32[]{:S(2)}) collective-permute-start(bf16[128,1664]{1,0:T(8,128)(2,1)} %get-tuple-element.177), channel_id=1, source_target_pairs={{0,1},{1,0},{2,3},{3,2},{4,5},{5,4},{6,7},{7,6},{8,9},{9,8},{10,11... | collective-permute-start | bytes 1277960 | tf_op jit(solution)/shard_map/ppermute | solution.py:311
  228.3 18.1 %collective-permute-start.46 = (bf16[128,1664]{1,0:T(8,128)(2,1)S(1)}, bf16[128,1664]{1,0:T(8,128)(2,1)S(1)}, u32[]{:S(2)}, u32[]{:S(2)}) collective-permute-start(bf16[128,1664]{1,0:T(8,128)(2,1)S(1)} %get-tuple-element.176), channel_id=1, source_target_pairs={{0,4},{4,0},{1,5},{5,1},{2,6},{6,2},{3,7},{7,3},{8,12},{12,8},{9,1... | collective-permute-start | bytes 1277960 | tf_op jit(solution)/shard_map/ppermute | solution.py:311
  230.3 41.1 %collective-permute-start.48 = (bf16[128,1664]{1,0:T(8,128)(2,1)}, bf16[128,1664]{1,0:T(8,128)(2,1)}, u32[]{:S(2)}, u32[]{:S(2)}) collective-permute-start(bf16[128,1664]{1,0:T(8,128)(2,1)} %slice.210), channel_id=1, source_target_pairs={{0,1},{1,0},{2,3},{3,2},{4,5},{5,4},{6,7},{7,6},{8,9},{9,8},{10,11... | collective-permute-start | bytes 1277960 | tf_op jit(solution)/shard_map/ppermute | solution.py:311
  247.3 24.2 %collective-permute-start.52 = (bf16[128,1664]{1,0:T(8,128)(2,1)}, bf16[128,1664]{1,0:T(8,128)(2,1)}, u32[]{:S(2)}, u32[]{:S(2)}) collective-permute-start(bf16[128,1664]{1,0:T(8,128)(2,1)} %reduce-precision_convert_fusion.8), channel_id=1, source_target_pairs={{0,1},{1,0},{2,3},{3,2},{4,5},{5,4},{6,7},{7,6},{8,9},{9,8},{10,11... | collective-permute-start | bytes 1277960 | tf_op jit(solution)/shard_map/ppermute | solution.py:311
  249.2 22.2 %collective-permute-start.51 = (bf16[128,1664]{1,0:T(8,128)(2,1)}, bf16[128,1664]{1,0:T(8,128)(2,1)}, u32[]{:S(2)}, u32[]{:S(2)}) collective-permute-start(bf16[128,1664]{1,0:T(8,128)(2,1)} %reduce-precision_convert_fusion.7), channel_id=1, source_target_pairs={{0,4},{4,0},{1,5},{5,1},{2,6},{6,2},{3,7},{7,3},{8,12},{12,8},{9,1... | collective-permute-start | bytes 1277960 | tf_op jit(solution)/shard_map/ppermute | solution.py:311
  295.0 67.7 %all-to-all-start = ((bf16[8,272,448]{2,1,0:T(8,128)(2,1)}), bf16[8,272,448]{2,1,0:T(8,128)(2,1)S(1)}, u32[]{:S(2)}, u32[]{:S(2)}) async-start(bf16[8,272,448]{2,1,0:T(8,128)(2,1)} %pad_maximum_fusion), calls=%async_computation | async-start | bytes 4456448 | tf_op jit(solution)/shard_map/all_to_all | solution.py:61
  298.6 145.1 %reduce-scatter.8.cloned.1.call-start = ((), (), s32[]{:S(2)}) async-start(), calls=%async_computation.9 | async-start | bytes 2949120 | tf_op jit(solution)/shard_map/reduce_scatter | solution.py:65
  301.8 57.6 %collective-permute-start.53 = (bf16[512,1536]{1,0:T(8,128)(2,1)}, bf16[512,1536]{1,0:T(8,128)(2,1)}, u32[]{:S(2)}, u32[]{:S(2)}) collective-permute-start(bf16[512,1536]{1,0:T(8,128)(2,1)} %constant_dynamic-update-slice_fusion.18.refs_0_), channel_id=1, source_target_pairs={{0,4},{4,0},{1,5},{5,1},{2,6},{6,2},{3,7},{7,3},{8,12},{12,8},{9,1... | collective-permute-start | bytes 4718600 | tf_op jit(solution)/shard_map/ppermute | solution.py:311
  303.7 57.8 %collective-permute-start.54 = (bf16[512,1536]{1,0:T(8,128)(2,1)}, bf16[512,1536]{1,0:T(8,128)(2,1)}, u32[]{:S(2)}, u32[]{:S(2)}) collective-permute-start(bf16[512,1536]{1,0:T(8,128)(2,1)} %constant_dynamic-update-slice_fusion.18.refs_0_), channel_id=1, source_target_pairs={{0,1},{1,0},{2,3},{3,2},{4,5},{5,4},{6,7},{7,6},{8,9},{9,8},{10,11... | collective-permute-start | bytes 4718600 | tf_op jit(solution)/shard_map/ppermute | solution.py:311
  305.2 144.4 %reduce-scatter.4.cloned.1.call-start = ((), (), s32[]{:S(2)}) async-start(), calls=%async_computation.7 | async-start | bytes 2048000 | tf_op jit(solution)/shard_map/reduce_scatter | solution.py:65
  362.7 19.4 %collective-permute-start.55 = (bf16[256,1536]{1,0:T(8,128)(2,1)}, bf16[256,1536]{1,0:T(8,128)(2,1)S(1)}, u32[]{:S(2)}, u32[]{:S(2)}) collective-permute-start(bf16[256,1536]{1,0:T(8,128)(2,1)} %slice.213), channel_id=1, source_target_pairs={{0,1},{1,0},{2,3},{3,2},{4,5},{5,4},{6,7},{7,6},{8,9},{9,8},{10,11... | collective-permute-start | bytes 2359304 | tf_op jit(solution)/shard_map/ppermute | solution.py:311
  364.2 18.8 %collective-permute-start.56 = (bf16[256,1536]{1,0:T(8,128)(2,1)S(1)}, bf16[256,1536]{1,0:T(8,128)(2,1)S(1)}, u32[]{:S(2)}, u32[]{:S(2)}) collective-permute-start(bf16[256,1536]{1,0:T(8,128)(2,1)S(1)} %slice.214), channel_id=1, source_target_pairs={{0,4},{4,0},{1,5},{5,1},{2,6},{6,2},{3,7},{7,3},{8,12},{12,8},{9,1... | collective-permute-start | bytes 2359304 | tf_op jit(solution)/shard_map/ppermute | solution.py:311
  364.7 18.4 %collective-permute-start.67 = (bf16[512,1536]{1,0:T(8,128)(2,1)}, bf16[512,1536]{1,0:T(8,128)(2,1)S(1)}, u32[]{:S(2)}, u32[]{:S(2)}) collective-permute-start(bf16[512,1536]{1,0:T(8,128)(2,1)} %constant_dynamic-update-slice_fusion.18.refs_0_), channel_id=1, source_target_pairs={{0,2},{2,0},{1,3},{3,1},{4,6},{6,4},{5,7},{7,5},{8,10},{10,8},{9,1... | collective-permute-start | bytes 4718600 | tf_op jit(solution)/shard_map/ppermute | solution.py:311
  364.7 18.4 %collective-permute-start.68 = (bf16[512,1536]{1,0:T(8,128)(2,1)}, bf16[512,1536]{1,0:T(8,128)(2,1)S(1)}, u32[]{:S(2)}, u32[]{:S(2)}) collective-permute-start(bf16[512,1536]{1,0:T(8,128)(2,1)} %collective-permute-done.54.refs_1_), channel_id=1, source_target_pairs={{0,2},{2,0},{1,3},{3,1},{4,6},{6,4},{5,7},{7,5},{8,10},{10,8},{9,1... | collective-permute-start | bytes 4718600 | tf_op jit(solution)/shard_map/ppermute | solution.py:311
  365.2 17.9 %collective-permute-start.69 = (bf16[512,1536]{1,0:T(8,128)(2,1)}, bf16[512,1536]{1,0:T(8,128)(2,1)S(1)}, u32[]{:S(2)}, u32[]{:S(2)}) collective-permute-start(bf16[512,1536]{1,0:T(8,128)(2,1)} %collective-permute-done.53.refs_2_), channel_id=1, source_target_pairs={{0,2},{2,0},{1,3},{3,1},{4,6},{6,4},{5,7},{7,5},{8,10},{10,8},{9,1... | collective-permute-start | bytes 4718600 | tf_op jit(solution)/shard_map/ppermute | solution.py:311
  395.1 124.2 %reduce-scatter.6.cloned.1.call-start = ((), (), s32[]{:S(2)}) async-start(), calls=%async_computation.8 | async-start | bytes 5898240 | tf_op jit(solution)/shard_map/reduce_scatter | solution.py:65
  414.0 48.9 %collective-permute-start.66 = (bf16[256,1536]{1,0:T(8,128)(2,1)}, bf16[256,1536]{1,0:T(8,128)(2,1)}, u32[]{:S(2)}, u32[]{:S(2)}) collective-permute-start(bf16[256,1536]{1,0:T(8,128)(2,1)} %copy-done.45), channel_id=1, source_target_pairs={{0,2},{2,0},{1,3},{3,1},{4,6},{6,4},{5,7},{7,5},{8,10},{10,8},{9,1... | collective-permute-start | bytes 2359304 | tf_op jit(solution)/shard_map/ppermute | solution.py:311
  417.2 12.0 %collective-permute-start.61 = (bf16[128,1536]{1,0:T(8,128)(2,1)S(1)}, bf16[128,1536]{1,0:T(8,128)(2,1)S(1)}, u32[]{:S(2)}, u32[]{:S(2)}) collective-permute-start(bf16[128,1536]{1,0:T(8,128)(2,1)S(1)} %get-tuple-element.180), channel_id=1, source_target_pairs={{0,1},{1,0},{2,3},{3,2},{4,5},{5,4},{6,7},{7,6},{8,9},{9,8},{10,11... | collective-permute-start | bytes 1179656 | tf_op jit(solution)/shard_map/ppermute | solution.py:311
  420.1 27.8 %collective-permute-start.58 = (bf16[128,1536]{1,0:T(8,128)(2,1)}, bf16[128,1536]{1,0:T(8,128)(2,1)}, u32[]{:S(2)}, u32[]{:S(2)}) collective-permute-start(bf16[128,1536]{1,0:T(8,128)(2,1)} %slice.216), channel_id=1, source_target_pairs={{0,1},{1,0},{2,3},{3,2},{4,5},{5,4},{6,7},{7,6},{8,9},{9,8},{10,11... | collective-permute-start | bytes 1179656 | tf_op jit(solution)/shard_map/ppermute | solution.py:311
  420.7 40.9 %collective-permute-start.63 = (bf16[128,1536]{1,0:T(8,128)(2,1)S(1)}, bf16[128,1536]{1,0:T(8,128)(2,1)}, u32[]{:S(2)}, u32[]{:S(2)}) collective-permute-start(bf16[128,1536]{1,0:T(8,128)(2,1)S(1)} %slice.219), channel_id=1, source_target_pairs={{0,4},{4,0},{1,5},{5,1},{2,6},{6,2},{3,7},{7,3},{8,12},{12,8},{9,1... | collective-permute-start | bytes 1179656 | tf_op jit(solution)/shard_map/ppermute | solution.py:311
  421.5 19.7 %collective-permute-start.64 = (bf16[128,1536]{1,0:T(8,128)(2,1)S(1)}, bf16[128,1536]{1,0:T(8,128)(2,1)S(1)}, u32[]{:S(2)}, u32[]{:S(2)}) collective-permute-start(bf16[128,1536]{1,0:T(8,128)(2,1)S(1)} %get-tuple-element.181), channel_id=1, source_target_pairs={{0,4},{4,0},{1,5},{5,1},{2,6},{6,2},{3,7},{7,3},{8,12},{12,8},{9,1... | collective-permute-start | bytes 1179656 | tf_op jit(solution)/shard_map/ppermute | solution.py:311
  429.3 19.2 %collective-permute-start.62 = (bf16[128,1536]{1,0:T(8,128)(2,1)S(1)}, bf16[128,1536]{1,0:T(8,128)(2,1)S(1)}, u32[]{:S(2)}, u32[]{:S(2)}) collective-permute-start(bf16[128,1536]{1,0:T(8,128)(2,1)S(1)} %reduce-precision_convert_fusion.10), channel_id=1, source_target_pairs={{0,4},{4,0},{1,5},{5,1},{2,6},{6,2},{3,7},{7,3},{8,12},{12,8},{9,1... | collective-permute-start | bytes 1179656 | tf_op jit(solution)/shard_map/ppermute | solution.py:311
  442.0 19.6 %collective-permute-start.65 = (bf16[128,1536]{1,0:T(8,128)(2,1)}, bf16[128,1536]{1,0:T(8,128)(2,1)}, u32[]{:S(2)}, u32[]{:S(2)}) collective-permute-start(bf16[128,1536]{1,0:T(8,128)(2,1)} %reduce-precision_convert_fusion.9), channel_id=1, source_target_pairs={{0,1},{1,0},{2,3},{3,2},{4,5},{5,4},{6,7},{7,6},{8,9},{9,8},{10,11... | collective-permute-start | bytes 1179656 | tf_op jit(solution)/shard_map/ppermute | solution.py:311
  443.6 13.8 %all-to-all-start.3 = ((bf16[4,1,96,768]{3,2,1,0:T(8,128)(2,1)}), bf16[4,1,96,768]{3,2,1,0:T(8,128)(2,1)}, u32[]{:S(2)}, u32[]{:S(2)}) async-start(bf16[4,1,96,768]{3,2,1,0:T(8,128)(2,1)} %reduce-scatter.8.cloned.1.call-done), calls=%async_computation.6 | async-start | bytes 1179648 | tf_op jit(solution)/shard_map/all_to_all | solution.py:61
  457.4 17.8 %all-to-all-start.1 = ((bf16[8,112,448]{2,1,0:T(8,128)(2,1)}), bf16[8,112,448]{2,1,0:T(8,128)(2,1)}, u32[]{:S(2)}, u32[]{:S(2)}) async-start(bf16[8,112,448]{2,1,0:T(8,128)(2,1)} %maximum_maximum_fusion), calls=%async_computation.2 | async-start | bytes 1835008 | tf_op jit(solution)/shard_map/all_to_all | solution.py:61
  519.3 19.4 %all-to-all-start.2 = ((bf16[4,2,96,768]{3,2,1,0:T(8,128)(2,1)}), bf16[4,2,96,768]{3,2,1,0:T(8,128)(2,1)S(1)}, u32[]{:S(2)}, u32[]{:S(2)}) async-start(bf16[4,2,96,768]{3,2,1,0:T(8,128)(2,1)} %reduce-scatter.6.cloned.1.call-done), calls=%async_computation.4 | async-start | bytes 2359296 | tf_op jit(solution)/shard_map/all_to_all | solution.py:61
  (137 other events, 1309.2 us)
Sparse Core Ops, SparseCore 0:
  305.3 48.9 reduce-scatter.7
  395.2 37.3 reduce-scatter.3
  435.0 84.2 reduce-scatter.5
